TPU v7x, 32 devices: a whole 2x2x4 slice. The times are simulated.
32 devices in a mesh: row: 4 (over z), col: 8 (over y, x, core).
Axes of the slice: x: 2, y: 2, z: 4, core: 2. Of those that a mesh axis runs over, the one named last changes fastest.
Arguments:
- images: bfloat16 [32, 3, 64, 96], P(('row', 'col')), may hold values from -1000 to 1000
- weights: bfloat16 [16, 24, 128, 1200], P('row', 'col'), may hold values from -0.1875 to 0.1875
Outputs:
- weight_grad: float32 [16, 24, 128, 1200], P('row', 'col')
All inputs are finite; a program needn't handle non-finite values.
Results may differ from a plain program's by a relative error of at most 0.006.
Values may be sent and summed in bfloat16 or wider, within the bound.
No kernel may reach another device: no remote copies, remote signals or barrier semaphores. Data moves between devices by JAX's collectives and lax.ppermute only.
A program may use at most 128 MiB of HBM per device.

v0:
```python
import functools

import jax
import jax.numpy as jnp
import numpy as np
from jax import lax
from jax.experimental import pallas as pl
from jax.experimental.pallas import tpu as pltpu
from jax.sharding import PartitionSpec as P

CH = 3
S = 4
FIELD = 20
PAD = 8
K = 1200
GROUP = FIELD // S

sparsity = 0.5
f32 = jnp.float32
bf16 = jnp.bfloat16
NT = (((1,), (1,)), ((), ()))
NN = (((1,), (0,)), ((), ()))
TN = (((0,), (0,)), ((), ()))
MIB = 1024 * 1024


def dot(a, b, dims=NN):
    return lax.dot_general(a, b, dims, preferred_element_type=f32)


class Sizes:
    def __init__(self, images, weights, mesh):
        self.R, self.C = mesh.shape["row"], mesh.shape["col"]
        self.bd = images[0]
        self.height, self.width = images[2], images[3]
        self.rd, self.cd, self.F = weights[0], weights[1], weights[2]
        self.B = self.bd * self.R * self.C
        self.h, self.w = S * self.rd, S * self.cd
        self.ext = self.w + 2 * PAD
        self.stride = -(-self.ext // 32) * 32
        self.lanes = S * self.stride
        self.YB = self.rd + 2 * PAD // S
        self.T = CH * self.YB
        assert self.C % 2 == 0 and self.rd >= 4 and self.cd >= 2 and self.lanes == 128
        assert self.height == self.R * self.h and self.width == self.C * self.w


PIECES = ((0, 0, 512, 0, 256), (1, 384, 512, 256, 256), (2, 768, 256, 512, 128))


def one_hot():
    out = []
    for _, first, depth, start, count in PIECES:
        n = np.arange(start, start + count)
        lane = 32 * (n // FIELD) + n % FIELD
        out.append((np.arange(first, first + depth)[:, None] == lane[None, :]).astype(np.float32))
    return [jnp.asarray(m, bf16) for m in out]


def split_kernel(z, images_ref, out_ref, rows_ref, pad_ref):
    margin = PAD // S
    blocks = z.height // S
    n = lax.broadcasted_iota(jnp.int32, (1, z.C * z.lanes), 1)
    column = n // z.lanes
    inner = n % z.lanes
    lane_row = inner // z.stride
    across = inner % z.stride
    source = jnp.where(across < z.ext, z.w * column - PAD + across, -1)
    pixel = lax.broadcasted_iota(jnp.int32, (128, z.C * z.lanes), 0)
    chunks = rows_ref.shape[1]
    rows_ref[...] = jnp.zeros_like(rows_ref)
    for i in range(z.bd):
        pixels = images_ref[i].astype(f32)
        count = CH * z.height * z.width
        center = jnp.sum(pixels) / count
        moved = pixels - center
        variance = jnp.sum(moved * moved) / count
        normed = (moved / jnp.sqrt(variance + 1e-05)).astype(bf16).astype(f32)
        for k in range(chunks):
            stop = min(128, z.width - 128 * k)
            rows_ref[:, k, :, :stop] = normed[:, :, 128 * k : 128 * k + stop]
        total = jnp.zeros((CH * blocks, z.C * z.lanes), f32)
        for k in range(chunks):
            for j in range(S):
                line = jnp.concatenate(
                    [rows_ref[c, k, pl.ds(j, blocks, stride=S), :] for c in range(CH)], axis=0
                ).astype(bf16)
                wanted = jnp.where(lane_row == j, source - 128 * k, -1)
                total = total + dot(line, (pixel == wanted).astype(f32).astype(bf16))
        pad_ref[...] = jnp.zeros_like(pad_ref)
        for c in range(CH):
            pad_ref[c, margin : margin + blocks, :] = total[c * blocks : (c + 1) * blocks]
        for r in range(z.R):
            for q in range(z.C):
                block = [
                    pad_ref[c, z.rd * r : z.rd * r + z.YB, q * z.lanes : (q + 1) * z.lanes]
                    for c in range(CH)
                ]
                out_ref[r * z.C + q, i] = jnp.concatenate(block, axis=0).astype(bf16)


def split(z, images):
    return pl.pallas_call(
        functools.partial(split_kernel, z),
        out_shape=jax.ShapeDtypeStruct((z.R * z.C, z.bd, z.T, z.lanes), bf16),
        in_specs=[pl.BlockSpec(memory_space=pltpu.VMEM)],
        out_specs=pl.BlockSpec(memory_space=pltpu.VMEM),
        scratch_shapes=[
            pltpu.VMEM((CH, -(-z.width // 128), z.height, 128), f32),
            pltpu.VMEM((CH, z.height // S + 2 * PAD // S, z.C * z.lanes), f32),
        ],
        compiler_params=pltpu.CompilerParams(vmem_limit_bytes=32 * MIB),
    )(images)


def shift_tiles(z, tile_of, rolled_ref):
    for t in range(z.T):
        tile = tile_of(t)
        for q in range(z.cd):
            moved = pltpu.roll(tile, z.lanes - S * q, 1) if q else tile
            rolled_ref[q, t] = moved.astype(bf16)


def field_slab(z, p, rolled_ref, slab_ref):
    for q in range(z.cd):
        for c in range(CH):
            for g in range(GROUP):
                at = (c * GROUP + g) * z.lanes
                slab_ref[q * z.B : (q + 1) * z.B, at : at + z.lanes] = rolled_ref[q, c * z.YB + p + g]


def gather_patches(slab_ref, picks, store):
    for half in range(2):
        for m, first, depth, start, count in PIECES:
            low = 1024 * half + first
            depth = min(depth, CH * GROUP * 128 - low)
            store(640 * half + start, count, dot(slab_ref[:, low : low + depth], picks[m][:depth, :]))


def encode_kernel(
    z, moved_ref, weights_ref, a_ref, b_ref, c_ref,
    patch_ref, window_ref, hidden_ref, contrib_ref, up_ref, down_ref,
    rows_ref, rolled_ref, slab_ref, high_ref, low_ref, spot_ref,
):
    p = pl.program_id(0)
    B = z.B
    picks = (a_ref, b_ref, c_ref)

    @pl.when(p == 0)
    def _():
        rows_ref[...] = moved_ref[...].reshape(B * z.T, z.lanes).astype(f32)
        for t in range(z.T):
            tile = rows_ref[pl.ds(t, B, stride=z.T), :]
            window_ref[t] = tile.astype(bf16)
            for q in range(z.cd):
                turned = pltpu.roll(tile, z.lanes - S * q, 1) if q else tile
                rolled_ref[q, t] = turned.astype(bf16)
        contrib_ref[...] = jnp.zeros_like(contrib_ref)
        high_ref[...] = jnp.zeros_like(high_ref)
        low_ref[...] = jnp.zeros_like(low_ref)

    field_slab(z, p, rolled_ref, slab_ref)

    def store(at, count, value):
        patch_ref[0, :, at : at + count] = value.astype(bf16)

    gather_patches(slab_ref, picks, store)
    for q in range(z.cd):
        weight = weights_ref[0, q]
        hidden = dot(patch_ref[0, q * B : (q + 1) * B, :K], weight, NT).astype(bf16)
        hidden_ref[p, q] = hidden
        terms = dot(hidden, weight)
        high = terms.astype(bf16)
        high_ref[q * B : (q + 1) * B, :K] = high
        low_ref[q * B : (q + 1) * B, :K] = (terms - high.astype(f32)).astype(bf16)
    spot_ref[...] = jnp.zeros_like(spot_ref)
    for half in range(2):
        for m, first, depth, start, count in PIECES:
            low = 1024 * half + first
            depth = min(depth, CH * GROUP * 128 - low)
            pick = picks[m][:depth, :]
            at = 640 * half + start
            value = dot(high_ref[:, at : at + count], pick, NT) + dot(low_ref[:, at : at + count], pick, NT)
            spot_ref[:, low : low + depth] += value
    for c in range(CH):
        for g in range(GROUP):
            at = (c * GROUP + g) * z.lanes
            total = spot_ref[:B, at : at + z.lanes]
            for q in range(1, z.cd):
                total = total + pltpu.roll(spot_ref[q * B : (q + 1) * B, at : at + z.lanes], S * q, 1)
            contrib_ref[c * z.YB + p + g] += total

    @pl.when(p == z.rd - 1)
    def _():
        half = z.YB // 2
        for c in range(CH):
            for y in range(half):
                up_ref[c * half + y] = contrib_ref[c * z.YB + y].astype(bf16)
                down_ref[c * half + y] = contrib_ref[c * z.YB + z.YB - half + y].astype(bf16)
        for i in range(2):
            for q in range(z.cd):
                up_ref[CH * half + i * z.cd + q] = hidden_ref[i, q]
                down_ref[CH * half + i * z.cd + q] = hidden_ref[z.rd - 2 + i, q]


def whole(shape):
    return pl.BlockSpec(shape, lambda p: (0,) * len(shape))


def encode(z, moved, weights, picks):
    B, F, L = z.B, z.F, z.lanes
    sent = CH * (z.YB // 2) + 2 * z.cd
    shapes = [
        ((z.rd, z.cd * B, 1280), bf16),
        ((z.T, B, L), bf16),
        ((z.rd, z.cd, B, F), bf16),
        ((z.T, B, L), f32),
        ((sent, B, L), bf16),
        ((sent, B, L), bf16),
    ]
    return pl.pallas_call(
        functools.partial(encode_kernel, z),
        grid=(z.rd,),
        out_shape=[jax.ShapeDtypeStruct(*s) for s in shapes],
        in_specs=[
            whole(moved.shape),
            pl.BlockSpec((1, z.cd, F, K), lambda p: (p, 0, 0, 0)),
        ] + [whole(m.shape) for m in picks],
        out_specs=[pl.BlockSpec((1, z.cd * B, 1280), lambda p: (p, 0, 0))] + [whole(s[0]) for s in shapes[1:]],
        scratch_shapes=[
            pltpu.VMEM((B * z.T, L), f32),
            pltpu.VMEM((z.cd, z.T, B, L), bf16),
            pltpu.VMEM((z.cd * B, CH * GROUP * L), bf16),
            pltpu.VMEM((z.cd * B, 1280), bf16),
            pltpu.VMEM((z.cd * B, 1280), bf16),
            pltpu.VMEM((z.cd * B, CH * GROUP * L), f32),
        ],
        compiler_params=pltpu.CompilerParams(vmem_limit_bytes=48 * MIB),
    )(moved, weights, *picks)


def vmem_call(kernel, shapes, scratch, *args):
    vmem = pl.BlockSpec(memory_space=pltpu.VMEM)
    return pl.pallas_call(
        kernel,
        out_shape=[jax.ShapeDtypeStruct(*s) for s in shapes],
        in_specs=[vmem] * len(args),
        out_specs=[vmem] * len(shapes),
        scratch_shapes=[pltpu.VMEM(*s) for s in scratch],
        compiler_params=pltpu.CompilerParams(vmem_limit_bytes=32 * MIB),
    )(*args)


def is_even():
    return lax.rem(lax.axis_index("col"), 2) == 0


def from_side(z, value, from_left):
    across = lax.broadcasted_iota(jnp.int32, value.shape, 1) % z.stride
    turned = pltpu.roll(value, jnp.where(from_left, z.lanes - z.w, z.w), 1)
    low = jnp.where(from_left, 0, z.w)
    high = jnp.where(from_left, z.ext - z.w, z.ext)
    return jnp.where((across >= low) & (across < high), turned, 0.0)


def rows_kernel(z, contrib_ref, hidden_ref, above_ref, below_ref, sum_ref, tall_ref, send_ref):
    half = z.YB // 2
    for c in range(CH):
        for y in range(z.YB):
            t = c * z.YB + y
            total = contrib_ref[t]
            if y < half:
                total = total + above_ref[c * half + y].astype(f32)
            if y >= z.YB - half:
                total = total + below_ref[c * half + y - (z.YB - half)].astype(f32)
            sum_ref[t] = total
            send_ref[t] = total.astype(bf16)
    for q in range(z.cd):
        for i in range(2):
            tall_ref[i, q] = above_ref[CH * half + i * z.cd + q]
            tall_ref[z.rd + 2 + i, q] = below_ref[CH * half + i * z.cd + q]
        for i in range(z.rd):
            tall_ref[2 + i, q] = hidden_ref[i, q]
    first = jnp.where(is_even(), z.cd - 2, 0)
    for i in range(z.rd + 4):
        for k in range(2):
            send_ref[z.T + 2 * i + k] = tall_ref[i, first + k]


def near_kernel(z, sum_ref, tall_ref, near_ref, out_ref, send_ref):
    even = is_even()
    for t in range(z.T):
        total = sum_ref[t] + from_side(z, near_ref[t].astype(f32), jnp.logical_not(even))
        out_ref[t] = total
        send_ref[t] = total.astype(bf16)
    first = jnp.where(even, 0, z.cd - 2)
    for i in range(z.rd + 4):
        for k in range(2):
            send_ref[z.T + 2 * i + k] = tall_ref[i, first + k]


def far_kernel(z, sum_ref, far_ref, out_ref, send_ref):
    even = is_even()
    for t in range(z.T):
        came = from_side(z, far_ref[t].astype(f32), even)
        out_ref[t] = sum_ref[t] + came
        send_ref[t] = came.astype(bf16)


def pool_kernel(z, tall_ref, near_ref, far_ref, out_ref, wide_ref, inverse_ref):
    even = is_even()
    row0 = lax.axis_index("row") * z.rd - 1
    col0 = lax.axis_index("col") * z.cd - 1
    near_at = jnp.where(even, z.cd + 2, 0)
    far_at = jnp.where(even, 0, z.cd + 2)
    for i in range(z.rd + 4):
        for k in range(2):
            wide_ref[i, near_at + k] = near_ref[z.T + 2 * i + k]
            wide_ref[i, far_at + k] = far_ref[z.T + 2 * i + k]
        for q in range(z.cd):
            wide_ref[i, 2 + q] = tall_ref[i, q]
    for i in range(z.rd + 2):
        columns = []
        for q in range(z.cd + 4):
            parts = [jnp.square(wide_ref[i + d, q].astype(f32)) for d in range(3)]
            columns.append(parts[0] + parts[1] + parts[2])
        for q in range(z.cd + 2):
            energy = jnp.sqrt(1.0 + (columns[q] + columns[q + 1] + columns[q + 2]))
            inverse = (1.0 / energy).astype(bf16).astype(f32)
            row, col = row0 + i, col0 + q
            inside = (row >= 0) & (row < z.R * z.rd) & (col >= 0) & (col < z.C * z.cd)
            inverse_ref[i, q] = inverse * jnp.where(inside, 1.0, 0.0)
    for i in range(z.rd):
        columns = []
        for q in range(z.cd + 2):
            columns.append(inverse_ref[i, q] + inverse_ref[i + 1, q] + inverse_ref[i + 2, q])
        for q in range(z.cd):
            spread = columns[q] + columns[q + 1] + columns[q + 2]
            out_ref[i, q] = sparsity * tall_ref[2 + i, q].astype(f32) * spread


def grad_kernel(
    z, sum_ref, last_ref, window_ref, patch_ref, hidden_ref, pooled_ref, weights_ref, a_ref, b_ref, c_ref,
    out_ref, rolled_ref, slab_ref, resid_ref,
):
    p = pl.program_id(0)
    B = z.B
    picks = (a_ref, b_ref, c_ref)

    @pl.when(p == 0)
    def _():
        from_left = jnp.logical_not(is_even())
        lane = lax.broadcasted_iota(jnp.int32, (1, z.lanes), 1) % z.stride
        x = lax.axis_index("col") * z.w - PAD + lane
        across = ((x >= 0) & (x < z.width)).astype(f32)
        first = lax.axis_index("row") * z.h - PAD
        for c in range(CH):
            for y in range(z.YB):
                t = c * z.YB + y
                recon = sum_ref[t] + from_side(z, last_ref[t].astype(f32), from_left)
                line = first + S * y
                inside = jnp.where((line >= 0) & (line < z.height), across, 0.0)
                tile = ((recon - window_ref[t].astype(f32)) * inside).astype(bf16).astype(f32)
                for q in range(z.cd):
                    turned = pltpu.roll(tile, z.lanes - S * q, 1) if q else tile
                    rolled_ref[q, t] = turned.astype(bf16)

    field_slab(z, p, rolled_ref, slab_ref)

    def store(at, count, value):
        resid_ref[:, at : at + count] = value.astype(bf16)

    gather_patches(slab_ref, picks, store)
    for q in range(z.cd):
        rows = slice(q * B, (q + 1) * B)
        resid = resid_ref[rows, :K]
        back = (pooled_ref[p, q] + dot(resid, weights_ref[0, q], NT)).astype(bf16)
        left = jnp.concatenate([back, hidden_ref[p, q]], axis=0)
        right = jnp.concatenate([patch_ref[0, rows, :K], resid], axis=0)
        out_ref[0, q] = dot(left, right, TN) * (1.0 / B)


def gradient(z, total, last, window, patch, hidden, pooled, weights, picks):
    B, F, L = z.B, z.F, z.lanes
    return pl.pallas_call(
        functools.partial(grad_kernel, z),
        grid=(z.rd,),
        out_shape=jax.ShapeDtypeStruct((z.rd, z.cd, F, K), f32),
        in_specs=[
            whole(total.shape),
            whole(last.shape),
            whole(window.shape),
            pl.BlockSpec((1, z.cd * B, 1280), lambda p: (p, 0, 0)),
            whole(hidden.shape),
            whole(pooled.shape),
            pl.BlockSpec((1, z.cd, F, K), lambda p: (p, 0, 0, 0)),
        ] + [whole(m.shape) for m in picks],
        out_specs=pl.BlockSpec((1, z.cd, F, K), lambda p: (p, 0, 0, 0)),
        scratch_shapes=[
            pltpu.VMEM((z.cd, z.T, B, L), bf16),
            pltpu.VMEM((z.cd * B, CH * GROUP * L), bf16),
            pltpu.VMEM((z.cd * B, 1280), bf16),
        ],
        compiler_params=pltpu.CompilerParams(vmem_limit_bytes=48 * MIB),
    )(total, last, window, patch, hidden, pooled, weights, *picks)


def body(z, images, weights):
    B, L = z.B, z.lanes
    picks = one_hot()
    blocks = split(z, images)
    moved = lax.all_to_all(
        blocks.reshape(z.R * z.C, z.bd * z.T, L), ("row", "col"), split_axis=0, concat_axis=0, tiled=True
    ).reshape(B, z.T, L)
    patch, window, hidden, contrib, up, down = encode(z, moved, weights, picks)

    below_to = [(r, r + 1) for r in range(z.R - 1)]
    above_to = [(r + 1, r) for r in range(z.R - 1)]
    above = lax.ppermute(down, "row", below_to)
    below = lax.ppermute(up, "row", above_to)
    tall = ((z.rd + 4, z.cd, B, z.F), bf16)
    tiles = ((z.T, B, L), f32)
    sent = ((z.T + 2 * (z.rd + 4), B, L), bf16)
    total, tall, send = vmem_call(
        functools.partial(rows_kernel, z), [tiles, tall, sent], [], contrib, hidden, above, below
    )
    swap = [(c, c ^ 1) for c in range(z.C)]
    cross = [(c, c + 1 if c % 2 else c - 1) for c in range(1, z.C - 1)]
    near = lax.ppermute(send, "col", swap)
    total, send = vmem_call(functools.partial(near_kernel, z), [tiles, sent], [], total, tall, near)
    far = lax.ppermute(send, "col", cross)
    total, send = vmem_call(
        functools.partial(far_kernel, z), [tiles, ((z.T, B, L), bf16)], [], total, far
    )
    last = lax.ppermute(send, "col", swap)
    (pooled,) = vmem_call(
        functools.partial(pool_kernel, z),
        [((z.rd, z.cd, B, z.F), f32)],
        [((z.rd + 4, z.cd + 4, B, z.F), bf16), ((z.rd + 2, z.cd + 2, B, z.F), f32)],
        tall, near, far,
    )
    return gradient(z, total, last, window, patch, hidden, pooled, weights, picks)


def solution(mesh):
    def run(images, weights):
        z = Sizes(
            (images.shape[0] // (mesh.shape["row"] * mesh.shape["col"]),) + images.shape[1:],
            (weights.shape[0] // mesh.shape["row"], weights.shape[1] // mesh.shape["col"]) + weights.shape[2:],
            mesh,
        )
        return jax.shard_map(
            functools.partial(body, z),
            mesh=mesh,
            in_specs=(P(("row", "col"), None, None, None), P("row", "col", None, None)),
            out_specs=P("row", "col", None, None),
            check_vma=False,
        )(images, weights)

    return run
```

profile of v0, /device:TPU:0, one launch (start us, length us, event | category | flops | bytes accessed | tf_op | source)
XLA Modules:
  0.0 72.5 jit_solution(10774748570355412424)
XLA Ops:
  0.0 0.0 copy-start.2
  0.0 0.0 copy-start
  0.0 0.0 copy-start.1
  0.0 0.0 copy-start.3
  0.0 0.9 %copy-done.3 = bf16[1,3,64,96]{3,2,1,0:T(8,128)(2,1)S(1)} copy-done((bf16[1,3,64,96]{3,2,1,0:T(8,128)(2,1)S(1)}, bf16[1,3,64,96]{3,2,1,0:T(8,128)(2,1)}, u32[]{:S(2)}) %copy-start.3) | copy-done | bytes 36888
  0.9 1.4 %shard_map.55 = bf16[32,1,24,128]{3,2,1,0:T(8,128)(2,1)} custom-call(bf16[1,3,64,96]{3,2,1,0:T(8,128)(2,1)S(1)} %copy-done.3), custom_call_target="tpu_custom_call" | custom-call | tf_op jit(solution)/shard_map/pallas_call | solution.py:103
  2.3 7.3 %all-to-all-start = ((bf16[32,24,128]{2,1,0:T(8,128)(2,1)}), bf16[32,24,128]{2,1,0:T(8,128)(2,1)S(1)}, u32[]{:S(2)}, u32[]{:S(2)}) async-start(bf16[32,24,128]{2,1,0:T(8,128)(2,1)} %bitcast), calls=%async_computation | async-start | bytes 393216 | tf_op jit(solution)/shard_map/all_to_all | solution.py:412
  9.6 6.0 %copy.6.weights_ref = bf16[4,3,128,1200]{3,2,1,0:T(8,128)(2,1)} copy(bf16[4,3,128,1200]{2,3,1,0:T(8,128)(2,1)} %param.6) | data formatting | bytes 7372800 | tf_op args[1]
  15.6 2.8 %all-to-all-done.moved_ref = bf16[32,24,128]{2,1,0:T(8,128)(2,1)S(1)} async-done(((bf16[32,24,128]{2,1,0:T(8,128)(2,1)}), bf16[32,24,128]{2,1,0:T(8,128)(2,1)S(1)}, u32[]{:S(2)}, u32[]{:S(2)}) %all-to-all-start) | async-done | bytes 196640 | tf_op jit(solution)/shard_map/all_to_all | solution.py:412
  18.5 0.0 copy-done.2
  18.5 0.0 copy-done
  18.5 0.0 copy-done.1
  18.5 10.5 %shard_map.56 = (bf16[4,96,1280]{2,1,0:T(8,128)(2,1)S(1)}, bf16[24,32,128]{2,1,0:T(8,128)(2,1)S(1)}, bf16[4,3,32,128]{3,2,1,0:T(8,128)(2,1)S(1)}, f32[24,32,128]...) custom-call(bf16[32,24,128]{2,1,0:T(8,128)(2,1)S(1)} %all-to-all-done.moved_ref, ...), custom_call_target="tpu_custom_call" | custom-call | tf_op jit(solution)/shard_map/pallas_call | solution.py:221
  29.0 2.9 %collective-permute-start = (bf16[18,32,128]{2,1,0:T(8,128)(2,1)S(1)}, bf16[18,32,128]{2,1,0:T(8,128)(2,1)S(1)}, u32[]{:S(2)}, u32[]{:S(2)}) collective-permute-start(bf16[18,32,128]{2,1,0:T(8,128)(2,1)S(1)} %get-tuple-element.20), channel_id=1, source_target_pairs={{0,8},{8,16},{16,24},{1,9},{9,17},{17,25},{2,10},{10,18},{18,26},{... | collective-permute-start | bytes 442376 | tf_op jit(solution)/shard_map/ppermute | solution.py:419
  31.9 1.3 %collective-permute-start.1 = (bf16[18,32,128]{2,1,0:T(8,128)(2,1)S(1)}, bf16[18,32,128]{2,1,0:T(8,128)(2,1)S(1)}, u32[]{:S(2)}, u32[]{:S(2)}) collective-permute-start(bf16[18,32,128]{2,1,0:T(8,128)(2,1)S(1)} %get-tuple-element.21), channel_id=1, source_target_pairs={{8,0},{16,8},{24,16},{9,1},{17,9},{25,17},{10,2},{18,10},{26,18},{... | collective-permute-start | bytes 442376 | tf_op jit(solution)/shard_map/ppermute | solution.py:420
  33.2 1.5 %collective-permute-done.above_ref = bf16[18,32,128]{2,1,0:T(8,128)(2,1)S(1)} collective-permute-done((bf16[18,32,128]{2,1,0:T(8,128)(2,1)S(1)}, bf16[18,32,128]{2,1,0:T(8,128)(2,1)S(1)}, u32[]{:S(2)}, u32[]{:S(2)}) %collective-permute-start) | collective-permute-done | bytes 147488 | tf_op jit(solution)/shard_map/ppermute | solution.py:419
  34.8 4.2 %collective-permute-done.1.below_ref = bf16[18,32,128]{2,1,0:T(8,128)(2,1)S(1)} collective-permute-done((bf16[18,32,128]{2,1,0:T(8,128)(2,1)S(1)}, bf16[18,32,128]{2,1,0:T(8,128)(2,1)S(1)}, u32[]{:S(2)}, u32[]{:S(2)}) %collective-permute-start.1) | collective-permute-done | bytes 147488 | tf_op jit(solution)/shard_map/ppermute | solution.py:420
  39.0 0.1 shard_map.57
  39.0 0.1 collective-permute-start.2
  39.1 1.6 %collective-permute-done.2.near_ref = bf16[40,32,128]{2,1,0:T(8,128)(2,1)S(1)} collective-permute-done((bf16[40,32,128]{2,1,0:T(8,128)(2,1)S(1)}, bf16[40,32,128]{2,1,0:T(8,128)(2,1)S(1)}, u32[]{:S(2)}, u32[]{:S(2)}) %collective-permute-start.2) | collective-permute-done | bytes 327712 | tf_op jit(solution)/shard_map/ppermute | solution.py:429
  40.7 0.1 shard_map.58
  40.9 0.7 collective-permute-start.3
  41.6 0.0 collective-permute-done.3.far_ref
  41.6 0.1 shard_map.59
  41.7 11.4 %collective-permute-start.4 = (bf16[24,32,128]{2,1,0:T(8,128)(2,1)S(1)}, bf16[24,32,128]{2,1,0:T(8,128)(2,1)S(1)}, u32[]{:S(2)}, u32[]{:S(2)}) collective-permute-start(bf16[24,32,128]{2,1,0:T(8,128)(2,1)S(1)} %get-tuple-element.28), channel_id=1, source_target_pairs={{0,1},{1,0},{2,3},{3,2},{4,5},{5,4},{6,7},{7,6},{8,9},{9,8},{10,11... | collective-permute-start | bytes 589832 | tf_op jit(solution)/shard_map/ppermute | solution.py:435
  53.1 0.5 shard_map.60.pooled_ref
  53.6 0.6 collective-permute-done.4.last_ref
  54.2 9.4 %shard_map.61 = f32[4,3,128,1200]{3,2,1,0:T(8,128)} custom-call(f32[24,32,128]{2,1,0:T(8,128)S(1)} %get-tuple-element.27.sum_ref, bf16[24,32,128]{2,1,0:T(8,128)(2,1)S(1)} %collective-permute-done.4.last_ref, bf16[24,32,128]{2,1,0:T(8,128)(2,1)S(1)} %get-tuple-element.29.window_ref, bf16[4,96,1280]{2,1,0:T(8,128)(2,1)S(1)} %get-tuple-element.30.patch_ref, ...), custom_call_target="tpu_custom_call" | custom-call | tf_op jit(solution)/shard_map/pallas_call | solution.py:385
  63.6 8.9 %copy.8 = f32[4,3,128,1200]{2,3,1,0:T(8,128)} copy(f32[4,3,128,1200]{3,2,1,0:T(8,128)} %shard_map.61) | data formatting | bytes 14745600 | tf_op jit(solution)/shard_map/pallas_call | solution.py:385
Async XLA Ops:
  0.0 18.5 %copy-start.2 = (bf16[256,128]{1,0:T(8,128)(2,1)S(1)}, bf16[256,128]{1,0:T(8,128)(2,1)}, u32[]{:S(2)}) copy-start(bf16[256,128]{1,0:T(8,128)(2,1)} %constant.8.clone.c_ref) | copy-start | bytes 196612
  0.0 18.5 %copy-start = (bf16[512,256]{1,0:T(8,128)(2,1)S(1)}, bf16[512,256]{1,0:T(8,128)(2,1)}, u32[]{:S(2)}) copy-start(bf16[512,256]{1,0:T(8,128)(2,1)} %constant.7.clone.b_ref) | copy-start | bytes 786436
  0.0 18.5 %copy-start.1 = (bf16[512,256]{1,0:T(8,128)(2,1)S(1)}, bf16[512,256]{1,0:T(8,128)(2,1)}, u32[]{:S(2)}) copy-start(bf16[512,256]{1,0:T(8,128)(2,1)} %constant.6.clone.a_ref) | copy-start | bytes 786436
  0.0 0.9 %copy-start.3 = (bf16[1,3,64,96]{3,2,1,0:T(8,128)(2,1)S(1)}, bf16[1,3,64,96]{3,2,1,0:T(8,128)(2,1)}, u32[]{:S(2)}) copy-start(bf16[1,3,64,96]{3,2,1,0:T(8,128)(2,1)} %images_ref.1) | copy-start | bytes 110596
  2.3 16.2 %all-to-all-start = ((bf16[32,24,128]{2,1,0:T(8,128)(2,1)}), bf16[32,24,128]{2,1,0:T(8,128)(2,1)S(1)}, u32[]{:S(2)}, u32[]{:S(2)}) async-start(bf16[32,24,128]{2,1,0:T(8,128)(2,1)} %bitcast), calls=%async_computation | async-start | bytes 393216 | tf_op jit(solution)/shard_map/all_to_all | solution.py:412
  29.0 5.8 %collective-permute-start = (bf16[18,32,128]{2,1,0:T(8,128)(2,1)S(1)}, bf16[18,32,128]{2,1,0:T(8,128)(2,1)S(1)}, u32[]{:S(2)}, u32[]{:S(2)}) collective-permute-start(bf16[18,32,128]{2,1,0:T(8,128)(2,1)S(1)} %get-tuple-element.20), channel_id=1, source_target_pairs={{0,8},{8,16},{16,24},{1,9},{9,17},{17,25},{2,10},{10,18},{18,26},{... | collective-permute-start | bytes 442376 | tf_op jit(solution)/shard_map/ppermute | solution.py:419
  31.9 7.0 %collective-permute-start.1 = (bf16[18,32,128]{2,1,0:T(8,128)(2,1)S(1)}, bf16[18,32,128]{2,1,0:T(8,128)(2,1)S(1)}, u32[]{:S(2)}, u32[]{:S(2)}) collective-permute-start(bf16[18,32,128]{2,1,0:T(8,128)(2,1)S(1)} %get-tuple-element.21), channel_id=1, source_target_pairs={{8,0},{16,8},{24,16},{9,1},{17,9},{25,17},{10,2},{18,10},{26,18},{... | collective-permute-start | bytes 442376 | tf_op jit(solution)/shard_map/ppermute | solution.py:420
  39.0 1.7 %collective-permute-start.2 = (bf16[40,32,128]{2,1,0:T(8,128)(2,1)S(1)}, bf16[40,32,128]{2,1,0:T(8,128)(2,1)S(1)}, u32[]{:S(2)}, u32[]{:S(2)}) collective-permute-start(bf16[40,32,128]{2,1,0:T(8,128)(2,1)S(1)} %get-tuple-element.24), channel_id=1, source_target_pairs={{0,1},{1,0},{2,3},{3,2},{4,5},{5,4},{6,7},{7,6},{8,9},{9,8},{10,11... | collective-permute-start | bytes 983048 | tf_op jit(solution)/shard_map/ppermute | solution.py:429
  40.9 0.7 collective-permute-start.3
  41.7 12.4 %collective-permute-start.4 = (bf16[24,32,128]{2,1,0:T(8,128)(2,1)S(1)}, bf16[24,32,128]{2,1,0:T(8,128)(2,1)S(1)}, u32[]{:S(2)}, u32[]{:S(2)}) collective-permute-start(bf16[24,32,128]{2,1,0:T(8,128)(2,1)S(1)} %get-tuple-element.28), channel_id=1, source_target_pairs={{0,1},{1,0},{2,3},{3,2},{4,5},{5,4},{6,7},{7,6},{8,9},{9,8},{10,11... | collective-permute-start | bytes 589832 | tf_op jit(solution)/shard_map/ppermute | solution.py:435
where the time goes:
time: 73 us; the launch traced here: 72.5 us
  starting transfers between devices  23.6 us (32%)
  Pallas kernels  22.2 us (30%)
  local copies, waits for them, and re-layouts  15.8 us (22%)
  waiting for transfers between devices  10.8 us (15%)
    ppermute x1, starting transfers between devices, body(): last = lax.ppermute(send, 'col', swap)  11.4 us
    pallas_call x1, Pallas kernels, encode(): pl.pallas_call(functools.partial(encode_kernel, z), grid=(z.rd,), out_sha...  10.5 us
    pallas_call x1, Pallas kernels, gradient(): pl.pallas_call(functools.partial(grad_kernel, z), grid=(z.rd,), out_shape...  9.42 us
    pallas_call x1, local copies, waits for them, and re-layouts, gradient(): pl.pallas_call(functools.partial(grad_kernel, z), grid=(z.rd,), out_shape...  8.9 us
    all_to_all x1, starting transfers between devices, body(): lax.all_to_all(blocks.reshape(z.R * z.C, z.bd * z.T, L), ('row', 'col'),...  7.3 us
    unnamed x9, local copies, waits for them, and re-layouts  6.92 us
    ppermute x1, waiting for transfers between devices, body(): below = lax.ppermute(up, 'row', above_to)  4.19 us
    ppermute x1, starting transfers between devices, body(): above = lax.ppermute(down, 'row', below_to)  2.93 us
  transfers between devices with their start and end apart: 6, of which 5 were waited for; matrix products, arithmetic and copies ran while one was open for 8% of the time, Pallas kernels for 1%

commit v1 on v0

v1 whole, which is shorter than its diff:
```python
import functools

import jax
import jax.numpy as jnp
from jax import lax
from jax.experimental import pallas as pl
from jax.experimental.pallas import tpu as pltpu
from jax.sharding import PartitionSpec as P

CH = 3
S = 4
FIELD = 20
PAD = 8
K = 1200
MARGIN = 16
HELD = 2
GROUP = FIELD // S

sparsity = 0.5
f32 = jnp.float32
bf16 = jnp.bfloat16
NT = (((1,), (1,)), ((), ()))
NN = (((1,), (0,)), ((), ()))
TN = (((0,), (0,)), ((), ()))
MIB = 1024 * 1024


def dot(a, b, dims=NN):
    return lax.dot_general(a, b, dims, preferred_element_type=f32)


class Sizes:
    def __init__(self, images, weights, mesh):
        self.R, self.C = mesh.shape["row"], mesh.shape["col"]
        self.bd = images[0]
        self.height, self.width = images[2], images[3]
        self.rd, self.cd, self.F = weights[0], weights[1], weights[2]
        self.B = self.bd * self.R * self.C
        self.h, self.w = S * self.rd, S * self.cd
        self.ext = self.w + 2 * PAD
        self.stride = -(-self.ext // 32) * 32
        self.lanes = S * self.stride
        self.YB = self.rd + 2 * PAD // S
        self.T = CH * self.YB
        self.KW = CH * FIELD * self.stride
        self.per = 128 // self.B
        self.groups = self.rd // self.per
        assert self.B * self.per == 128 and self.groups * self.per == self.rd and self.F == 128
        assert self.C % 2 == 0 and self.R % 2 == 0 and self.rd >= 4 and self.cd >= 2 and self.lanes == 128
        assert self.height == self.R * self.h and self.width == self.C * self.w


def split_kernel(z, images_ref, out_ref, rows_ref, pad_ref):
    margin = PAD // S
    blocks = z.height // S
    n = lax.broadcasted_iota(jnp.int32, (1, z.C * z.lanes), 1)
    column = n // z.lanes
    inner = n % z.lanes
    lane_row = inner // z.stride
    across = inner % z.stride
    source = jnp.where(across < z.ext, z.w * column - PAD + across, -1)
    pixel = lax.broadcasted_iota(jnp.int32, (128, z.C * z.lanes), 0)
    chunks = rows_ref.shape[1]
    rows_ref[...] = jnp.zeros_like(rows_ref)
    for i in range(z.bd):
        pixels = images_ref[i].astype(f32)
        count = CH * z.height * z.width
        center = jnp.sum(pixels) / count
        moved = pixels - center
        variance = jnp.sum(moved * moved) / count
        normed = (moved / jnp.sqrt(variance + 1e-05)).astype(bf16).astype(f32)
        for k in range(chunks):
            stop = min(128, z.width - 128 * k)
            rows_ref[:, k, :, :stop] = normed[:, :, 128 * k : 128 * k + stop]
        total = jnp.zeros((CH * blocks, z.C * z.lanes), f32)
        for k in range(chunks):
            for j in range(S):
                line = jnp.concatenate(
                    [rows_ref[c, k, pl.ds(j, blocks, stride=S), :] for c in range(CH)], axis=0
                ).astype(bf16)
                wanted = jnp.where(lane_row == j, source - 128 * k, -1)
                total = total + dot(line, (pixel == wanted).astype(f32).astype(bf16))
        pad_ref[...] = jnp.zeros_like(pad_ref)
        for c in range(CH):
            pad_ref[c, margin : margin + blocks, :] = total[c * blocks : (c + 1) * blocks]
        for r in range(z.R):
            for q in range(z.C):
                block = [
                    pad_ref[c, z.rd * r : z.rd * r + z.YB, q * z.lanes : (q + 1) * z.lanes]
                    for c in range(CH)
                ]
                out_ref[r * z.C + q, i] = jnp.concatenate(block, axis=0).astype(bf16)


def split(z, images):
    return pl.pallas_call(
        functools.partial(split_kernel, z),
        out_shape=pltpu.VMEM((z.R * z.C, z.bd, z.T, z.lanes), bf16),
        in_specs=[pl.BlockSpec(memory_space=pltpu.VMEM)],
        out_specs=pl.BlockSpec(memory_space=pltpu.VMEM),
        scratch_shapes=[
            pltpu.VMEM((CH, -(-z.width // 128), z.height, 128), f32),
            pltpu.VMEM((CH, z.height // S + 2 * PAD // S, z.C * z.lanes), f32),
        ],
        compiler_params=pltpu.CompilerParams(vmem_limit_bytes=32 * MIB),
    )(images)


def spread_kernel(z, weights_ref, out_ref, rows_ref):
    row = lax.broadcasted_iota(jnp.int32, (z.stride, z.F), 0)
    for q in range(z.cd):
        rows_ref[MARGIN : MARGIN + K, :] = weights_ref[0, q].astype(f32)
        inside = (row >= S * q) & (row < S * q + FIELD)
        for i in range(CH * FIELD):
            at = MARGIN + FIELD * i - S * q
            value = jnp.where(inside, rows_ref[at : at + z.stride, :], 0.0)
            out_ref[0, z.stride * i : z.stride * (i + 1), q * z.F : (q + 1) * z.F] = value.astype(bf16)


def spread_weights(z, weights, first, count, space):
    return pl.pallas_call(
        functools.partial(spread_kernel, z),
        grid=(count,),
        out_shape=space((count, z.KW, z.cd * z.F), bf16),
        in_specs=[pl.BlockSpec((1, z.cd, K, z.F), lambda p: (p + first, 0, 0, 0))],
        out_specs=pl.BlockSpec((1, z.KW, z.cd * z.F), lambda p: (p, 0, 0)),
        scratch_shapes=[pltpu.VMEM((K + 2 * MARGIN, z.F), f32)],
        compiler_params=pltpu.CompilerParams(vmem_limit_bytes=32 * MIB),
    )(weights)


def field(z, p, tiles_ref):
    return jnp.concatenate(
        [tiles_ref[c * z.YB + p + g] for c in range(CH) for g in range(GROUP)], axis=1
    )


def encode_kernel(
    z, moved_ref, first_ref, wide_hbm, window_ref, hidden_ref, contrib_ref, swap_ref, cross_ref, wide_ref, rows_ref, sems
):
    B = z.B
    copies = [pltpu.make_async_copy(wide_hbm.at[p], wide_ref.at[p], sems.at[p]) for p in range(z.rd - HELD)]
    for copy in copies[:2]:
        copy.start()
    rows_ref[...] = moved_ref[...].reshape(B * z.T, z.lanes).astype(f32)
    for t in range(z.T):
        window_ref[t] = rows_ref[pl.ds(t, B, stride=z.T), :].astype(bf16)
    contrib_ref[...] = jnp.zeros_like(contrib_ref)
    for p in range(z.rd):
        if p >= HELD:
            copies[p - HELD].wait()
            if p - HELD + 2 < len(copies):
                copies[p - HELD + 2].start()
        weight = first_ref.at[p] if p < HELD else wide_ref.at[p - HELD]
        hidden = dot(field(z, p, window_ref), weight[...]).astype(bf16)
        for q in range(z.cd):
            hidden_ref[p, q] = hidden[:, q * z.F : (q + 1) * z.F]
        terms = dot(hidden, weight[...], NT)
        for c in range(CH):
            for g in range(GROUP):
                at = (c * GROUP + g) * z.lanes
                contrib_ref[c * z.YB + p + g] += terms[:, at : at + z.lanes]
    half = z.YB // 2
    even = row_is_even()
    for ref, below in ((swap_ref, even), (cross_ref, jnp.logical_not(even))):
        first = jnp.where(below, z.YB - half, 0)
        row = jnp.where(below, z.rd - 2, 0)
        for c in range(CH):
            for y in range(half):
                ref[c * half + y] = contrib_ref[c * z.YB + first + y].astype(bf16)
        for i in range(2):
            for q in range(z.cd):
                ref[CH * half + i * z.cd + q] = hidden_ref[row + i, q]


def encode(z, moved, first, wide):
    B, L = z.B, z.lanes
    vmem = pl.BlockSpec(memory_space=pltpu.VMEM)
    sent = CH * (z.YB // 2) + 2 * z.cd
    shapes = [
        ((z.T, B, L), bf16),
        ((z.rd, z.cd, B, z.F), bf16),
        ((z.T, B, L), f32),
        ((sent, B, L), bf16),
        ((sent, B, L), bf16),
        ((z.rd - HELD, z.KW, z.cd * z.F), bf16),
    ]
    return pl.pallas_call(
        functools.partial(encode_kernel, z),
        out_shape=[pltpu.VMEM(*s) for s in shapes],
        in_specs=[vmem, vmem, pl.BlockSpec(memory_space=pltpu.HBM)],
        out_specs=[vmem] * len(shapes),
        scratch_shapes=[
            pltpu.VMEM((B * z.T, L), f32),
            pltpu.SemaphoreType.DMA((z.rd - HELD,)),
        ],
        compiler_params=pltpu.CompilerParams(vmem_limit_bytes=32 * MIB),
    )(moved, first, pltpu.with_memory_space_constraint(wide, pltpu.HBM))


def turn_fields(z, tile_of, flat_ref):
    for group in range(z.groups):
        for c in range(CH):
            for g in range(GROUP):
                first = c * z.YB + group * z.per + g
                stack = jnp.concatenate([tile_of(first + p) for p in range(z.per)], axis=0)
                at = (c * GROUP + g) * z.lanes
                flat_ref[group, at : at + z.lanes, :] = stack.astype(f32).T


def place_fields(z, q, flat_ref, dense_ref, out_ref):
    for group in range(z.groups):
        for i in range(CH * FIELD):
            at = z.stride * i + S * q
            dense_ref[FIELD * i : FIELD * (i + 1), :] = flat_ref[group, at : at + FIELD, :]
        out_ref[q, group] = dense_ref[...].astype(bf16)


def patches_kernel(z, window_ref, out_ref, flat_ref, dense_ref):
    turn_fields(z, lambda t: window_ref[t], flat_ref)
    for q in range(z.cd):
        place_fields(z, q, flat_ref, dense_ref, out_ref)


def vmem_call(kernel, shapes, scratch, *args):
    vmem = pl.BlockSpec(memory_space=pltpu.VMEM)
    return pl.pallas_call(
        kernel,
        out_shape=[pltpu.VMEM(*s) for s in shapes],
        in_specs=[vmem] * len(args),
        out_specs=[vmem] * len(shapes),
        scratch_shapes=[pltpu.VMEM(*s) for s in scratch],
        compiler_params=pltpu.CompilerParams(vmem_limit_bytes=32 * MIB),
    )(*args)


def is_even():
    return lax.rem(lax.axis_index("col"), 2) == 0


def row_is_even():
    return lax.rem(lax.axis_index("row"), 2) == 0


def pack_side(z, to_right, first, second):
    wide = 2 * PAD
    across = lax.broadcasted_iota(jnp.int32, first.shape, 1) % z.stride
    low = pltpu.roll(first, jnp.where(to_right, z.lanes - z.w, 0), 1)
    high = pltpu.roll(second, jnp.where(to_right, z.lanes - z.w + wide, wide) % z.lanes, 1)
    return jnp.where(across < wide, low, jnp.where(across < 2 * wide, high, 0.0))


def unpack_side(z, from_left, packed):
    wide = 2 * PAD
    across = lax.broadcasted_iota(jnp.int32, packed.shape, 1) % z.stride
    start = jnp.where(from_left, 0, z.w)
    inside = (across >= start) & (across < start + wide)
    first = pltpu.roll(packed, start, 1)
    second = pltpu.roll(packed, (start + z.lanes - wide) % z.lanes, 1)
    return jnp.where(inside, first, 0.0), jnp.where(inside, second, 0.0)


def rows_kernel(z, contrib_ref, hidden_ref, swap_ref, cross_ref, sum_ref, tall_ref, send_ref):
    half = z.YB // 2
    sum_ref[...] = contrib_ref[...]
    for i in range(z.rd):
        for q in range(z.cd):
            tall_ref[2 + i, q] = hidden_ref[i, q]
    row = lax.axis_index("row")
    even_row = row_is_even()
    for ref, below in ((swap_ref, even_row), (cross_ref, jnp.logical_not(even_row))):
        exists = jnp.where(below, row < z.R - 1, row > 0)
        first = jnp.where(below, z.YB - half, 0)
        at = jnp.where(below, z.rd + 2, 0)
        for c in range(CH):
            for y in range(half):
                sum_ref[c * z.YB + first + y] += jnp.where(exists, ref[c * half + y].astype(f32), 0.0)
        for i in range(2):
            for q in range(z.cd):
                value = ref[CH * half + i * z.cd + q]
                tall_ref[at + i, q] = jnp.where(exists, value, jnp.zeros_like(value))
    even = is_even()
    for t in range(0, z.T, 2):
        send_ref[t // 2] = pack_side(z, even, sum_ref[t], sum_ref[t + 1]).astype(bf16)
    first = jnp.where(even, z.cd - 2, 0)
    for i in range(z.rd + 4):
        for k in range(2):
            send_ref[z.T // 2 + 2 * i + k] = tall_ref[i, first + k]


def near_kernel(z, sum_ref, tall_ref, near_ref, out_ref, send_ref):
    even = is_even()
    for t in range(0, z.T, 2):
        came = unpack_side(z, jnp.logical_not(even), near_ref[t // 2].astype(f32))
        total = [sum_ref[t + k] + came[k] for k in range(2)]
        for k in range(2):
            out_ref[t + k] = total[k]
        send_ref[t // 2] = pack_side(z, jnp.logical_not(even), *total).astype(bf16)
    first = jnp.where(even, 0, z.cd - 2)
    for i in range(z.rd + 4):
        for k in range(2):
            send_ref[z.T // 2 + 2 * i + k] = tall_ref[i, first + k]


def far_kernel(z, sum_ref, far_ref, out_ref, send_ref):
    even = is_even()
    exists = jnp.where(even, lax.axis_index("col") > 0, lax.axis_index("col") < z.C - 1)
    for t in range(0, z.T, 2):
        came = unpack_side(z, even, jnp.where(exists, far_ref[t // 2].astype(f32), 0.0))
        for k in range(2):
            out_ref[t + k] = sum_ref[t + k] + came[k]
        send_ref[t // 2] = pack_side(z, even, *came).astype(bf16)


def pool_kernel(z, tall_ref, near_ref, far_ref, out_ref, wide_ref, inverse_ref):
    even = is_even()
    row0 = lax.axis_index("row") * z.rd - 1
    col0 = lax.axis_index("col") * z.cd - 1
    near_at = jnp.where(even, z.cd + 2, 0)
    far_at = jnp.where(even, 0, z.cd + 2)
    exists = jnp.where(even, lax.axis_index("col") > 0, lax.axis_index("col") < z.C - 1)
    for i in range(z.rd + 4):
        for k in range(2):
            wide_ref[i, near_at + k] = near_ref[z.T // 2 + 2 * i + k]
            far = far_ref[z.T // 2 + 2 * i + k]
            wide_ref[i, far_at + k] = jnp.where(exists, far, jnp.zeros_like(far))
        for q in range(z.cd):
            wide_ref[i, 2 + q] = tall_ref[i, q]
    for i in range(z.rd + 2):
        columns = []
        for q in range(z.cd + 4):
            parts = [jnp.square(wide_ref[i + d, q].astype(f32)) for d in range(3)]
            columns.append(parts[0] + parts[1] + parts[2])
        for q in range(z.cd + 2):
            energy = jnp.sqrt(1.0 + (columns[q] + columns[q + 1] + columns[q + 2]))
            inverse = (1.0 / energy).astype(bf16).astype(f32)
            row, col = row0 + i, col0 + q
            inside = (row >= 0) & (row < z.R * z.rd) & (col >= 0) & (col < z.C * z.cd)
            inverse_ref[i, q] = inverse * jnp.where(inside, 1.0, 0.0)
    for i in range(z.rd):
        columns = []
        for q in range(z.cd + 2):
            columns.append(inverse_ref[i, q] + inverse_ref[i + 1, q] + inverse_ref[i + 2, q])
        for q in range(z.cd):
            spread = columns[q] + columns[q + 1] + columns[q + 2]
            out_ref[i, q] = sparsity * tall_ref[2 + i, q].astype(f32) * spread


CHUNKS = 3


def grad_kernel(
    z, sum_ref, last_ref, window_ref, patch_ref, hidden_ref, pooled_ref, first_ref, wide_ref,
    out_hbm, resid_ref, flat_ref, dense_ref, resid_patch_ref, factor_ref, out_ref, sems,
):
    B, F = z.B, z.F
    from_left = jnp.logical_not(is_even())
    lane = lax.broadcasted_iota(jnp.int32, (1, z.lanes), 1) % z.stride
    x = lax.axis_index("col") * z.w - PAD + lane
    across = ((x >= 0) & (x < z.width)).astype(f32)
    first = lax.axis_index("row") * z.h - PAD
    for t in range(0, z.T, 2):
        came = unpack_side(z, from_left, last_ref[t // 2].astype(f32))
        for n in range(2):
            line = first + S * ((t + n) % z.YB)
            inside = jnp.where((line >= 0) & (line < z.height), across, 0.0)
            recon = sum_ref[t + n] + came[n]
            resid_ref[t + n] = ((recon - window_ref[t + n].astype(f32)) * inside).astype(bf16)

    turn_fields(z, lambda t: resid_ref[t], flat_ref)
    factor_ref[...] = jnp.zeros_like(factor_ref)
    size = K // CHUNKS
    copies = []
    for q in range(z.cd):
        for p in range(z.rd):
            weight = first_ref.at[p] if p < HELD else wide_ref.at[p - HELD]
            back = dot(field(z, p, resid_ref), weight[:, q * F : (q + 1) * F])
            group, inner = p // z.per, p % z.per
            columns = slice(inner * F, (inner + 1) * F)
            at = inner * B
            factor_ref[q, group, at : at + B, columns] = (pooled_ref[p, q] + back).astype(bf16)
            factor_ref[q, group, 128 + at : 128 + at + B, columns] = hidden_ref[p, q]
        place_fields(z, q, flat_ref, dense_ref, resid_patch_ref)
        for k in range(CHUNKS):
            rows = slice(k * size, (k + 1) * size)
            for group in range(z.groups):
                both = jnp.concatenate([patch_ref[q, group, rows, :], resid_patch_ref[q, group, rows, :]], axis=1)
                value = dot(both, factor_ref[q, group]) * (1.0 / B)
                for inner in range(z.per):
                    out_ref[group * z.per + inner, q, rows, :] = value[:, inner * F : (inner + 1) * F]
            copy = pltpu.make_async_copy(out_ref.at[:, q, rows, :], out_hbm.at[:, q, rows, :], sems.at[q, k])
            copy.start()
            copies.append(copy)
    for copy in copies:
        copy.wait()


def gradient(z, *args):
    B, F, L = z.B, z.F, z.lanes
    return pl.pallas_call(
        functools.partial(grad_kernel, z),
        out_shape=pltpu.HBM((z.rd, z.cd, K, F), f32),
        in_specs=[pl.BlockSpec(memory_space=pltpu.VMEM)] * len(args),
        out_specs=pl.BlockSpec(memory_space=pltpu.HBM),
        scratch_shapes=[
            pltpu.VMEM((z.T, B, L), bf16),
            pltpu.VMEM((z.groups, z.KW, 128), f32),
            pltpu.VMEM((K, 128), f32),
            pltpu.VMEM((z.cd, z.groups, K, 128), bf16),
            pltpu.VMEM((z.cd, z.groups, 256, z.per * F), bf16),
            pltpu.VMEM((z.rd, z.cd, K, F), f32),
            pltpu.SemaphoreType.DMA((z.cd, CHUNKS)),
        ],
        compiler_params=pltpu.CompilerParams(vmem_limit_bytes=40 * MIB),
    )(*args)


def exchange(z, value, partner):
    pairs = []
    for r in range(z.R):
        for c in range(z.C):
            to = partner(z, r, c)
            pairs.append((r * z.C + c, to[0] * z.C + to[1]))
    return lax.ppermute(value, ("row", "col"), pairs)


def cross_row(z, r, c):
    to = r + 1 if r % 2 else r - 1
    return (to, c) if 0 <= to < z.R else (r, c ^ 1)


def swap_col(z, r, c):
    return (r, c ^ 1)


def cross_col(z, r, c):
    to = c + 1 if c % 2 else c - 1
    return (r, to) if 0 <= to < z.C else (r ^ 1, c)


def body(z, images, weights):
    B, L = z.B, z.lanes
    tiles = ((z.T, B, L), f32)
    blocks = split(z, images)
    moved = lax.all_to_all(
        blocks.reshape(z.R * z.C, z.bd * z.T, L), ("row", "col"), split_axis=0, concat_axis=0, tiled=True
    ).reshape(B, z.T, L)
    turned = jnp.swapaxes(weights, 2, 3)
    wide_first = spread_weights(z, turned, 0, HELD, pltpu.VMEM)
    wide = spread_weights(z, turned, HELD, z.rd - HELD, pltpu.HBM)
    window, hidden, contrib, to_swap, to_cross, wide = encode(z, moved, wide_first, wide)
    crossed = exchange(z, to_cross, cross_row)
    swapped = exchange(z, to_swap, lambda z, r, c: (r ^ 1, c))
    tall = ((z.rd + 4, z.cd, B, z.F), bf16)
    sent = ((z.T // 2 + 2 * (z.rd + 4), B, L), bf16)
    total, tall, send = vmem_call(
        functools.partial(rows_kernel, z), [tiles, tall, sent], [], contrib, hidden, swapped, crossed
    )
    near = exchange(z, send, swap_col)
    total, send = vmem_call(functools.partial(near_kernel, z), [tiles, sent], [], total, tall, near)
    far = exchange(z, send, cross_col)
    total, send = vmem_call(
        functools.partial(far_kernel, z), [tiles, ((z.T // 2, B, L), bf16)], [], total, far
    )
    last = exchange(z, send, swap_col)
    (pooled,) = vmem_call(
        functools.partial(pool_kernel, z),
        [((z.rd, z.cd, B, z.F), f32)],
        [((z.rd + 4, z.cd + 4, B, z.F), bf16), ((z.rd + 2, z.cd + 2, B, z.F), f32)],
        tall, near, far,
    )
    (patch,) = vmem_call(
        functools.partial(patches_kernel, z),
        [((z.cd, z.groups, K, 128), bf16)],
        [((z.groups, z.KW, 128), f32), ((K, 128), f32)],
        window,
    )
    return jnp.swapaxes(gradient(z, total, last, window, patch, hidden, pooled, wide_first, wide), 2, 3)


def solution(mesh):
    def run(images, weights):
        z = Sizes(
            (images.shape[0] // (mesh.shape["row"] * mesh.shape["col"]),) + images.shape[1:],
            (weights.shape[0] // mesh.shape["row"], weights.shape[1] // mesh.shape["col"]) + weights.shape[2:],
            mesh,
        )
        return jax.shard_map(
            functools.partial(body, z),
            mesh=mesh,
            in_specs=(P(("row", "col"), None, None, None), P("row", "col", None, None)),
            out_specs=P("row", "col", None, None),
            check_vma=False,
        )(images, weights)

    return run
```

time: 73 us -> 43.6 us (0.60)
  local copies, waits for them, and re-layouts: 15.8 us -> 2.84 us
  starting transfers between devices: 23.6 us -> 11.5 us
  Pallas kernels: 22.2 us -> 13.6 us
  waiting for transfers between devices: 10.8 us -> 15.3 us
    ppermute x5, starting transfers between devices: 16.3 us -> 4.18 us  [exchange(): return lax.ppermute(value, ('row', 'col'), pairs)]
    pallas_call x1 -> x0, local copies, waits for them, and re-layouts: 8.9 us -> none  [gradient(): pl.pallas_call(functools.partial(grad_kernel, z), grid=(z.rd,), out_shape...]
    pallas_call x7 -> x10, Pallas kernels: 22.2 us -> 13.6 us  [the longest x1 4.06 us: gradient(): pl.pallas_call(functools.partial(grad_kernel, z), out_shape=pltpu.HBM((z....]
    unnamed x9 -> x4, local copies, waits for them, and re-layouts: 6.92 us -> 2.84 us
    ppermute x5, waiting for transfers between devices: 7.92 us -> 11.1 us  [exchange(): return lax.ppermute(value, ('row', 'col'), pairs)]
    all_to_all x1, waiting for transfers between devices: 2.84 us -> 4.25 us  [body(): lax.all_to_all(blocks.reshape(z.R * z.C, z.bd * z.T, L), ('row', 'col'),...]
  transfers between devices with their start and end apart: 6 -> 6, of which waited for: 5 -> 4; matrix products, arithmetic and copies ran while one was open for 8% -> 0% of each run, Pallas kernels for 1% -> 8%
where the time goes in v1:
time: 43.6 us; the launch traced here: 43.3 us
  waiting for transfers between devices  15.3 us (35%)
  Pallas kernels  13.6 us (31%)
  starting transfers between devices  11.5 us (26%)
  local copies, waits for them, and re-layouts  2.84 us (7%)
    ppermute x5, waiting for transfers between devices, exchange(): return lax.ppermute(value, ('row', 'col'), pairs)  11.1 us
    all_to_all x1, starting transfers between devices, body(): lax.all_to_all(blocks.reshape(z.R * z.C, z.bd * z.T, L), ('row', 'col'),...  7.3 us
    all_to_all x1, waiting for transfers between devices, body(): lax.all_to_all(blocks.reshape(z.R * z.C, z.bd * z.T, L), ('row', 'col'),...  4.25 us
    ppermute x5, starting transfers between devices, exchange(): return lax.ppermute(value, ('row', 'col'), pairs)  4.18 us
    pallas_call x1, Pallas kernels, gradient(): pl.pallas_call(functools.partial(grad_kernel, z), out_shape=pltpu.HBM((z....  4.06 us
    pallas_call x1, Pallas kernels, encode(): pl.pallas_call(functools.partial(encode_kernel, z), out_shape=[pltpu.VMEM...  3.94 us
    unnamed x4, local copies, waits for them, and re-layouts  2.84 us
    pallas_call x2, Pallas kernels, spread_weights(): pl.pallas_call(functools.partial(spread_kernel, z), grid=(count,), out_sh...  2.58 us
  transfers between devices with their start and end apart: 6, of which 4 were waited for; matrix products, arithmetic and copies ran while one was open for 0% of the time, Pallas kernels for 8%

profile of v1, /device:TPU:0, one launch (start us, length us, event | category | flops | bytes accessed | tf_op | source)
XLA Modules:
  0.0 43.3 jit_solution(2888768145461010751)
XLA Ops:
  0.0 0.0 copy-start.1
  0.0 0.8 %copy-done.1 = bf16[1,3,64,96]{3,2,1,0:T(8,128)(2,1)S(1)} copy-done((bf16[1,3,64,96]{3,2,1,0:T(8,128)(2,1)S(1)}, bf16[1,3,64,96]{3,2,1,0:T(8,128)(2,1)}, u32[]{:S(2)}) %copy-start.1) | copy-done | bytes 36888
  0.8 1.4 %shard_map.28 = bf16[32,1,24,128]{3,2,1,0:T(8,128)(2,1)} custom-call(bf16[1,3,64,96]{3,2,1,0:T(8,128)(2,1)S(1)} %copy-done.1), custom_call_target="tpu_custom_call" | custom-call | tf_op jit(solution)/shard_map/pallas_call | solution.py:96
  2.2 7.3 %all-to-all-start = ((bf16[32,24,128]{2,1,0:T(8,128)(2,1)}), bf16[32,24,128]{2,1,0:T(8,128)(2,1)S(1)}, u32[]{:S(2)}, u32[]{:S(2)}) async-start(bf16[32,24,128]{2,1,0:T(8,128)(2,1)} %bitcast), calls=%async_computation | async-start | bytes 393216 | tf_op jit(solution)/shard_map/all_to_all | solution.py:445
  9.5 0.0 copy-start
  9.5 2.0 %copy-done = bf16[4,3,128,1200]{2,3,1,0:T(8,128)(2,1)S(1)} copy-done((bf16[4,3,128,1200]{2,3,1,0:T(8,128)(2,1)S(1)}, bf16[4,3,128,1200]{2,3,1,0:T(8,128)(2,1)}, u32[]{:S(2)}) %copy-start) | copy-done | bytes 3686424
  11.5 0.6 %shard_map.29.first_ref = bf16[2,1920,384]{2,1,0:T(8,128)(2,1)S(1)} custom-call(bf16[4,3,1200,128]{3,2,1,0:T(8,128)(2,1)S(1)} %bitcast.3), custom_call_target="tpu_custom_call" | custom-call | tf_op jit(solution)/shard_map/pallas_call | solution.py:121
  12.2 1.9 %shard_map.30.wide_hbm = bf16[2,1920,384]{2,1,0:T(8,128)(2,1)} custom-call(bf16[4,3,1200,128]{3,2,1,0:T(8,128)(2,1)S(1)} %bitcast.4), custom_call_target="tpu_custom_call" | custom-call | tf_op jit(solution)/shard_map/pallas_call | solution.py:121
  14.1 4.2 %all-to-all-done.moved_ref = bf16[32,24,128]{2,1,0:T(8,128)(2,1)S(1)} async-done(((bf16[32,24,128]{2,1,0:T(8,128)(2,1)}), bf16[32,24,128]{2,1,0:T(8,128)(2,1)S(1)}, u32[]{:S(2)}, u32[]{:S(2)}) %all-to-all-start) | async-done | bytes 196640 | tf_op jit(solution)/shard_map/all_to_all | solution.py:445
  18.4 3.9 %shard_map.31 = (bf16[24,32,128]{2,1,0:T(8,128)(2,1)S(1)}, bf16[4,3,32,128]{3,2,1,0:T(8,128)(2,1)S(1)}, f32[24,32,128]{2,1,0:T(8,128)S(1)}, bf16[18,32,128]{2,1,...) custom-call(bf16[32,24,128]{2,1,0:T(8,128)(2,1)S(1)} %all-to-all-done.moved_ref, ...), custom_call_target="tpu_custom_call" | custom-call | tf_op jit(solution)/shard_map/pallas_call | solution.py:188
  22.3 1.1 %collective-permute-start = (bf16[18,32,128]{2,1,0:T(8,128)(2,1)S(1)}, bf16[18,32,128]{2,1,0:T(8,128)(2,1)S(1)}, u32[]{:S(2)}, u32[]{:S(2)}) collective-permute-start(bf16[18,32,128]{2,1,0:T(8,128)(2,1)S(1)} %get-tuple-element.20), channel_id=1, source_target_pairs={{0,8},{1,9},{2,10},{3,11},{4,12},{5,13},{6,14},{7,15},{8,0},{9,1},... | collective-permute-start | bytes 442376 | tf_op jit(solution)/shard_map/ppermute | solution.py:424
  23.4 0.0 collective-permute-start.1
  23.4 5.3 %collective-permute-done.swap_ref = bf16[18,32,128]{2,1,0:T(8,128)(2,1)S(1)} collective-permute-done((bf16[18,32,128]{2,1,0:T(8,128)(2,1)S(1)}, bf16[18,32,128]{2,1,0:T(8,128)(2,1)S(1)}, u32[]{:S(2)}, u32[]{:S(2)}) %collective-permute-start) | collective-permute-done | bytes 147488 | tf_op jit(solution)/shard_map/ppermute | solution.py:424
  28.7 0.0 collective-permute-done.1.cross_ref
  28.7 0.3 shard_map.32
  29.0 0.1 collective-permute-start.2
  29.1 1.5 %collective-permute-done.2.near_ref = bf16[28,32,128]{2,1,0:T(8,128)(2,1)S(1)} collective-permute-done((bf16[28,32,128]{2,1,0:T(8,128)(2,1)S(1)}, bf16[28,32,128]{2,1,0:T(8,128)(2,1)S(1)}, u32[]{:S(2)}, u32[]{:S(2)}) %collective-permute-start.2) | collective-permute-done | bytes 229408 | tf_op jit(solution)/shard_map/ppermute | solution.py:424
  30.6 0.2 shard_map.33
  30.8 1.8 %collective-permute-start.3 = (bf16[28,32,128]{2,1,0:T(8,128)(2,1)S(1)}, bf16[28,32,128]{2,1,0:T(8,128)(2,1)S(1)}, u32[]{:S(2)}, u32[]{:S(2)}) collective-permute-start(bf16[28,32,128]{2,1,0:T(8,128)(2,1)S(1)} %get-tuple-element.26), channel_id=1, source_target_pairs={{0,8},{1,2},{2,1},{3,4},{4,3},{5,6},{6,5},{7,15},{8,0},{9,10},{10,... | collective-permute-start | bytes 688136 | tf_op jit(solution)/shard_map/ppermute | solution.py:424
  32.6 4.3 %collective-permute-done.3.far_ref = bf16[28,32,128]{2,1,0:T(8,128)(2,1)S(1)} collective-permute-done((bf16[28,32,128]{2,1,0:T(8,128)(2,1)S(1)}, bf16[28,32,128]{2,1,0:T(8,128)(2,1)S(1)}, u32[]{:S(2)}, u32[]{:S(2)}) %collective-permute-start.3) | collective-permute-done | bytes 229408 | tf_op jit(solution)/shard_map/ppermute | solution.py:424
  36.9 0.2 shard_map.34
  37.1 1.2 %collective-permute-start.4 = (bf16[12,32,128]{2,1,0:T(8,128)(2,1)S(1)}, bf16[12,32,128]{2,1,0:T(8,128)(2,1)S(1)}, u32[]{:S(2)}, u32[]{:S(2)}) collective-permute-start(bf16[12,32,128]{2,1,0:T(8,128)(2,1)S(1)} %get-tuple-element.28), channel_id=1, source_target_pairs={{0,1},{1,0},{2,3},{3,2},{4,5},{5,4},{6,7},{7,6},{8,9},{9,8},{10,11... | collective-permute-start | bytes 294920 | tf_op jit(solution)/shard_map/ppermute | solution.py:424
  38.3 0.4 shard_map.35.patch_ref
  38.7 0.5 %shard_map.36.pooled_ref = f32[4,3,32,128]{3,2,1,0:T(8,128)S(1)} custom-call(bf16[8,3,32,128]{3,2,1,0:T(8,128)(2,1)S(1)} %get-tuple-element.23.tall_ref, bf16[28,32,128]{2,1,0:T(8,128)(2,1)S(1)} %collective-permute-done.2.near_ref, bf16[28,32,128]{2,1,0:T(8,128)(2,1)S(1)} %collective-permute-done.3.far_ref), custom_call_target="tpu_custom_call" | custom-call | tf_op jit(solution)/shard_map/pallas_call | solution.py:227
  39.2 0.0 collective-permute-done.4.last_ref
  39.3 4.1 %shard_map.37 = f32[4,3,1200,128]{3,2,1,0:T(8,128)} custom-call(f32[24,32,128]{2,1,0:T(8,128)S(1)} %get-tuple-element.27.sum_ref, bf16[12,32,128]{2,1,0:T(8,128)(2,1)S(1)} %collective-permute-done.4.last_ref, bf16[24,32,128]{2,1,0:T(8,128)(2,1)S(1)} %get-tuple-element.29.window_ref, bf16[3,1,1200,128]{3,2,1,0:T(8,128)(2,1)S(1)} %shard_map.35.patch_ref, ...), custom_call_target="tpu_custom_call" | custom-call | tf_op jit(solution)/shard_map/pallas_call | solution.py:400
Async XLA Ops:
  0.0 0.8 %copy-start.1 = (bf16[1,3,64,96]{3,2,1,0:T(8,128)(2,1)S(1)}, bf16[1,3,64,96]{3,2,1,0:T(8,128)(2,1)}, u32[]{:S(2)}) copy-start(bf16[1,3,64,96]{3,2,1,0:T(8,128)(2,1)} %images_ref.1) | copy-start | bytes 110596
  2.2 16.2 %all-to-all-start = ((bf16[32,24,128]{2,1,0:T(8,128)(2,1)}), bf16[32,24,128]{2,1,0:T(8,128)(2,1)S(1)}, u32[]{:S(2)}, u32[]{:S(2)}) async-start(bf16[32,24,128]{2,1,0:T(8,128)(2,1)} %bitcast), calls=%async_computation | async-start | bytes 393216 | tf_op jit(solution)/shard_map/all_to_all | solution.py:445
  9.5 2.0 %copy-start = (bf16[4,3,128,1200]{2,3,1,0:T(8,128)(2,1)S(1)}, bf16[4,3,128,1200]{2,3,1,0:T(8,128)(2,1)}, u32[]{:S(2)}) copy-start(bf16[4,3,128,1200]{2,3,1,0:T(8,128)(2,1)} %param.3) | copy-start | bytes 11059204
  22.3 6.4 %collective-permute-start = (bf16[18,32,128]{2,1,0:T(8,128)(2,1)S(1)}, bf16[18,32,128]{2,1,0:T(8,128)(2,1)S(1)}, u32[]{:S(2)}, u32[]{:S(2)}) collective-permute-start(bf16[18,32,128]{2,1,0:T(8,128)(2,1)S(1)} %get-tuple-element.20), channel_id=1, source_target_pairs={{0,8},{1,9},{2,10},{3,11},{4,12},{5,13},{6,14},{7,15},{8,0},{9,1},... | collective-permute-start | bytes 442376 | tf_op jit(solution)/shard_map/ppermute | solution.py:424
  23.4 5.3 %collective-permute-start.1 = (bf16[18,32,128]{2,1,0:T(8,128)(2,1)S(1)}, bf16[18,32,128]{2,1,0:T(8,128)(2,1)S(1)}, u32[]{:S(2)}, u32[]{:S(2)}) collective-permute-start(bf16[18,32,128]{2,1,0:T(8,128)(2,1)S(1)} %get-tuple-element.21), channel_id=1, source_target_pairs={{0,1},{1,0},{2,3},{3,2},{4,5},{5,4},{6,7},{7,6},{8,16},{9,17},{10,... | collective-permute-start | bytes 442376 | tf_op jit(solution)/shard_map/ppermute | solution.py:424
  29.0 1.6 %collective-permute-start.2 = (bf16[28,32,128]{2,1,0:T(8,128)(2,1)S(1)}, bf16[28,32,128]{2,1,0:T(8,128)(2,1)S(1)}, u32[]{:S(2)}, u32[]{:S(2)}) collective-permute-start(bf16[28,32,128]{2,1,0:T(8,128)(2,1)S(1)} %get-tuple-element.24), channel_id=1, source_target_pairs={{0,1},{1,0},{2,3},{3,2},{4,5},{5,4},{6,7},{7,6},{8,9},{9,8},{10,11... | collective-permute-start | bytes 688136 | tf_op jit(solution)/shard_map/ppermute | solution.py:424
  30.8 6.1 %collective-permute-start.3 = (bf16[28,32,128]{2,1,0:T(8,128)(2,1)S(1)}, bf16[28,32,128]{2,1,0:T(8,128)(2,1)S(1)}, u32[]{:S(2)}, u32[]{:S(2)}) collective-permute-start(bf16[28,32,128]{2,1,0:T(8,128)(2,1)S(1)} %get-tuple-element.26), channel_id=1, source_target_pairs={{0,8},{1,2},{2,1},{3,4},{4,3},{5,6},{6,5},{7,15},{8,0},{9,10},{10,... | collective-permute-start | bytes 688136 | tf_op jit(solution)/shard_map/ppermute | solution.py:424
  37.1 2.2 %collective-permute-start.4 = (bf16[12,32,128]{2,1,0:T(8,128)(2,1)S(1)}, bf16[12,32,128]{2,1,0:T(8,128)(2,1)S(1)}, u32[]{:S(2)}, u32[]{:S(2)}) collective-permute-start(bf16[12,32,128]{2,1,0:T(8,128)(2,1)S(1)} %get-tuple-element.28), channel_id=1, source_target_pairs={{0,1},{1,0},{2,3},{3,2},{4,5},{5,4},{6,7},{7,6},{8,9},{9,8},{10,11... | collective-permute-start | bytes 294920 | tf_op jit(solution)/shard_map/ppermute | solution.py:424

commit v2 on v1

--- a/solution.py
+++ b/solution.py
@@ -50,7 +50,9 @@
         assert self.height == self.R * self.h and self.width == self.C * self.w
 
 
-def split_kernel(z, images_ref, out_ref, rows_ref, pad_ref):
+def split_kernel(z, images_hbm, out_hbm, images_ref, rows_ref, pad_ref, pick_ref, out_ref, in_sem, out_sems):
+    load = pltpu.make_async_copy(images_hbm, images_ref, in_sem)
+    load.start()
     margin = PAD // S
     blocks = z.height // S
     n = lax.broadcasted_iota(jnp.int32, (1, z.C * z.lanes), 1)
@@ -61,7 +63,13 @@
     source = jnp.where(across < z.ext, z.w * column - PAD + across, -1)
     pixel = lax.broadcasted_iota(jnp.int32, (128, z.C * z.lanes), 0)
     chunks = rows_ref.shape[1]
+    for k in range(chunks):
+        for j in range(S):
+            wanted = jnp.where(lane_row == j, source - 128 * k, -1)
+            pick_ref[k, j] = (pixel == wanted).astype(f32).astype(bf16)
     rows_ref[...] = jnp.zeros_like(rows_ref)
+    pad_ref[...] = jnp.zeros_like(pad_ref)
+    load.wait()
     for i in range(z.bd):
         pixels = images_ref[i].astype(f32)
         count = CH * z.height * z.width
@@ -78,9 +86,7 @@
                 line = jnp.concatenate(
                     [rows_ref[c, k, pl.ds(j, blocks, stride=S), :] for c in range(CH)], axis=0
                 ).astype(bf16)
-                wanted = jnp.where(lane_row == j, source - 128 * k, -1)
-                total = total + dot(line, (pixel == wanted).astype(f32).astype(bf16))
-        pad_ref[...] = jnp.zeros_like(pad_ref)
+                total = total + dot(line, pick_ref[k, j])
         for c in range(CH):
             pad_ref[c, margin : margin + blocks, :] = total[c * blocks : (c + 1) * blocks]
         for r in range(z.R):
@@ -90,20 +96,32 @@
                     for c in range(CH)
                 ]
                 out_ref[r * z.C + q, i] = jnp.concatenate(block, axis=0).astype(bf16)
+            if i == z.bd - 1:
+                part = pl.ds(r * z.C, z.C)
+                pltpu.make_async_copy(out_ref.at[part], out_hbm.at[part], out_sems.at[r]).start()
+    for r in range(z.R):
+        part = pl.ds(r * z.C, z.C)
+        pltpu.make_async_copy(out_ref.at[part], out_hbm.at[part], out_sems.at[r]).wait()
 
 
 def split(z, images):
+    shape = (z.R * z.C, z.bd, z.T, z.lanes)
     return pl.pallas_call(
         functools.partial(split_kernel, z),
-        out_shape=pltpu.VMEM((z.R * z.C, z.bd, z.T, z.lanes), bf16),
-        in_specs=[pl.BlockSpec(memory_space=pltpu.VMEM)],
-        out_specs=pl.BlockSpec(memory_space=pltpu.VMEM),
+        out_shape=pltpu.HBM(shape, bf16),
+        in_specs=[pl.BlockSpec(memory_space=pltpu.HBM)],
+        out_specs=pl.BlockSpec(memory_space=pltpu.HBM),
         scratch_shapes=[
+            pltpu.VMEM((z.bd, CH, z.height, z.width), bf16),
             pltpu.VMEM((CH, -(-z.width // 128), z.height, 128), f32),
             pltpu.VMEM((CH, z.height // S + 2 * PAD // S, z.C * z.lanes), f32),
+            pltpu.VMEM((-(-z.width // 128), S, 128, z.C * z.lanes), bf16),
+            pltpu.VMEM(shape, bf16),
+            pltpu.SemaphoreType.DMA,
+            pltpu.SemaphoreType.DMA((z.R,)),
         ],
         compiler_params=pltpu.CompilerParams(vmem_limit_bytes=32 * MIB),
-    )(images)
+    )(pltpu.with_memory_space_constraint(images, pltpu.HBM))
 
 
 def spread_kernel(z, weights_ref, out_ref, rows_ref):
@@ -146,20 +164,23 @@
     for t in range(z.T):
         window_ref[t] = rows_ref[pl.ds(t, B, stride=z.T), :].astype(bf16)
     contrib_ref[...] = jnp.zeros_like(contrib_ref)
-    for p in range(z.rd):
-        if p >= HELD:
-            copies[p - HELD].wait()
-            if p - HELD + 2 < len(copies):
-                copies[p - HELD + 2].start()
-        weight = first_ref.at[p] if p < HELD else wide_ref.at[p - HELD]
-        hidden = dot(field(z, p, window_ref), weight[...]).astype(bf16)
-        for q in range(z.cd):
-            hidden_ref[p, q] = hidden[:, q * z.F : (q + 1) * z.F]
-        terms = dot(hidden, weight[...], NT)
-        for c in range(CH):
-            for g in range(GROUP):
-                at = (c * GROUP + g) * z.lanes
-                contrib_ref[c * z.YB + p + g] += terms[:, at : at + z.lanes]
+    for first in range(0, z.rd, HELD):
+        rows = range(first, min(first + HELD, z.rd))
+        for p in rows:
+            if p >= HELD:
+                copies[p - HELD].wait()
+                if p - HELD + 2 < len(copies):
+                    copies[p - HELD + 2].start()
+        weight = [first_ref.at[p] if p < HELD else wide_ref.at[p - HELD] for p in rows]
+        hidden = [dot(field(z, p, window_ref), w[...]).astype(bf16) for p, w in zip(rows, weight)]
+        terms = [dot(h, w[...], NT) for h, w in zip(hidden, weight)]
+        for p, h, value in zip(rows, hidden, terms):
+            for q in range(z.cd):
+                hidden_ref[p, q] = h[:, q * z.F : (q + 1) * z.F]
+            for c in range(CH):
+                for g in range(GROUP):
+                    at = (c * GROUP + g) * z.lanes
+                    contrib_ref[c * z.YB + p + g] += value[:, at : at + z.lanes]
     half = z.YB // 2
     even = row_is_even()
     for ref, below in ((swap_ref, even), (cross_ref, jnp.logical_not(even))):
@@ -208,18 +229,20 @@
                 flat_ref[group, at : at + z.lanes, :] = stack.astype(f32).T
 
 
-def place_fields(z, q, flat_ref, dense_ref, out_ref):
+def place_fields(z, q, c, flat_ref, dense_ref, out_ref):
+    rows = slice(c * FIELD * FIELD, (c + 1) * FIELD * FIELD)
     for group in range(z.groups):
-        for i in range(CH * FIELD):
+        for i in range(c * FIELD, (c + 1) * FIELD):
             at = z.stride * i + S * q
             dense_ref[FIELD * i : FIELD * (i + 1), :] = flat_ref[group, at : at + FIELD, :]
-        out_ref[q, group] = dense_ref[...].astype(bf16)
+        out_ref[q, group, rows, :] = dense_ref[rows, :].astype(bf16)
 
 
 def patches_kernel(z, window_ref, out_ref, flat_ref, dense_ref):
     turn_fields(z, lambda t: window_ref[t], flat_ref)
     for q in range(z.cd):
-        place_fields(z, q, flat_ref, dense_ref, out_ref)
+        for c in range(CH):
+            place_fields(z, q, c, flat_ref, dense_ref, out_ref)
 
 
 def vmem_call(kernel, shapes, scratch, *args):
@@ -263,29 +286,35 @@
 def rows_kernel(z, contrib_ref, hidden_ref, swap_ref, cross_ref, sum_ref, tall_ref, send_ref):
     half = z.YB // 2
     sum_ref[...] = contrib_ref[...]
-    for i in range(z.rd):
-        for q in range(z.cd):
-            tall_ref[2 + i, q] = hidden_ref[i, q]
     row = lax.axis_index("row")
     even_row = row_is_even()
+    above_exists, below_exists = row > 0, row < z.R - 1
     for ref, below in ((swap_ref, even_row), (cross_ref, jnp.logical_not(even_row))):
-        exists = jnp.where(below, row < z.R - 1, row > 0)
+        exists = jnp.where(below, below_exists, above_exists)
         first = jnp.where(below, z.YB - half, 0)
-        at = jnp.where(below, z.rd + 2, 0)
         for c in range(CH):
             for y in range(half):
                 sum_ref[c * z.YB + first + y] += jnp.where(exists, ref[c * half + y].astype(f32), 0.0)
-        for i in range(2):
-            for q in range(z.cd):
-                value = ref[CH * half + i * z.cd + q]
-                tall_ref[at + i, q] = jnp.where(exists, value, jnp.zeros_like(value))
     even = is_even()
     for t in range(0, z.T, 2):
         send_ref[t // 2] = pack_side(z, even, sum_ref[t], sum_ref[t + 1]).astype(bf16)
+    for q in range(z.cd):
+        squares = [jnp.square(hidden_ref[i, q].astype(f32)) for i in range(z.rd)]
+        above, below = [], []
+        for i in range(2):
+            swapped = swap_ref[CH * half + i * z.cd + q].astype(f32)
+            crossed = cross_ref[CH * half + i * z.cd + q].astype(f32)
+            upper = jnp.where(above_exists, jnp.where(even_row, crossed, swapped), 0.0)
+            lower = jnp.where(below_exists, jnp.where(even_row, swapped, crossed), 0.0)
+            above.append(jnp.square(upper))
+            below.append(jnp.square(lower))
+        squares = above + squares + below
+        for i in range(z.rd + 2):
+            tall_ref[i, q] = squares[i] + squares[i + 1] + squares[i + 2]
     first = jnp.where(even, z.cd - 2, 0)
-    for i in range(z.rd + 4):
+    for i in range(z.rd + 2):
         for k in range(2):
-            send_ref[z.T // 2 + 2 * i + k] = tall_ref[i, first + k]
+            send_ref[z.T // 2 + 2 * i + k] = tall_ref[i, first + k].astype(bf16)
 
 
 def near_kernel(z, sum_ref, tall_ref, near_ref, out_ref, send_ref):
@@ -297,9 +326,9 @@
             out_ref[t + k] = total[k]
         send_ref[t // 2] = pack_side(z, jnp.logical_not(even), *total).astype(bf16)
     first = jnp.where(even, 0, z.cd - 2)
-    for i in range(z.rd + 4):
+    for i in range(z.rd + 2):
         for k in range(2):
-            send_ref[z.T // 2 + 2 * i + k] = tall_ref[i, first + k]
+            send_ref[z.T // 2 + 2 * i + k] = tall_ref[i, first + k].astype(bf16)
 
 
 def far_kernel(z, sum_ref, far_ref, out_ref, send_ref):
@@ -312,25 +341,20 @@
         send_ref[t // 2] = pack_side(z, even, *came).astype(bf16)
 
 
-def pool_kernel(z, tall_ref, near_ref, far_ref, out_ref, wide_ref, inverse_ref):
+def pool_kernel(z, hidden_ref, tall_ref, near_ref, far_ref, out_ref, wide_ref, inverse_ref):
     even = is_even()
     row0 = lax.axis_index("row") * z.rd - 1
     col0 = lax.axis_index("col") * z.cd - 1
     near_at = jnp.where(even, z.cd + 2, 0)
     far_at = jnp.where(even, 0, z.cd + 2)
     exists = jnp.where(even, lax.axis_index("col") > 0, lax.axis_index("col") < z.C - 1)
-    for i in range(z.rd + 4):
+    for i in range(z.rd + 2):
         for k in range(2):
-            wide_ref[i, near_at + k] = near_ref[z.T // 2 + 2 * i + k]
-            far = far_ref[z.T // 2 + 2 * i + k]
-            wide_ref[i, far_at + k] = jnp.where(exists, far, jnp.zeros_like(far))
+            wide_ref[near_at + k] = near_ref[z.T // 2 + 2 * i + k].astype(f32)
+            wide_ref[far_at + k] = jnp.where(exists, far_ref[z.T // 2 + 2 * i + k].astype(f32), 0.0)
         for q in range(z.cd):
-            wide_ref[i, 2 + q] = tall_ref[i, q]
-    for i in range(z.rd + 2):
-        columns = []
-        for q in range(z.cd + 4):
-            parts = [jnp.square(wide_ref[i + d, q].astype(f32)) for d in range(3)]
-            columns.append(parts[0] + parts[1] + parts[2])
+            wide_ref[2 + q] = tall_ref[i, q]
+        columns = [wide_ref[q] for q in range(z.cd + 4)]
         for q in range(z.cd + 2):
             energy = jnp.sqrt(1.0 + (columns[q] + columns[q + 1] + columns[q + 2]))
             inverse = (1.0 / energy).astype(bf16).astype(f32)
@@ -343,10 +367,7 @@
             columns.append(inverse_ref[i, q] + inverse_ref[i + 1, q] + inverse_ref[i + 2, q])
         for q in range(z.cd):
             spread = columns[q] + columns[q + 1] + columns[q + 2]
-            out_ref[i, q] = sparsity * tall_ref[2 + i, q].astype(f32) * spread
-
-
-CHUNKS = 3
+            out_ref[i, q] = sparsity * hidden_ref[i, q].astype(f32) * spread
 
 
 def grad_kernel(
@@ -369,7 +390,6 @@
 
     turn_fields(z, lambda t: resid_ref[t], flat_ref)
     factor_ref[...] = jnp.zeros_like(factor_ref)
-    size = K // CHUNKS
     copies = []
     for q in range(z.cd):
         for p in range(z.rd):
@@ -380,9 +400,9 @@
             at = inner * B
             factor_ref[q, group, at : at + B, columns] = (pooled_ref[p, q] + back).astype(bf16)
             factor_ref[q, group, 128 + at : 128 + at + B, columns] = hidden_ref[p, q]
-        place_fields(z, q, flat_ref, dense_ref, resid_patch_ref)
-        for k in range(CHUNKS):
-            rows = slice(k * size, (k + 1) * size)
+        for k in range(CH):
+            place_fields(z, q, k, flat_ref, dense_ref, resid_patch_ref)
+            rows = slice(k * FIELD * FIELD, (k + 1) * FIELD * FIELD)
             for group in range(z.groups):
                 both = jnp.concatenate([patch_ref[q, group, rows, :], resid_patch_ref[q, group, rows, :]], axis=1)
                 value = dot(both, factor_ref[q, group]) * (1.0 / B)
@@ -409,7 +429,7 @@
             pltpu.VMEM((z.cd, z.groups, K, 128), bf16),
             pltpu.VMEM((z.cd, z.groups, 256, z.per * F), bf16),
             pltpu.VMEM((z.rd, z.cd, K, F), f32),
-            pltpu.SemaphoreType.DMA((z.cd, CHUNKS)),
+            pltpu.SemaphoreType.DMA((z.cd, CH)),
         ],
         compiler_params=pltpu.CompilerParams(vmem_limit_bytes=40 * MIB),
     )(*args)
@@ -451,14 +471,20 @@
     window, hidden, contrib, to_swap, to_cross, wide = encode(z, moved, wide_first, wide)
     crossed = exchange(z, to_cross, cross_row)
     swapped = exchange(z, to_swap, lambda z, r, c: (r ^ 1, c))
-    tall = ((z.rd + 4, z.cd, B, z.F), bf16)
-    sent = ((z.T // 2 + 2 * (z.rd + 4), B, L), bf16)
+    tall = ((z.rd + 2, z.cd, B, z.F), f32)
+    sent = ((z.T // 2 + 2 * (z.rd + 2), B, L), bf16)
     total, tall, send = vmem_call(
         functools.partial(rows_kernel, z), [tiles, tall, sent], [], contrib, hidden, swapped, crossed
     )
     near = exchange(z, send, swap_col)
     total, send = vmem_call(functools.partial(near_kernel, z), [tiles, sent], [], total, tall, near)
-    far = exchange(z, send, cross_col)
+    (patch,) = vmem_call(
+        functools.partial(patches_kernel, z),
+        [((z.cd, z.groups, K, 128), bf16)],
+        [((z.groups, z.KW, 128), f32), ((K, 128), f32)],
+        window,
+    )
+    far, patch = lax.optimization_barrier((exchange(z, send, cross_col), patch))
     total, send = vmem_call(
         functools.partial(far_kernel, z), [tiles, ((z.T // 2, B, L), bf16)], [], total, far
     )
@@ -466,14 +492,8 @@
     (pooled,) = vmem_call(
         functools.partial(pool_kernel, z),
         [((z.rd, z.cd, B, z.F), f32)],
-        [((z.rd + 4, z.cd + 4, B, z.F), bf16), ((z.rd + 2, z.cd + 2, B, z.F), f32)],
-        tall, near, far,
-    )
-    (patch,) = vmem_call(
-        functools.partial(patches_kernel, z),
-        [((z.cd, z.groups, K, 128), bf16)],
-        [((z.groups, z.KW, 128), f32), ((K, 128), f32)],
-        window,
+        [((z.cd + 4, B, z.F), f32), ((z.rd + 2, z.cd + 2, B, z.F), f32)],
+        hidden, tall, near, far,
     )
     return jnp.swapaxes(gradient(z, total, last, window, patch, hidden, pooled, wide_first, wide), 2, 3)
 

time: 43.6 us -> 42.2 us (0.968)
  local copies, waits for them, and re-layouts: 2.84 us -> 2.04 us
    unnamed x4 -> x2, local copies, waits for them, and re-layouts: 2.84 us -> 2.04 us
    pallas_call x1, Pallas kernels: 1.39 us -> 2.16 us  [split(): pl.pallas_call(functools.partial(split_kernel, z), out_shape=pltpu.HBM(sh...]
    pallas_call x1, Pallas kernels: 3.94 us -> 3.3 us  [encode(): pl.pallas_call(functools.partial(encode_kernel, z), out_shape=[pltpu.VMEM...]
  transfers between devices with their start and end apart: 6 -> 6, of which waited for: 4 -> 5; matrix products, arithmetic and copies ran while one was open for 0% -> 0% of each run, Pallas kernels for 8% -> 8%
where the time goes in v2:
time: 42.2 us; the launch traced here: 42 us
  waiting for transfers between devices  15.1 us (36%)
  Pallas kernels  13.6 us (32%)
  starting transfers between devices  11.1 us (26%)
  local copies, waits for them, and re-layouts  2.04 us (5%)
    ppermute x5, waiting for transfers between devices, exchange(): return lax.ppermute(value, ('row', 'col'), pairs)  10.9 us
    all_to_all x1, starting transfers between devices, body(): lax.all_to_all(blocks.reshape(z.R * z.C, z.bd * z.T, L), ('row', 'col'),...  7.3 us
    all_to_all x1, waiting for transfers between devices, body(): lax.all_to_all(blocks.reshape(z.R * z.C, z.bd * z.T, L), ('row', 'col'),...  4.25 us
    pallas_call x1, Pallas kernels, gradient(): pl.pallas_call(functools.partial(grad_kernel, z), out_shape=pltpu.HBM((z....  4.08 us
    ppermute x5, starting transfers between devices, exchange(): return lax.ppermute(value, ('row', 'col'), pairs)  3.83 us
    pallas_call x1, Pallas kernels, encode(): pl.pallas_call(functools.partial(encode_kernel, z), out_shape=[pltpu.VMEM...  3.3 us
    pallas_call x2, Pallas kernels, spread_weights(): pl.pallas_call(functools.partial(spread_kernel, z), grid=(count,), out_sh...  2.58 us
    pallas_call x1, Pallas kernels, split(): pl.pallas_call(functools.partial(split_kernel, z), out_shape=pltpu.HBM(sh...  2.16 us
  transfers between devices with their start and end apart: 6, of which 5 were waited for; matrix products, arithmetic and copies ran while one was open for 0% of the time, Pallas kernels for 8%

profile of v2, /device:TPU:0, one launch (start us, length us, event | category | flops | bytes accessed | tf_op | source)
XLA Modules:
  0.0 42.0 jit_solution(4733691336691855130)
XLA Ops:
  0.0 2.2 %shard_map.28 = bf16[32,1,24,128]{3,2,1,0:T(8,128)(2,1)} custom-call(bf16[1,3,64,96]{3,2,1,0:T(8,128)(2,1)} %images_hbm.1), custom_call_target="tpu_custom_call" | custom-call | tf_op jit(solution)/shard_map/pallas_call | solution.py:109
  2.2 7.3 %all-to-all-start = ((bf16[32,24,128]{2,1,0:T(8,128)(2,1)}), bf16[32,24,128]{2,1,0:T(8,128)(2,1)S(1)}, u32[]{:S(2)}, u32[]{:S(2)}) async-start(bf16[32,24,128]{2,1,0:T(8,128)(2,1)} %bitcast.5), calls=%async_computation | async-start | bytes 393216 | tf_op jit(solution)/shard_map/all_to_all | solution.py:465
  9.5 0.0 copy-start
  9.5 2.0 %copy-done = bf16[4,3,128,1200]{2,3,1,0:T(8,128)(2,1)S(1)} copy-done((bf16[4,3,128,1200]{2,3,1,0:T(8,128)(2,1)S(1)}, bf16[4,3,128,1200]{2,3,1,0:T(8,128)(2,1)}, u32[]{:S(2)}) %copy-start) | copy-done | bytes 3686424
  11.5 0.6 %shard_map.29.first_ref = bf16[2,1920,384]{2,1,0:T(8,128)(2,1)S(1)} custom-call(bf16[4,3,1200,128]{3,2,1,0:T(8,128)(2,1)S(1)} %bitcast.3), custom_call_target="tpu_custom_call" | custom-call | tf_op jit(solution)/shard_map/pallas_call | solution.py:139
  12.2 1.9 %shard_map.30.wide_hbm = bf16[2,1920,384]{2,1,0:T(8,128)(2,1)} custom-call(bf16[4,3,1200,128]{3,2,1,0:T(8,128)(2,1)S(1)} %bitcast.4), custom_call_target="tpu_custom_call" | custom-call | tf_op jit(solution)/shard_map/pallas_call | solution.py:139
  14.1 4.2 %all-to-all-done.moved_ref = bf16[32,24,128]{2,1,0:T(8,128)(2,1)S(1)} async-done(((bf16[32,24,128]{2,1,0:T(8,128)(2,1)}), bf16[32,24,128]{2,1,0:T(8,128)(2,1)S(1)}, u32[]{:S(2)}, u32[]{:S(2)}) %all-to-all-start) | async-done | bytes 196640 | tf_op jit(solution)/shard_map/all_to_all | solution.py:465
  18.4 3.3 %shard_map.31 = (bf16[24,32,128]{2,1,0:T(8,128)(2,1)S(1)}, bf16[4,3,32,128]{3,2,1,0:T(8,128)(2,1)S(1)}, f32[24,32,128]{2,1,0:T(8,128)S(1)}, bf16[18,32,128]{2,1,...) custom-call(bf16[32,24,128]{2,1,0:T(8,128)(2,1)S(1)} %all-to-all-done.moved_ref, ...), custom_call_target="tpu_custom_call" | custom-call | tf_op jit(solution)/shard_map/pallas_call | solution.py:209
  21.7 1.1 %collective-permute-start = (bf16[18,32,128]{2,1,0:T(8,128)(2,1)S(1)}, bf16[18,32,128]{2,1,0:T(8,128)(2,1)S(1)}, u32[]{:S(2)}, u32[]{:S(2)}) collective-permute-start(bf16[18,32,128]{2,1,0:T(8,128)(2,1)S(1)} %get-tuple-element.22), channel_id=1, source_target_pairs={{0,8},{1,9},{2,10},{3,11},{4,12},{5,13},{6,14},{7,15},{8,0},{9,1},... | collective-permute-start | bytes 442376 | tf_op jit(solution)/shard_map/ppermute | solution.py:444
  22.8 0.0 collective-permute-start.1
  22.8 5.3 %collective-permute-done.swap_ref = bf16[18,32,128]{2,1,0:T(8,128)(2,1)S(1)} collective-permute-done((bf16[18,32,128]{2,1,0:T(8,128)(2,1)S(1)}, bf16[18,32,128]{2,1,0:T(8,128)(2,1)S(1)}, u32[]{:S(2)}, u32[]{:S(2)}) %collective-permute-start) | collective-permute-done | bytes 147488 | tf_op jit(solution)/shard_map/ppermute | solution.py:444
  28.1 0.0 collective-permute-done.1.cross_ref
  28.1 0.3 shard_map.32
  28.4 0.1 collective-permute-start.2
  28.5 1.4 %collective-permute-done.2.near_ref = bf16[24,32,128]{2,1,0:T(8,128)(2,1)S(1)} collective-permute-done((bf16[24,32,128]{2,1,0:T(8,128)(2,1)S(1)}, bf16[24,32,128]{2,1,0:T(8,128)(2,1)S(1)}, u32[]{:S(2)}, u32[]{:S(2)}) %collective-permute-start.2) | collective-permute-done | bytes 196640 | tf_op jit(solution)/shard_map/ppermute | solution.py:444
  29.9 0.2 shard_map.33
  30.1 1.8 %collective-permute-start.3 = (bf16[24,32,128]{2,1,0:T(8,128)(2,1)S(1)}, bf16[24,32,128]{2,1,0:T(8,128)(2,1)S(1)}, u32[]{:S(2)}, u32[]{:S(2)}) collective-permute-start(bf16[24,32,128]{2,1,0:T(8,128)(2,1)S(1)} %get-tuple-element.28), channel_id=1, source_target_pairs={{0,8},{1,2},{2,1},{3,4},{4,3},{5,6},{6,5},{7,15},{8,0},{9,10},{10,... | collective-permute-start | bytes 589832 | tf_op jit(solution)/shard_map/ppermute | solution.py:444
  31.9 0.4 shard_map.34.patch_ref
  32.3 3.5 %collective-permute-done.3.far_ref = bf16[24,32,128]{2,1,0:T(8,128)(2,1)S(1)} collective-permute-done((bf16[24,32,128]{2,1,0:T(8,128)(2,1)S(1)}, bf16[24,32,128]{2,1,0:T(8,128)(2,1)S(1)}, u32[]{:S(2)}, u32[]{:S(2)}) %collective-permute-start.3) | collective-permute-done | bytes 196640 | tf_op jit(solution)/shard_map/ppermute | solution.py:444
  35.8 0.2 shard_map.35
  36.1 0.9 %collective-permute-start.4 = (bf16[12,32,128]{2,1,0:T(8,128)(2,1)S(1)}, bf16[12,32,128]{2,1,0:T(8,128)(2,1)S(1)}, u32[]{:S(2)}, u32[]{:S(2)}) collective-permute-start(bf16[12,32,128]{2,1,0:T(8,128)(2,1)S(1)} %get-tuple-element.32), channel_id=1, source_target_pairs={{0,1},{1,0},{2,3},{3,2},{4,5},{5,4},{6,7},{7,6},{8,9},{9,8},{10,11... | collective-permute-start | bytes 294920 | tf_op jit(solution)/shard_map/ppermute | solution.py:444
  36.9 0.4 shard_map.36.pooled_ref
  37.3 0.6 %collective-permute-done.4.last_ref = bf16[12,32,128]{2,1,0:T(8,128)(2,1)S(1)} collective-permute-done((bf16[12,32,128]{2,1,0:T(8,128)(2,1)S(1)}, bf16[12,32,128]{2,1,0:T(8,128)(2,1)S(1)}, u32[]{:S(2)}, u32[]{:S(2)}) %collective-permute-start.4) | collective-permute-done | bytes 98336 | tf_op jit(solution)/shard_map/ppermute | solution.py:444
  37.9 4.1 %shard_map.37 = f32[4,3,1200,128]{3,2,1,0:T(8,128)} custom-call(f32[24,32,128]{2,1,0:T(8,128)S(1)} %get-tuple-element.31.sum_ref, bf16[12,32,128]{2,1,0:T(8,128)(2,1)S(1)} %collective-permute-done.4.last_ref, bf16[24,32,128]{2,1,0:T(8,128)(2,1)S(1)} %get-tuple-element.29.window_ref, bf16[3,1,1200,128]{3,2,1,0:T(8,128)(2,1)S(1)} %shard_map.34.patch_ref, ...), custom_call_target="tpu_custom_call" | custom-call | tf_op jit(solution)/shard_map/pallas_call | solution.py:420
Async XLA Ops:
  2.2 16.2 %all-to-all-start = ((bf16[32,24,128]{2,1,0:T(8,128)(2,1)}), bf16[32,24,128]{2,1,0:T(8,128)(2,1)S(1)}, u32[]{:S(2)}, u32[]{:S(2)}) async-start(bf16[32,24,128]{2,1,0:T(8,128)(2,1)} %bitcast.5), calls=%async_computation | async-start | bytes 393216 | tf_op jit(solution)/shard_map/all_to_all | solution.py:465
  9.5 2.0 %copy-start = (bf16[4,3,128,1200]{2,3,1,0:T(8,128)(2,1)S(1)}, bf16[4,3,128,1200]{2,3,1,0:T(8,128)(2,1)}, u32[]{:S(2)}) copy-start(bf16[4,3,128,1200]{2,3,1,0:T(8,128)(2,1)} %param.3) | copy-start | bytes 11059204
  21.7 6.4 %collective-permute-start = (bf16[18,32,128]{2,1,0:T(8,128)(2,1)S(1)}, bf16[18,32,128]{2,1,0:T(8,128)(2,1)S(1)}, u32[]{:S(2)}, u32[]{:S(2)}) collective-permute-start(bf16[18,32,128]{2,1,0:T(8,128)(2,1)S(1)} %get-tuple-element.22), channel_id=1, source_target_pairs={{0,8},{1,9},{2,10},{3,11},{4,12},{5,13},{6,14},{7,15},{8,0},{9,1},... | collective-permute-start | bytes 442376 | tf_op jit(solution)/shard_map/ppermute | solution.py:444
  22.8 5.3 %collective-permute-start.1 = (bf16[18,32,128]{2,1,0:T(8,128)(2,1)S(1)}, bf16[18,32,128]{2,1,0:T(8,128)(2,1)S(1)}, u32[]{:S(2)}, u32[]{:S(2)}) collective-permute-start(bf16[18,32,128]{2,1,0:T(8,128)(2,1)S(1)} %get-tuple-element.23), channel_id=1, source_target_pairs={{0,1},{1,0},{2,3},{3,2},{4,5},{5,4},{6,7},{7,6},{8,16},{9,17},{10,... | collective-permute-start | bytes 442376 | tf_op jit(solution)/shard_map/ppermute | solution.py:444
  28.4 1.5 %collective-permute-start.2 = (bf16[24,32,128]{2,1,0:T(8,128)(2,1)S(1)}, bf16[24,32,128]{2,1,0:T(8,128)(2,1)S(1)}, u32[]{:S(2)}, u32[]{:S(2)}) collective-permute-start(bf16[24,32,128]{2,1,0:T(8,128)(2,1)S(1)} %get-tuple-element.26), channel_id=1, source_target_pairs={{0,1},{1,0},{2,3},{3,2},{4,5},{5,4},{6,7},{7,6},{8,9},{9,8},{10,11... | collective-permute-start | bytes 589832 | tf_op jit(solution)/shard_map/ppermute | solution.py:444
  30.1 5.7 %collective-permute-start.3 = (bf16[24,32,128]{2,1,0:T(8,128)(2,1)S(1)}, bf16[24,32,128]{2,1,0:T(8,128)(2,1)S(1)}, u32[]{:S(2)}, u32[]{:S(2)}) collective-permute-start(bf16[24,32,128]{2,1,0:T(8,128)(2,1)S(1)} %get-tuple-element.28), channel_id=1, source_target_pairs={{0,8},{1,2},{2,1},{3,4},{4,3},{5,6},{6,5},{7,15},{8,0},{9,10},{10,... | collective-permute-start | bytes 589832 | tf_op jit(solution)/shard_map/ppermute | solution.py:444
  36.1 1.8 %collective-permute-start.4 = (bf16[12,32,128]{2,1,0:T(8,128)(2,1)S(1)}, bf16[12,32,128]{2,1,0:T(8,128)(2,1)S(1)}, u32[]{:S(2)}, u32[]{:S(2)}) collective-permute-start(bf16[12,32,128]{2,1,0:T(8,128)(2,1)S(1)} %get-tuple-element.32), channel_id=1, source_target_pairs={{0,1},{1,0},{2,3},{3,2},{4,5},{5,4},{6,7},{7,6},{8,9},{9,8},{10,11... | collective-permute-start | bytes 294920 | tf_op jit(solution)/shard_map/ppermute | solution.py:444

commit v3 on v2

--- a/solution.py
+++ b/solution.py
@@ -69,17 +69,13 @@
             pick_ref[k, j] = (pixel == wanted).astype(f32).astype(bf16)
     rows_ref[...] = jnp.zeros_like(rows_ref)
     pad_ref[...] = jnp.zeros_like(pad_ref)
+    inside = (source >= 0) & (source < z.width)
     load.wait()
     for i in range(z.bd):
         pixels = images_ref[i].astype(f32)
-        count = CH * z.height * z.width
-        center = jnp.sum(pixels) / count
-        moved = pixels - center
-        variance = jnp.sum(moved * moved) / count
-        normed = (moved / jnp.sqrt(variance + 1e-05)).astype(bf16).astype(f32)
         for k in range(chunks):
             stop = min(128, z.width - 128 * k)
-            rows_ref[:, k, :, :stop] = normed[:, :, 128 * k : 128 * k + stop]
+            rows_ref[:, k, :, :stop] = pixels[:, :, 128 * k : 128 * k + stop]
         total = jnp.zeros((CH * blocks, z.C * z.lanes), f32)
         for k in range(chunks):
             for j in range(S):
@@ -87,6 +83,10 @@
                     [rows_ref[c, k, pl.ds(j, blocks, stride=S), :] for c in range(CH)], axis=0
                 ).astype(bf16)
                 total = total + dot(line, pick_ref[k, j])
+        count = CH * z.height * z.width
+        center = jnp.sum(pixels) / count
+        variance = jnp.sum(jnp.square(pixels - center)) / count
+        total = jnp.where(inside, (total - center) / jnp.sqrt(variance + 1e-05), 0.0)
         for c in range(CH):
             pad_ref[c, margin : margin + blocks, :] = total[c * blocks : (c + 1) * blocks]
         for r in range(z.R):

time: 42.2 us -> 42 us (level)
  no operation moved by 1% of the time
where the time goes in v3:
time: 42 us; the launch traced here: 41.7 us
  waiting for transfers between devices  15.1 us (36%)
  Pallas kernels  13.4 us (32%)
  starting transfers between devices  11.1 us (26%)
  local copies, waits for them, and re-layouts  2.04 us (5%)
    ppermute x5, waiting for transfers between devices, exchange(): return lax.ppermute(value, ('row', 'col'), pairs)  10.9 us
    all_to_all x1, starting transfers between devices, body(): lax.all_to_all(blocks.reshape(z.R * z.C, z.bd * z.T, L), ('row', 'col'),...  7.3 us
    all_to_all x1, waiting for transfers between devices, body(): lax.all_to_all(blocks.reshape(z.R * z.C, z.bd * z.T, L), ('row', 'col'),...  4.25 us
    pallas_call x1, Pallas kernels, gradient(): pl.pallas_call(functools.partial(grad_kernel, z), out_shape=pltpu.HBM((z....  4.08 us
    ppermute x5, starting transfers between devices, exchange(): return lax.ppermute(value, ('row', 'col'), pairs)  3.83 us
    pallas_call x1, Pallas kernels, encode(): pl.pallas_call(functools.partial(encode_kernel, z), out_shape=[pltpu.VMEM...  3.3 us
    pallas_call x2, Pallas kernels, spread_weights(): pl.pallas_call(functools.partial(spread_kernel, z), grid=(count,), out_sh...  2.58 us
    unnamed x2, local copies, waits for them, and re-layouts  2.04 us
  transfers between devices with their start and end apart: 6, of which 5 were waited for; matrix products, arithmetic and copies ran while one was open for 0% of the time, Pallas kernels for 8%

profile of v3, /device:TPU:0, one launch (start us, length us, event | category | flops | bytes accessed | tf_op | source)
XLA Modules:
  0.0 41.7 jit_solution(14553031489156182683)
XLA Ops:
  0.0 1.9 %shard_map.28 = bf16[32,1,24,128]{3,2,1,0:T(8,128)(2,1)} custom-call(bf16[1,3,64,96]{3,2,1,0:T(8,128)(2,1)} %images_hbm.1), custom_call_target="tpu_custom_call" | custom-call | tf_op jit(solution)/shard_map/pallas_call | solution.py:109
  1.9 7.3 %all-to-all-start = ((bf16[32,24,128]{2,1,0:T(8,128)(2,1)}), bf16[32,24,128]{2,1,0:T(8,128)(2,1)S(1)}, u32[]{:S(2)}, u32[]{:S(2)}) async-start(bf16[32,24,128]{2,1,0:T(8,128)(2,1)} %bitcast.5), calls=%async_computation | async-start | bytes 393216 | tf_op jit(solution)/shard_map/all_to_all | solution.py:465
  9.3 0.0 copy-start
  9.3 2.0 %copy-done = bf16[4,3,128,1200]{2,3,1,0:T(8,128)(2,1)S(1)} copy-done((bf16[4,3,128,1200]{2,3,1,0:T(8,128)(2,1)S(1)}, bf16[4,3,128,1200]{2,3,1,0:T(8,128)(2,1)}, u32[]{:S(2)}) %copy-start) | copy-done | bytes 3686424
  11.3 0.6 %shard_map.29.first_ref = bf16[2,1920,384]{2,1,0:T(8,128)(2,1)S(1)} custom-call(bf16[4,3,1200,128]{3,2,1,0:T(8,128)(2,1)S(1)} %bitcast.3), custom_call_target="tpu_custom_call" | custom-call | tf_op jit(solution)/shard_map/pallas_call | solution.py:139
  12.0 1.9 %shard_map.30.wide_hbm = bf16[2,1920,384]{2,1,0:T(8,128)(2,1)} custom-call(bf16[4,3,1200,128]{3,2,1,0:T(8,128)(2,1)S(1)} %bitcast.4), custom_call_target="tpu_custom_call" | custom-call | tf_op jit(solution)/shard_map/pallas_call | solution.py:139
  13.9 4.2 %all-to-all-done.moved_ref = bf16[32,24,128]{2,1,0:T(8,128)(2,1)S(1)} async-done(((bf16[32,24,128]{2,1,0:T(8,128)(2,1)}), bf16[32,24,128]{2,1,0:T(8,128)(2,1)S(1)}, u32[]{:S(2)}, u32[]{:S(2)}) %all-to-all-start) | async-done | bytes 196640 | tf_op jit(solution)/shard_map/all_to_all | solution.py:465
  18.1 3.3 %shard_map.31 = (bf16[24,32,128]{2,1,0:T(8,128)(2,1)S(1)}, bf16[4,3,32,128]{3,2,1,0:T(8,128)(2,1)S(1)}, f32[24,32,128]{2,1,0:T(8,128)S(1)}, bf16[18,32,128]{2,1,...) custom-call(bf16[32,24,128]{2,1,0:T(8,128)(2,1)S(1)} %all-to-all-done.moved_ref, ...), custom_call_target="tpu_custom_call" | custom-call | tf_op jit(solution)/shard_map/pallas_call | solution.py:209
  21.4 1.1 %collective-permute-start = (bf16[18,32,128]{2,1,0:T(8,128)(2,1)S(1)}, bf16[18,32,128]{2,1,0:T(8,128)(2,1)S(1)}, u32[]{:S(2)}, u32[]{:S(2)}) collective-permute-start(bf16[18,32,128]{2,1,0:T(8,128)(2,1)S(1)} %get-tuple-element.22), channel_id=1, source_target_pairs={{0,8},{1,9},{2,10},{3,11},{4,12},{5,13},{6,14},{7,15},{8,0},{9,1},... | collective-permute-start | bytes 442376 | tf_op jit(solution)/shard_map/ppermute | solution.py:444
  22.5 0.0 collective-permute-start.1
  22.5 5.3 %collective-permute-done.swap_ref = bf16[18,32,128]{2,1,0:T(8,128)(2,1)S(1)} collective-permute-done((bf16[18,32,128]{2,1,0:T(8,128)(2,1)S(1)}, bf16[18,32,128]{2,1,0:T(8,128)(2,1)S(1)}, u32[]{:S(2)}, u32[]{:S(2)}) %collective-permute-start) | collective-permute-done | bytes 147488 | tf_op jit(solution)/shard_map/ppermute | solution.py:444
  27.9 0.0 collective-permute-done.1.cross_ref
  27.9 0.3 shard_map.32
  28.2 0.1 collective-permute-start.2
  28.2 1.4 %collective-permute-done.2.near_ref = bf16[24,32,128]{2,1,0:T(8,128)(2,1)S(1)} collective-permute-done((bf16[24,32,128]{2,1,0:T(8,128)(2,1)S(1)}, bf16[24,32,128]{2,1,0:T(8,128)(2,1)S(1)}, u32[]{:S(2)}, u32[]{:S(2)}) %collective-permute-start.2) | collective-permute-done | bytes 196640 | tf_op jit(solution)/shard_map/ppermute | solution.py:444
  29.7 0.2 shard_map.33
  29.9 1.8 %collective-permute-start.3 = (bf16[24,32,128]{2,1,0:T(8,128)(2,1)S(1)}, bf16[24,32,128]{2,1,0:T(8,128)(2,1)S(1)}, u32[]{:S(2)}, u32[]{:S(2)}) collective-permute-start(bf16[24,32,128]{2,1,0:T(8,128)(2,1)S(1)} %get-tuple-element.28), channel_id=1, source_target_pairs={{0,8},{1,2},{2,1},{3,4},{4,3},{5,6},{6,5},{7,15},{8,0},{9,10},{10,... | collective-permute-start | bytes 589832 | tf_op jit(solution)/shard_map/ppermute | solution.py:444
  31.7 0.4 shard_map.34.patch_ref
  32.1 3.5 %collective-permute-done.3.far_ref = bf16[24,32,128]{2,1,0:T(8,128)(2,1)S(1)} collective-permute-done((bf16[24,32,128]{2,1,0:T(8,128)(2,1)S(1)}, bf16[24,32,128]{2,1,0:T(8,128)(2,1)S(1)}, u32[]{:S(2)}, u32[]{:S(2)}) %collective-permute-start.3) | collective-permute-done | bytes 196640 | tf_op jit(solution)/shard_map/ppermute | solution.py:444
  35.6 0.2 shard_map.35
  35.8 0.9 %collective-permute-start.4 = (bf16[12,32,128]{2,1,0:T(8,128)(2,1)S(1)}, bf16[12,32,128]{2,1,0:T(8,128)(2,1)S(1)}, u32[]{:S(2)}, u32[]{:S(2)}) collective-permute-start(bf16[12,32,128]{2,1,0:T(8,128)(2,1)S(1)} %get-tuple-element.32), channel_id=1, source_target_pairs={{0,1},{1,0},{2,3},{3,2},{4,5},{5,4},{6,7},{7,6},{8,9},{9,8},{10,11... | collective-permute-start | bytes 294920 | tf_op jit(solution)/shard_map/ppermute | solution.py:444
  36.7 0.4 shard_map.36.pooled_ref
  37.1 0.6 %collective-permute-done.4.last_ref = bf16[12,32,128]{2,1,0:T(8,128)(2,1)S(1)} collective-permute-done((bf16[12,32,128]{2,1,0:T(8,128)(2,1)S(1)}, bf16[12,32,128]{2,1,0:T(8,128)(2,1)S(1)}, u32[]{:S(2)}, u32[]{:S(2)}) %collective-permute-start.4) | collective-permute-done | bytes 98336 | tf_op jit(solution)/shard_map/ppermute | solution.py:444
  37.7 4.1 %shard_map.37 = f32[4,3,1200,128]{3,2,1,0:T(8,128)} custom-call(f32[24,32,128]{2,1,0:T(8,128)S(1)} %get-tuple-element.31.sum_ref, bf16[12,32,128]{2,1,0:T(8,128)(2,1)S(1)} %collective-permute-done.4.last_ref, bf16[24,32,128]{2,1,0:T(8,128)(2,1)S(1)} %get-tuple-element.29.window_ref, bf16[3,1,1200,128]{3,2,1,0:T(8,128)(2,1)S(1)} %shard_map.34.patch_ref, ...), custom_call_target="tpu_custom_call" | custom-call | tf_op jit(solution)/shard_map/pallas_call | solution.py:420
Async XLA Ops:
  1.9 16.2 %all-to-all-start = ((bf16[32,24,128]{2,1,0:T(8,128)(2,1)}), bf16[32,24,128]{2,1,0:T(8,128)(2,1)S(1)}, u32[]{:S(2)}, u32[]{:S(2)}) async-start(bf16[32,24,128]{2,1,0:T(8,128)(2,1)} %bitcast.5), calls=%async_computation | async-start | bytes 393216 | tf_op jit(solution)/shard_map/all_to_all | solution.py:465
  9.3 2.0 %copy-start = (bf16[4,3,128,1200]{2,3,1,0:T(8,128)(2,1)S(1)}, bf16[4,3,128,1200]{2,3,1,0:T(8,128)(2,1)}, u32[]{:S(2)}) copy-start(bf16[4,3,128,1200]{2,3,1,0:T(8,128)(2,1)} %param.3) | copy-start | bytes 11059204
  21.4 6.4 %collective-permute-start = (bf16[18,32,128]{2,1,0:T(8,128)(2,1)S(1)}, bf16[18,32,128]{2,1,0:T(8,128)(2,1)S(1)}, u32[]{:S(2)}, u32[]{:S(2)}) collective-permute-start(bf16[18,32,128]{2,1,0:T(8,128)(2,1)S(1)} %get-tuple-element.22), channel_id=1, source_target_pairs={{0,8},{1,9},{2,10},{3,11},{4,12},{5,13},{6,14},{7,15},{8,0},{9,1},... | collective-permute-start | bytes 442376 | tf_op jit(solution)/shard_map/ppermute | solution.py:444
  22.5 5.3 %collective-permute-start.1 = (bf16[18,32,128]{2,1,0:T(8,128)(2,1)S(1)}, bf16[18,32,128]{2,1,0:T(8,128)(2,1)S(1)}, u32[]{:S(2)}, u32[]{:S(2)}) collective-permute-start(bf16[18,32,128]{2,1,0:T(8,128)(2,1)S(1)} %get-tuple-element.23), channel_id=1, source_target_pairs={{0,1},{1,0},{2,3},{3,2},{4,5},{5,4},{6,7},{7,6},{8,16},{9,17},{10,... | collective-permute-start | bytes 442376 | tf_op jit(solution)/shard_map/ppermute | solution.py:444
  28.2 1.5 %collective-permute-start.2 = (bf16[24,32,128]{2,1,0:T(8,128)(2,1)S(1)}, bf16[24,32,128]{2,1,0:T(8,128)(2,1)S(1)}, u32[]{:S(2)}, u32[]{:S(2)}) collective-permute-start(bf16[24,32,128]{2,1,0:T(8,128)(2,1)S(1)} %get-tuple-element.26), channel_id=1, source_target_pairs={{0,1},{1,0},{2,3},{3,2},{4,5},{5,4},{6,7},{7,6},{8,9},{9,8},{10,11... | collective-permute-start | bytes 589832 | tf_op jit(solution)/shard_map/ppermute | solution.py:444
  29.9 5.7 %collective-permute-start.3 = (bf16[24,32,128]{2,1,0:T(8,128)(2,1)S(1)}, bf16[24,32,128]{2,1,0:T(8,128)(2,1)S(1)}, u32[]{:S(2)}, u32[]{:S(2)}) collective-permute-start(bf16[24,32,128]{2,1,0:T(8,128)(2,1)S(1)} %get-tuple-element.28), channel_id=1, source_target_pairs={{0,8},{1,2},{2,1},{3,4},{4,3},{5,6},{6,5},{7,15},{8,0},{9,10},{10,... | collective-permute-start | bytes 589832 | tf_op jit(solution)/shard_map/ppermute | solution.py:444
  35.8 1.8 %collective-permute-start.4 = (bf16[12,32,128]{2,1,0:T(8,128)(2,1)S(1)}, bf16[12,32,128]{2,1,0:T(8,128)(2,1)S(1)}, u32[]{:S(2)}, u32[]{:S(2)}) collective-permute-start(bf16[12,32,128]{2,1,0:T(8,128)(2,1)S(1)} %get-tuple-element.32), channel_id=1, source_target_pairs={{0,1},{1,0},{2,3},{3,2},{4,5},{5,4},{6,7},{7,6},{8,9},{9,8},{10,11... | collective-permute-start | bytes 294920 | tf_op jit(solution)/shard_map/ppermute | solution.py:444

commit v4 on v3

--- a/solution.py
+++ b/solution.py
@@ -88,24 +88,27 @@
         variance = jnp.sum(jnp.square(pixels - center)) / count
         total = jnp.where(inside, (total - center) / jnp.sqrt(variance + 1e-05), 0.0)
         for c in range(CH):
-            pad_ref[c, margin : margin + blocks, :] = total[c * blocks : (c + 1) * blocks]
-        for r in range(z.R):
-            for q in range(z.C):
-                block = [
-                    pad_ref[c, z.rd * r : z.rd * r + z.YB, q * z.lanes : (q + 1) * z.lanes]
-                    for c in range(CH)
-                ]
-                out_ref[r * z.C + q, i] = jnp.concatenate(block, axis=0).astype(bf16)
-            if i == z.bd - 1:
-                part = pl.ds(r * z.C, z.C)
-                pltpu.make_async_copy(out_ref.at[part], out_hbm.at[part], out_sems.at[r]).start()
+            pad_ref[i, c, margin : margin + blocks, :] = total[c * blocks : (c + 1) * blocks]
+    copies = []
     for r in range(z.R):
-        part = pl.ds(r * z.C, z.C)
-        pltpu.make_async_copy(out_ref.at[part], out_hbm.at[part], out_sems.at[r]).wait()
+        parts = [
+            pad_ref[i, c, z.rd * r : z.rd * r + z.YB, q * z.lanes : (q + 1) * z.lanes]
+            for q in range(z.C)
+            for i in range(z.bd)
+            for c in range(CH)
+        ]
+        for k in range(0, len(parts), 2 * CH):
+            pair = jnp.concatenate(parts[k : k + 2 * CH], axis=0)
+            out_ref[r, k * z.YB : (k + 2 * CH) * z.YB, :] = pair.astype(bf16)
+        copy = pltpu.make_async_copy(out_ref.at[r], out_hbm.at[r], out_sems.at[r])
+        copy.start()
+        copies.append(copy)
+    for copy in copies:
+        copy.wait()
 
 
 def split(z, images):
-    shape = (z.R * z.C, z.bd, z.T, z.lanes)
+    shape = (z.R, z.C * z.bd * z.T, z.lanes)
     return pl.pallas_call(
         functools.partial(split_kernel, z),
         out_shape=pltpu.HBM(shape, bf16),
@@ -114,7 +117,7 @@
         scratch_shapes=[
             pltpu.VMEM((z.bd, CH, z.height, z.width), bf16),
             pltpu.VMEM((CH, -(-z.width // 128), z.height, 128), f32),
-            pltpu.VMEM((CH, z.height // S + 2 * PAD // S, z.C * z.lanes), f32),
+            pltpu.VMEM((z.bd, CH, z.height // S + 2 * PAD // S, z.C * z.lanes), f32),
             pltpu.VMEM((-(-z.width // 128), S, 128, z.C * z.lanes), bf16),
             pltpu.VMEM(shape, bf16),
             pltpu.SemaphoreType.DMA,

time: 42 us -> 42 us (level)
  no operation moved by 1% of the time
where the time goes in v4:
time: 42 us; the launch traced here: 41.7 us
  waiting for transfers between devices  15.1 us (36%)
  Pallas kernels  13.4 us (32%)
  starting transfers between devices  11.1 us (26%)
  local copies, waits for them, and re-layouts  2.04 us (5%)
    ppermute x5, waiting for transfers between devices, exchange(): return lax.ppermute(value, ('row', 'col'), pairs)  10.9 us
    all_to_all x1, starting transfers between devices, body(): lax.all_to_all(blocks.reshape(z.R * z.C, z.bd * z.T, L), ('row', 'col'),...  7.3 us
    all_to_all x1, waiting for transfers between devices, body(): lax.all_to_all(blocks.reshape(z.R * z.C, z.bd * z.T, L), ('row', 'col'),...  4.25 us
    pallas_call x1, Pallas kernels, gradient(): pl.pallas_call(functools.partial(grad_kernel, z), out_shape=pltpu.HBM((z....  4.08 us
    ppermute x5, starting transfers between devices, exchange(): return lax.ppermute(value, ('row', 'col'), pairs)  3.83 us
    pallas_call x1, Pallas kernels, encode(): pl.pallas_call(functools.partial(encode_kernel, z), out_shape=[pltpu.VMEM...  3.3 us
    pallas_call x2, Pallas kernels, spread_weights(): pl.pallas_call(functools.partial(spread_kernel, z), grid=(count,), out_sh...  2.58 us
    unnamed x2, local copies, waits for them, and re-layouts  2.04 us
  transfers between devices with their start and end apart: 6, of which 5 were waited for; matrix products, arithmetic and copies ran while one was open for 0% of the time, Pallas kernels for 8%

profile of v4, /device:TPU:0, one launch (start us, length us, event | category | flops | bytes accessed | tf_op | source)
XLA Modules:
  0.0 41.7 jit_solution(17415133022106682503)
XLA Ops:
  0.0 1.9 %shard_map.28 = bf16[4,192,128]{2,1,0:T(8,128)(2,1)} custom-call(bf16[1,3,64,96]{3,2,1,0:T(8,128)(2,1)} %images_hbm.1), custom_call_target="tpu_custom_call" | custom-call | tf_op jit(solution)/shard_map/pallas_call | solution.py:112
  1.9 7.3 %all-to-all-start = ((bf16[32,24,128]{2,1,0:T(8,128)(2,1)}), bf16[32,24,128]{2,1,0:T(8,128)(2,1)S(1)}, u32[]{:S(2)}, u32[]{:S(2)}) async-start(bf16[32,24,128]{2,1,0:T(8,128)(2,1)} %bitcast.5), calls=%async_computation | async-start | bytes 393216 | tf_op jit(solution)/shard_map/all_to_all | solution.py:468
  9.3 0.0 copy-start
  9.3 2.0 %copy-done = bf16[4,3,128,1200]{2,3,1,0:T(8,128)(2,1)S(1)} copy-done((bf16[4,3,128,1200]{2,3,1,0:T(8,128)(2,1)S(1)}, bf16[4,3,128,1200]{2,3,1,0:T(8,128)(2,1)}, u32[]{:S(2)}) %copy-start) | copy-done | bytes 3686424
  11.3 0.6 %shard_map.29.first_ref = bf16[2,1920,384]{2,1,0:T(8,128)(2,1)S(1)} custom-call(bf16[4,3,1200,128]{3,2,1,0:T(8,128)(2,1)S(1)} %bitcast.3), custom_call_target="tpu_custom_call" | custom-call | tf_op jit(solution)/shard_map/pallas_call | solution.py:142
  12.0 1.9 %shard_map.30.wide_hbm = bf16[2,1920,384]{2,1,0:T(8,128)(2,1)} custom-call(bf16[4,3,1200,128]{3,2,1,0:T(8,128)(2,1)S(1)} %bitcast.4), custom_call_target="tpu_custom_call" | custom-call | tf_op jit(solution)/shard_map/pallas_call | solution.py:142
  13.9 4.2 %all-to-all-done.moved_ref = bf16[32,24,128]{2,1,0:T(8,128)(2,1)S(1)} async-done(((bf16[32,24,128]{2,1,0:T(8,128)(2,1)}), bf16[32,24,128]{2,1,0:T(8,128)(2,1)S(1)}, u32[]{:S(2)}, u32[]{:S(2)}) %all-to-all-start) | async-done | bytes 196640 | tf_op jit(solution)/shard_map/all_to_all | solution.py:468
  18.1 3.3 %shard_map.31 = (bf16[24,32,128]{2,1,0:T(8,128)(2,1)S(1)}, bf16[4,3,32,128]{3,2,1,0:T(8,128)(2,1)S(1)}, f32[24,32,128]{2,1,0:T(8,128)S(1)}, bf16[18,32,128]{2,1,...) custom-call(bf16[32,24,128]{2,1,0:T(8,128)(2,1)S(1)} %all-to-all-done.moved_ref, ...), custom_call_target="tpu_custom_call" | custom-call | tf_op jit(solution)/shard_map/pallas_call | solution.py:212
  21.4 1.1 %collective-permute-start = (bf16[18,32,128]{2,1,0:T(8,128)(2,1)S(1)}, bf16[18,32,128]{2,1,0:T(8,128)(2,1)S(1)}, u32[]{:S(2)}, u32[]{:S(2)}) collective-permute-start(bf16[18,32,128]{2,1,0:T(8,128)(2,1)S(1)} %get-tuple-element.22), channel_id=1, source_target_pairs={{0,8},{1,9},{2,10},{3,11},{4,12},{5,13},{6,14},{7,15},{8,0},{9,1},... | collective-permute-start | bytes 442376 | tf_op jit(solution)/shard_map/ppermute | solution.py:447
  22.5 0.0 collective-permute-start.1
  22.5 5.3 %collective-permute-done.swap_ref = bf16[18,32,128]{2,1,0:T(8,128)(2,1)S(1)} collective-permute-done((bf16[18,32,128]{2,1,0:T(8,128)(2,1)S(1)}, bf16[18,32,128]{2,1,0:T(8,128)(2,1)S(1)}, u32[]{:S(2)}, u32[]{:S(2)}) %collective-permute-start) | collective-permute-done | bytes 147488 | tf_op jit(solution)/shard_map/ppermute | solution.py:447
  27.9 0.0 collective-permute-done.1.cross_ref
  27.9 0.3 shard_map.32
  28.2 0.1 collective-permute-start.2
  28.2 1.4 %collective-permute-done.2.near_ref = bf16[24,32,128]{2,1,0:T(8,128)(2,1)S(1)} collective-permute-done((bf16[24,32,128]{2,1,0:T(8,128)(2,1)S(1)}, bf16[24,32,128]{2,1,0:T(8,128)(2,1)S(1)}, u32[]{:S(2)}, u32[]{:S(2)}) %collective-permute-start.2) | collective-permute-done | bytes 196640 | tf_op jit(solution)/shard_map/ppermute | solution.py:447
  29.7 0.2 shard_map.33
  29.9 1.8 %collective-permute-start.3 = (bf16[24,32,128]{2,1,0:T(8,128)(2,1)S(1)}, bf16[24,32,128]{2,1,0:T(8,128)(2,1)S(1)}, u32[]{:S(2)}, u32[]{:S(2)}) collective-permute-start(bf16[24,32,128]{2,1,0:T(8,128)(2,1)S(1)} %get-tuple-element.28), channel_id=1, source_target_pairs={{0,8},{1,2},{2,1},{3,4},{4,3},{5,6},{6,5},{7,15},{8,0},{9,10},{10,... | collective-permute-start | bytes 589832 | tf_op jit(solution)/shard_map/ppermute | solution.py:447
  31.7 0.4 shard_map.34.patch_ref
  32.1 3.5 %collective-permute-done.3.far_ref = bf16[24,32,128]{2,1,0:T(8,128)(2,1)S(1)} collective-permute-done((bf16[24,32,128]{2,1,0:T(8,128)(2,1)S(1)}, bf16[24,32,128]{2,1,0:T(8,128)(2,1)S(1)}, u32[]{:S(2)}, u32[]{:S(2)}) %collective-permute-start.3) | collective-permute-done | bytes 196640 | tf_op jit(solution)/shard_map/ppermute | solution.py:447
  35.6 0.2 shard_map.35
  35.8 0.9 %collective-permute-start.4 = (bf16[12,32,128]{2,1,0:T(8,128)(2,1)S(1)}, bf16[12,32,128]{2,1,0:T(8,128)(2,1)S(1)}, u32[]{:S(2)}, u32[]{:S(2)}) collective-permute-start(bf16[12,32,128]{2,1,0:T(8,128)(2,1)S(1)} %get-tuple-element.32), channel_id=1, source_target_pairs={{0,1},{1,0},{2,3},{3,2},{4,5},{5,4},{6,7},{7,6},{8,9},{9,8},{10,11... | collective-permute-start | bytes 294920 | tf_op jit(solution)/shard_map/ppermute | solution.py:447
  36.7 0.4 shard_map.36.pooled_ref
  37.1 0.6 %collective-permute-done.4.last_ref = bf16[12,32,128]{2,1,0:T(8,128)(2,1)S(1)} collective-permute-done((bf16[12,32,128]{2,1,0:T(8,128)(2,1)S(1)}, bf16[12,32,128]{2,1,0:T(8,128)(2,1)S(1)}, u32[]{:S(2)}, u32[]{:S(2)}) %collective-permute-start.4) | collective-permute-done | bytes 98336 | tf_op jit(solution)/shard_map/ppermute | solution.py:447
  37.7 4.1 %shard_map.37 = f32[4,3,1200,128]{3,2,1,0:T(8,128)} custom-call(f32[24,32,128]{2,1,0:T(8,128)S(1)} %get-tuple-element.31.sum_ref, bf16[12,32,128]{2,1,0:T(8,128)(2,1)S(1)} %collective-permute-done.4.last_ref, bf16[24,32,128]{2,1,0:T(8,128)(2,1)S(1)} %get-tuple-element.29.window_ref, bf16[3,1,1200,128]{3,2,1,0:T(8,128)(2,1)S(1)} %shard_map.34.patch_ref, ...), custom_call_target="tpu_custom_call" | custom-call | tf_op jit(solution)/shard_map/pallas_call | solution.py:423
Async XLA Ops:
  1.9 16.2 %all-to-all-start = ((bf16[32,24,128]{2,1,0:T(8,128)(2,1)}), bf16[32,24,128]{2,1,0:T(8,128)(2,1)S(1)}, u32[]{:S(2)}, u32[]{:S(2)}) async-start(bf16[32,24,128]{2,1,0:T(8,128)(2,1)} %bitcast.5), calls=%async_computation | async-start | bytes 393216 | tf_op jit(solution)/shard_map/all_to_all | solution.py:468
  9.3 2.0 %copy-start = (bf16[4,3,128,1200]{2,3,1,0:T(8,128)(2,1)S(1)}, bf16[4,3,128,1200]{2,3,1,0:T(8,128)(2,1)}, u32[]{:S(2)}) copy-start(bf16[4,3,128,1200]{2,3,1,0:T(8,128)(2,1)} %param.3) | copy-start | bytes 11059204
  21.4 6.4 %collective-permute-start = (bf16[18,32,128]{2,1,0:T(8,128)(2,1)S(1)}, bf16[18,32,128]{2,1,0:T(8,128)(2,1)S(1)}, u32[]{:S(2)}, u32[]{:S(2)}) collective-permute-start(bf16[18,32,128]{2,1,0:T(8,128)(2,1)S(1)} %get-tuple-element.22), channel_id=1, source_target_pairs={{0,8},{1,9},{2,10},{3,11},{4,12},{5,13},{6,14},{7,15},{8,0},{9,1},... | collective-permute-start | bytes 442376 | tf_op jit(solution)/shard_map/ppermute | solution.py:447
  22.5 5.3 %collective-permute-start.1 = (bf16[18,32,128]{2,1,0:T(8,128)(2,1)S(1)}, bf16[18,32,128]{2,1,0:T(8,128)(2,1)S(1)}, u32[]{:S(2)}, u32[]{:S(2)}) collective-permute-start(bf16[18,32,128]{2,1,0:T(8,128)(2,1)S(1)} %get-tuple-element.23), channel_id=1, source_target_pairs={{0,1},{1,0},{2,3},{3,2},{4,5},{5,4},{6,7},{7,6},{8,16},{9,17},{10,... | collective-permute-start | bytes 442376 | tf_op jit(solution)/shard_map/ppermute | solution.py:447
  28.2 1.5 %collective-permute-start.2 = (bf16[24,32,128]{2,1,0:T(8,128)(2,1)S(1)}, bf16[24,32,128]{2,1,0:T(8,128)(2,1)S(1)}, u32[]{:S(2)}, u32[]{:S(2)}) collective-permute-start(bf16[24,32,128]{2,1,0:T(8,128)(2,1)S(1)} %get-tuple-element.26), channel_id=1, source_target_pairs={{0,1},{1,0},{2,3},{3,2},{4,5},{5,4},{6,7},{7,6},{8,9},{9,8},{10,11... | collective-permute-start | bytes 589832 | tf_op jit(solution)/shard_map/ppermute | solution.py:447
  29.9 5.7 %collective-permute-start.3 = (bf16[24,32,128]{2,1,0:T(8,128)(2,1)S(1)}, bf16[24,32,128]{2,1,0:T(8,128)(2,1)S(1)}, u32[]{:S(2)}, u32[]{:S(2)}) collective-permute-start(bf16[24,32,128]{2,1,0:T(8,128)(2,1)S(1)} %get-tuple-element.28), channel_id=1, source_target_pairs={{0,8},{1,2},{2,1},{3,4},{4,3},{5,6},{6,5},{7,15},{8,0},{9,10},{10,... | collective-permute-start | bytes 589832 | tf_op jit(solution)/shard_map/ppermute | solution.py:447
  35.8 1.8 %collective-permute-start.4 = (bf16[12,32,128]{2,1,0:T(8,128)(2,1)S(1)}, bf16[12,32,128]{2,1,0:T(8,128)(2,1)S(1)}, u32[]{:S(2)}, u32[]{:S(2)}) collective-permute-start(bf16[12,32,128]{2,1,0:T(8,128)(2,1)S(1)} %get-tuple-element.32), channel_id=1, source_target_pairs={{0,1},{1,0},{2,3},{3,2},{4,5},{5,4},{6,7},{7,6},{8,9},{9,8},{10,11... | collective-permute-start | bytes 294920 | tf_op jit(solution)/shard_map/ppermute | solution.py:447

commit v5 on v4

--- a/solution.py
+++ b/solution.py
@@ -42,9 +42,11 @@
         self.lanes = S * self.stride
         self.YB = self.rd + 2 * PAD // S
         self.T = CH * self.YB
+        self.late = 2 * PAD - self.w
         self.KW = CH * FIELD * self.stride
         self.per = 128 // self.B
         self.groups = self.rd // self.per
+        assert self.late > 0 and self.stride % self.late == 0 and self.T % (self.stride // self.late) == 0
         assert self.B * self.per == 128 and self.groups * self.per == self.rd and self.F == 128
         assert self.C % 2 == 0 and self.R % 2 == 0 and self.rd >= 4 and self.cd >= 2 and self.lanes == 128
         assert self.height == self.R * self.h and self.width == self.C * self.w
@@ -286,7 +288,27 @@
     return jnp.where(inside, first, 0.0), jnp.where(inside, second, 0.0)
 
 
-def rows_kernel(z, contrib_ref, hidden_ref, swap_ref, cross_ref, sum_ref, tall_ref, send_ref):
+def pack_late(z, to_right, tiles):
+    across = lax.broadcasted_iota(jnp.int32, tiles[0].shape, 1) % z.stride
+    start = jnp.where(to_right, 2 * z.w, 0)
+    packed = jnp.zeros_like(tiles[0])
+    for k, tile in enumerate(tiles):
+        at = k * z.late
+        turned = pltpu.roll(tile, (z.lanes + at - start) % z.lanes, 1)
+        packed = jnp.where((across >= at) & (across < at + z.late), turned, packed)
+    return packed
+
+
+def unpack_late(z, from_left, packed, k):
+    across = lax.broadcasted_iota(jnp.int32, packed.shape, 1) % z.stride
+    start = jnp.where(from_left, 0, 2 * z.w)
+    turned = pltpu.roll(packed, (z.lanes + start - k * z.late) % z.lanes, 1)
+    return jnp.where((across >= start) & (across < start + z.late), turned, 0.0)
+
+
+def rows_kernel(
+    z, contrib_ref, hidden_ref, swap_ref, cross_ref, sum_ref, tall_ref, near_ref, far_ref, late_ref
+):
     half = z.YB // 2
     sum_ref[...] = contrib_ref[...]
     row = lax.axis_index("row")
@@ -299,8 +321,14 @@
             for y in range(half):
                 sum_ref[c * z.YB + first + y] += jnp.where(exists, ref[c * half + y].astype(f32), 0.0)
     even = is_even()
+    odd = jnp.logical_not(even)
     for t in range(0, z.T, 2):
-        send_ref[t // 2] = pack_side(z, even, sum_ref[t], sum_ref[t + 1]).astype(bf16)
+        pair = sum_ref[t], sum_ref[t + 1]
+        far_ref[t // 2] = pack_side(z, odd, *pair).astype(bf16)
+        near_ref[t // 2] = pack_side(z, even, *pair).astype(bf16)
+    slots = z.stride // z.late
+    for t in range(0, z.T, slots):
+        late_ref[t // slots] = pack_late(z, even, [sum_ref[t + k] for k in range(slots)]).astype(bf16)
     for q in range(z.cd):
         squares = [jnp.square(hidden_ref[i, q].astype(f32)) for i in range(z.rd)]
         above, below = [], []
@@ -314,34 +342,38 @@
         squares = above + squares + below
         for i in range(z.rd + 2):
             tall_ref[i, q] = squares[i] + squares[i + 1] + squares[i + 2]
-    first = jnp.where(even, z.cd - 2, 0)
-    for i in range(z.rd + 2):
+    for ref, right in ((near_ref, even), (far_ref, odd)):
+        first = jnp.where(right, z.cd - 2, 0)
+        for i in range(z.rd + 2):
+            for k in range(2):
+                ref[z.T // 2 + 2 * i + k] = tall_ref[i, first + k].astype(bf16)
+
+
+def merge_kernel(z, sum_ref, near_ref, far_ref, late_ref, out_ref):
+    even = is_even()
+    col = lax.axis_index("col")
+    exists = jnp.where(even, col > 0, col < z.C - 1)
+    late_exists = jnp.where(even, col > 1, col < z.C - 2)
+    slots = z.stride // z.late
+    for t in range(0, z.T, 2):
+        near = unpack_side(z, jnp.logical_not(even), near_ref[t // 2].astype(f32))
+        came = unpack_side(z, even, jnp.where(exists, far_ref[t // 2].astype(f32), 0.0))
+        late = jnp.where(late_exists, late_ref[t // slots].astype(f32), 0.0)
         for k in range(2):
-            send_ref[z.T // 2 + 2 * i + k] = tall_ref[i, first + k].astype(bf16)
-
-
-def near_kernel(z, sum_ref, tall_ref, near_ref, out_ref, send_ref):
+            out_ref[t + k] = sum_ref[t + k] + near[k] + came[k] + unpack_late(z, even, late, t % slots + k)
+
+
+def unpack_last(z, packed):
     even = is_even()
-    for t in range(0, z.T, 2):
-        came = unpack_side(z, jnp.logical_not(even), near_ref[t // 2].astype(f32))
-        total = [sum_ref[t + k] + came[k] for k in range(2)]
-        for k in range(2):
-            out_ref[t + k] = total[k]
-        send_ref[t // 2] = pack_side(z, jnp.logical_not(even), *total).astype(bf16)
-    first = jnp.where(even, 0, z.cd - 2)
-    for i in range(z.rd + 2):
-        for k in range(2):
-            send_ref[z.T // 2 + 2 * i + k] = tall_ref[i, first + k].astype(bf16)
-
-
-def far_kernel(z, sum_ref, far_ref, out_ref, send_ref):
-    even = is_even()
-    exists = jnp.where(even, lax.axis_index("col") > 0, lax.axis_index("col") < z.C - 1)
-    for t in range(0, z.T, 2):
-        came = unpack_side(z, even, jnp.where(exists, far_ref[t // 2].astype(f32), 0.0))
-        for k in range(2):
-            out_ref[t + k] = sum_ref[t + k] + came[k]
-        send_ref[t // 2] = pack_side(z, even, *came).astype(bf16)
+    col = lax.axis_index("col")
+    exists = jnp.where(even, col + 1 < z.C - 1, col - 1 > 0)
+    across = lax.broadcasted_iota(jnp.int32, packed.shape, 1) % z.stride
+    start = jnp.where(even, 2 * z.w, 0)
+    inside = (across >= start) & (across < start + z.late) & exists
+    by = jnp.where(even, 2 * z.w, z.lanes - z.w)
+    first = pltpu.roll(packed, by, 1)
+    second = pltpu.roll(packed, (by + z.lanes - 2 * PAD) % z.lanes, 1)
+    return jnp.where(inside, first, 0.0), jnp.where(inside, second, 0.0)
 
 
 def pool_kernel(z, hidden_ref, tall_ref, near_ref, far_ref, out_ref, wide_ref, inverse_ref):
@@ -378,13 +410,12 @@
     out_hbm, resid_ref, flat_ref, dense_ref, resid_patch_ref, factor_ref, out_ref, sems,
 ):
     B, F = z.B, z.F
-    from_left = jnp.logical_not(is_even())
     lane = lax.broadcasted_iota(jnp.int32, (1, z.lanes), 1) % z.stride
     x = lax.axis_index("col") * z.w - PAD + lane
     across = ((x >= 0) & (x < z.width)).astype(f32)
     first = lax.axis_index("row") * z.h - PAD
     for t in range(0, z.T, 2):
-        came = unpack_side(z, from_left, last_ref[t // 2].astype(f32))
+        came = unpack_last(z, last_ref[t // 2].astype(f32))
         for n in range(2):
             line = first + S * ((t + n) % z.YB)
             inside = jnp.where((line >= 0) & (line < z.height), across, 0.0)
@@ -447,6 +478,15 @@
     return lax.ppermute(value, ("row", "col"), pairs)
 
 
+def shift(z, value):
+    pairs = []
+    for r in range(z.R):
+        for c in range(z.C):
+            to = (c + (-2 if c % 2 else 2)) % z.C
+            pairs.append((r * z.C + c, r * z.C + to))
+    return lax.ppermute(value, ("row", "col"), pairs)
+
+
 def cross_row(z, r, c):
     to = r + 1 if r % 2 else r - 1
     return (to, c) if 0 <= to < z.R else (r, c ^ 1)
@@ -476,22 +516,22 @@
     swapped = exchange(z, to_swap, lambda z, r, c: (r ^ 1, c))
     tall = ((z.rd + 2, z.cd, B, z.F), f32)
     sent = ((z.T // 2 + 2 * (z.rd + 2), B, L), bf16)
-    total, tall, send = vmem_call(
-        functools.partial(rows_kernel, z), [tiles, tall, sent], [], contrib, hidden, swapped, crossed
+    late = ((z.T * z.late // z.stride, B, L), bf16)
+    total, tall, to_near, to_far, to_late = vmem_call(
+        functools.partial(rows_kernel, z), [tiles, tall, sent, sent, late], [], contrib, hidden, swapped, crossed
     )
-    near = exchange(z, send, swap_col)
-    total, send = vmem_call(functools.partial(near_kernel, z), [tiles, sent], [], total, tall, near)
+    far = exchange(z, to_far, cross_col)
+    late = shift(z, to_late)
+    near = exchange(z, to_near, swap_col)
     (patch,) = vmem_call(
         functools.partial(patches_kernel, z),
         [((z.cd, z.groups, K, 128), bf16)],
         [((z.groups, z.KW, 128), f32), ((K, 128), f32)],
         window,
     )
-    far, patch = lax.optimization_barrier((exchange(z, send, cross_col), patch))
-    total, send = vmem_call(
-        functools.partial(far_kernel, z), [tiles, ((z.T // 2, B, L), bf16)], [], total, far
-    )
-    last = exchange(z, send, swap_col)
+    far, near, late, patch = lax.optimization_barrier((far, near, late, patch))
+    last = exchange(z, far, swap_col)
+    (total,) = vmem_call(functools.partial(merge_kernel, z), [tiles], [], total, near, far, late)
     (pooled,) = vmem_call(
         functools.partial(pool_kernel, z),
         [((z.rd, z.cd, B, z.F), f32)],

time: 42 us -> 40.6 us (0.967)
  starting transfers between devices: 11.1 us -> 10.5 us
  waiting for transfers between devices: 15.1 us -> 14.5 us
    ppermute x5, waiting for transfers between devices: 10.9 us -> 5.91 us  [exchange(): return lax.ppermute(value, ('row', 'col'), pairs)]
    ppermute x0 -> x1, waiting for transfers between devices: none -> 4.32 us  [shift(): return lax.ppermute(value, ('row', 'col'), pairs)]
    ppermute x5, starting transfers between devices: 3.83 us -> 3.16 us  [exchange(): return lax.ppermute(value, ('row', 'col'), pairs)]
    pallas_call x5 -> x4, Pallas kernels: 1.47 us -> 1.4 us  [vmem_call(): pl.pallas_call(kernel, out_shape=[pltpu.VMEM(*s) for s in shapes], in_spe...]
  transfers between devices with their start and end apart: 6 -> 7, of which waited for: 5 -> 4; matrix products, arithmetic and copies ran while one was open for 0% -> 0% of each run, Pallas kernels for 8% -> 9%
where the time goes in v5:
time: 40.6 us; the launch traced here: 40.3 us
  waiting for transfers between devices  14.5 us (36%)
  Pallas kernels  13.3 us (33%)
  starting transfers between devices  10.5 us (26%)
  local copies, waits for them, and re-layouts  2.04 us (5%)
    all_to_all x1, starting transfers between devices, body(): lax.all_to_all(blocks.reshape(z.R * z.C, z.bd * z.T, L), ('row', 'col'),...  7.3 us
    ppermute x5, waiting for transfers between devices, exchange(): return lax.ppermute(value, ('row', 'col'), pairs)  5.91 us
    ppermute x1, waiting for transfers between devices, shift(): return lax.ppermute(value, ('row', 'col'), pairs)  4.32 us
    all_to_all x1, waiting for transfers between devices, body(): lax.all_to_all(blocks.reshape(z.R * z.C, z.bd * z.T, L), ('row', 'col'),...  4.25 us
    pallas_call x1, Pallas kernels, gradient(): pl.pallas_call(functools.partial(grad_kernel, z), out_shape=pltpu.HBM((z....  4.04 us
    pallas_call x1, Pallas kernels, encode(): pl.pallas_call(functools.partial(encode_kernel, z), out_shape=[pltpu.VMEM...  3.3 us
    ppermute x5, starting transfers between devices, exchange(): return lax.ppermute(value, ('row', 'col'), pairs)  3.16 us
    pallas_call x2, Pallas kernels, spread_weights(): pl.pallas_call(functools.partial(spread_kernel, z), grid=(count,), out_sh...  2.58 us
  transfers between devices with their start and end apart: 7, of which 4 were waited for; matrix products, arithmetic and copies ran while one was open for 0% of the time, Pallas kernels for 9%

profile of v5, /device:TPU:0, one launch (start us, length us, event | category | flops | bytes accessed | tf_op | source)
XLA Modules:
  0.0 40.3 jit_solution(2645854564026639931)
XLA Ops:
  0.0 1.9 %shard_map.28 = bf16[4,192,128]{2,1,0:T(8,128)(2,1)} custom-call(bf16[1,3,64,96]{3,2,1,0:T(8,128)(2,1)} %images_hbm.1), custom_call_target="tpu_custom_call" | custom-call | tf_op jit(solution)/shard_map/pallas_call | solution.py:114
  1.9 7.3 %all-to-all-start = ((bf16[32,24,128]{2,1,0:T(8,128)(2,1)}), bf16[32,24,128]{2,1,0:T(8,128)(2,1)S(1)}, u32[]{:S(2)}, u32[]{:S(2)}) async-start(bf16[32,24,128]{2,1,0:T(8,128)(2,1)} %bitcast.5), calls=%async_computation | async-start | bytes 393216 | tf_op jit(solution)/shard_map/all_to_all | solution.py:508
  9.3 0.0 copy-start
  9.3 2.0 %copy-done = bf16[4,3,128,1200]{2,3,1,0:T(8,128)(2,1)S(1)} copy-done((bf16[4,3,128,1200]{2,3,1,0:T(8,128)(2,1)S(1)}, bf16[4,3,128,1200]{2,3,1,0:T(8,128)(2,1)}, u32[]{:S(2)}) %copy-start) | copy-done | bytes 3686424
  11.3 0.6 %shard_map.29.first_ref = bf16[2,1920,384]{2,1,0:T(8,128)(2,1)S(1)} custom-call(bf16[4,3,1200,128]{3,2,1,0:T(8,128)(2,1)S(1)} %bitcast.3), custom_call_target="tpu_custom_call" | custom-call | tf_op jit(solution)/shard_map/pallas_call | solution.py:144
  12.0 1.9 %shard_map.30.wide_hbm = bf16[2,1920,384]{2,1,0:T(8,128)(2,1)} custom-call(bf16[4,3,1200,128]{3,2,1,0:T(8,128)(2,1)S(1)} %bitcast.4), custom_call_target="tpu_custom_call" | custom-call | tf_op jit(solution)/shard_map/pallas_call | solution.py:144
  13.9 4.2 %all-to-all-done.moved_ref = bf16[32,24,128]{2,1,0:T(8,128)(2,1)S(1)} async-done(((bf16[32,24,128]{2,1,0:T(8,128)(2,1)}), bf16[32,24,128]{2,1,0:T(8,128)(2,1)S(1)}, u32[]{:S(2)}, u32[]{:S(2)}) %all-to-all-start) | async-done | bytes 196640 | tf_op jit(solution)/shard_map/all_to_all | solution.py:508
  18.1 3.3 %shard_map.31 = (bf16[24,32,128]{2,1,0:T(8,128)(2,1)S(1)}, bf16[4,3,32,128]{3,2,1,0:T(8,128)(2,1)S(1)}, f32[24,32,128]{2,1,0:T(8,128)S(1)}, bf16[18,32,128]{2,1,...) custom-call(bf16[32,24,128]{2,1,0:T(8,128)(2,1)S(1)} %all-to-all-done.moved_ref, ...), custom_call_target="tpu_custom_call" | custom-call | tf_op jit(solution)/shard_map/pallas_call | solution.py:214
  21.4 1.1 %collective-permute-start = (bf16[18,32,128]{2,1,0:T(8,128)(2,1)S(1)}, bf16[18,32,128]{2,1,0:T(8,128)(2,1)S(1)}, u32[]{:S(2)}, u32[]{:S(2)}) collective-permute-start(bf16[18,32,128]{2,1,0:T(8,128)(2,1)S(1)} %get-tuple-element.22), channel_id=1, source_target_pairs={{0,8},{1,9},{2,10},{3,11},{4,12},{5,13},{6,14},{7,15},{8,0},{9,1},... | collective-permute-start | bytes 442376 | tf_op jit(solution)/shard_map/ppermute | solution.py:478
  22.5 0.0 collective-permute-start.1
  22.5 5.3 %collective-permute-done.swap_ref = bf16[18,32,128]{2,1,0:T(8,128)(2,1)S(1)} collective-permute-done((bf16[18,32,128]{2,1,0:T(8,128)(2,1)S(1)}, bf16[18,32,128]{2,1,0:T(8,128)(2,1)S(1)}, u32[]{:S(2)}, u32[]{:S(2)}) %collective-permute-start) | collective-permute-done | bytes 147488 | tf_op jit(solution)/shard_map/ppermute | solution.py:478
  27.9 0.0 collective-permute-done.1.cross_ref
  27.9 0.4 %shard_map.32 = (f32[24,32,128]{2,1,0:T(8,128)S(1)}, f32[6,3,32,128]{3,2,1,0:T(8,128)S(1)}, bf16[24,32,128]{2,1,0:T(8,128)(2,1)S(1)}, bf16[24,32,128]{2,1,0:T(8,128)(2,1)S(1)}, bf16[3,32,128]{2,1,0:T(8,128)(2,1)S(1)}) custom-call(f32[24,32,128]{2,1,0:T(8,128)S(1)} %get-tuple-element.20.contrib_ref, bf16[4,3,32,128]{3,2,1,0:T(8,128)(2,1)S(1)} %get-tuple-element.21.hidden_ref, ...), custom_call_target="tpu_custom_call" | custom-call | tf_op jit(solution)/shard_map/pallas_call | solution.py:255
  28.3 1.8 %collective-permute-start.2 = (bf16[24,32,128]{2,1,0:T(8,128)(2,1)S(1)}, bf16[24,32,128]{2,1,0:T(8,128)(2,1)S(1)}, u32[]{:S(2)}, u32[]{:S(2)}) collective-permute-start(bf16[24,32,128]{2,1,0:T(8,128)(2,1)S(1)} %get-tuple-element.25), channel_id=1, source_target_pairs={{0,8},{1,2},{2,1},{3,4},{4,3},{5,6},{6,5},{7,15},{8,0},{9,10},{10,... | collective-permute-start | bytes 589832 | tf_op jit(solution)/shard_map/ppermute | solution.py:478
  30.1 0.0 collective-permute-start.3
  30.1 0.0 collective-permute-start.4
  30.1 0.4 shard_map.33.patch_ref
  30.5 4.3 %collective-permute-done.4.late_ref = bf16[3,32,128]{2,1,0:T(8,128)(2,1)S(1)} collective-permute-done((bf16[3,32,128]{2,1,0:T(8,128)(2,1)S(1)}, bf16[3,32,128]{2,1,0:T(8,128)(2,1)S(1)}, u32[]{:S(2)}, u32[]{:S(2)}) %collective-permute-start.4) | collective-permute-done | bytes 24608 | tf_op jit(solution)/shard_map/ppermute | solution.py:487
  34.8 0.0 collective-permute-done.2.far_ref
  34.8 0.0 collective-permute-done.3.near_ref
  34.8 0.3 collective-permute-start.5
  35.1 0.4 shard_map.35.pooled_ref
  35.4 0.2 shard_map.34.sum_ref
  35.7 0.6 %collective-permute-done.5.last_ref = bf16[24,32,128]{2,1,0:T(8,128)(2,1)S(1)} collective-permute-done((bf16[24,32,128]{2,1,0:T(8,128)(2,1)S(1)}, bf16[24,32,128]{2,1,0:T(8,128)(2,1)S(1)}, u32[]{:S(2)}, u32[]{:S(2)}) %collective-permute-start.5) | collective-permute-done | bytes 196640 | tf_op jit(solution)/shard_map/ppermute | solution.py:478
  36.3 4.0 %shard_map.36 = f32[4,3,1200,128]{3,2,1,0:T(8,128)} custom-call(f32[24,32,128]{2,1,0:T(8,128)S(1)} %shard_map.34.sum_ref, bf16[24,32,128]{2,1,0:T(8,128)(2,1)S(1)} %collective-permute-done.5.last_ref, bf16[24,32,128]{2,1,0:T(8,128)(2,1)S(1)} %get-tuple-element.28.window_ref, bf16[3,1,1200,128]{3,2,1,0:T(8,128)(2,1)S(1)} %shard_map.33.patch_ref, ...), custom_call_target="tpu_custom_call" | custom-call | tf_op jit(solution)/shard_map/pallas_call | solution.py:454
Async XLA Ops:
  1.9 16.2 %all-to-all-start = ((bf16[32,24,128]{2,1,0:T(8,128)(2,1)}), bf16[32,24,128]{2,1,0:T(8,128)(2,1)S(1)}, u32[]{:S(2)}, u32[]{:S(2)}) async-start(bf16[32,24,128]{2,1,0:T(8,128)(2,1)} %bitcast.5), calls=%async_computation | async-start | bytes 393216 | tf_op jit(solution)/shard_map/all_to_all | solution.py:508
  9.3 2.0 %copy-start = (bf16[4,3,128,1200]{2,3,1,0:T(8,128)(2,1)S(1)}, bf16[4,3,128,1200]{2,3,1,0:T(8,128)(2,1)}, u32[]{:S(2)}) copy-start(bf16[4,3,128,1200]{2,3,1,0:T(8,128)(2,1)} %param.3) | copy-start | bytes 11059204
  21.4 6.4 %collective-permute-start = (bf16[18,32,128]{2,1,0:T(8,128)(2,1)S(1)}, bf16[18,32,128]{2,1,0:T(8,128)(2,1)S(1)}, u32[]{:S(2)}, u32[]{:S(2)}) collective-permute-start(bf16[18,32,128]{2,1,0:T(8,128)(2,1)S(1)} %get-tuple-element.22), channel_id=1, source_target_pairs={{0,8},{1,9},{2,10},{3,11},{4,12},{5,13},{6,14},{7,15},{8,0},{9,1},... | collective-permute-start | bytes 442376 | tf_op jit(solution)/shard_map/ppermute | solution.py:478
  22.5 5.3 %collective-permute-start.1 = (bf16[18,32,128]{2,1,0:T(8,128)(2,1)S(1)}, bf16[18,32,128]{2,1,0:T(8,128)(2,1)S(1)}, u32[]{:S(2)}, u32[]{:S(2)}) collective-permute-start(bf16[18,32,128]{2,1,0:T(8,128)(2,1)S(1)} %get-tuple-element.23), channel_id=1, source_target_pairs={{0,1},{1,0},{2,3},{3,2},{4,5},{5,4},{6,7},{7,6},{8,16},{9,17},{10,... | collective-permute-start | bytes 442376 | tf_op jit(solution)/shard_map/ppermute | solution.py:478
  28.3 6.5 %collective-permute-start.2 = (bf16[24,32,128]{2,1,0:T(8,128)(2,1)S(1)}, bf16[24,32,128]{2,1,0:T(8,128)(2,1)S(1)}, u32[]{:S(2)}, u32[]{:S(2)}) collective-permute-start(bf16[24,32,128]{2,1,0:T(8,128)(2,1)S(1)} %get-tuple-element.25), channel_id=1, source_target_pairs={{0,8},{1,2},{2,1},{3,4},{4,3},{5,6},{6,5},{7,15},{8,0},{9,10},{10,... | collective-permute-start | bytes 589832 | tf_op jit(solution)/shard_map/ppermute | solution.py:478
  30.1 4.7 %collective-permute-start.3 = (bf16[24,32,128]{2,1,0:T(8,128)(2,1)S(1)}, bf16[24,32,128]{2,1,0:T(8,128)(2,1)S(1)}, u32[]{:S(2)}, u32[]{:S(2)}) collective-permute-start(bf16[24,32,128]{2,1,0:T(8,128)(2,1)S(1)} %get-tuple-element.26), channel_id=1, source_target_pairs={{0,1},{1,0},{2,3},{3,2},{4,5},{5,4},{6,7},{7,6},{8,9},{9,8},{10,11... | collective-permute-start | bytes 589832 | tf_op jit(solution)/shard_map/ppermute | solution.py:478
  30.1 4.7 %collective-permute-start.4 = (bf16[3,32,128]{2,1,0:T(8,128)(2,1)S(1)}, bf16[3,32,128]{2,1,0:T(8,128)(2,1)S(1)}, u32[]{:S(2)}, u32[]{:S(2)}) collective-permute-start(bf16[3,32,128]{2,1,0:T(8,128)(2,1)S(1)} %get-tuple-element.27), channel_id=1, source_target_pairs={{0,2},{1,7},{2,4},{3,1},{4,6},{5,3},{6,0},{7,5},{8,10},{9,15},{10,... | collective-permute-start | bytes 73736 | tf_op jit(solution)/shard_map/ppermute | solution.py:487
  34.8 1.4 %collective-permute-start.5 = (bf16[24,32,128]{2,1,0:T(8,128)(2,1)S(1)}, bf16[24,32,128]{2,1,0:T(8,128)(2,1)S(1)}, u32[]{:S(2)}, u32[]{:S(2)}) collective-permute-start(bf16[24,32,128]{2,1,0:T(8,128)(2,1)S(1)} %collective-permute-done.2.far_ref), channel_id=1, source_target_pairs={{0,1},{1,0},{2,3},{3,2},{4,5},{5,4},{6,7},{7,6},{8,9},{9,8},{10,11... | collective-permute-start | bytes 589832 | tf_op jit(solution)/shard_map/ppermute | solution.py:478

commit v6 on v5

--- a/solution.py
+++ b/solution.py
@@ -43,6 +43,9 @@
         self.YB = self.rd + 2 * PAD // S
         self.T = CH * self.YB
         self.late = 2 * PAD - self.w
+        late_even = [q for q in range(self.cd) if S * q + FIELD > 2 * self.w]
+        late_odd = [q for q in range(self.cd) if S * q < self.late]
+        self.early = next(q for q in range(self.cd) if q not in late_even + late_odd)
         self.KW = CH * FIELD * self.stride
         self.per = 128 // self.B
         self.groups = self.rd // self.per
@@ -240,14 +243,39 @@
         for i in range(c * FIELD, (c + 1) * FIELD):
             at = z.stride * i + S * q
             dense_ref[FIELD * i : FIELD * (i + 1), :] = flat_ref[group, at : at + FIELD, :]
-        out_ref[q, group, rows, :] = dense_ref[rows, :].astype(bf16)
+        out_ref[group, rows, :] = dense_ref[rows, :].astype(bf16)
 
 
 def patches_kernel(z, window_ref, out_ref, flat_ref, dense_ref):
     turn_fields(z, lambda t: window_ref[t], flat_ref)
     for q in range(z.cd):
         for c in range(CH):
-            place_fields(z, q, c, flat_ref, dense_ref, out_ref)
+            place_fields(z, q, c, flat_ref, dense_ref, out_ref.at[q])
+
+
+def store_residual(z, recon_of, window_ref, resid_ref):
+    lane = lax.broadcasted_iota(jnp.int32, (1, z.lanes), 1) % z.stride
+    x = lax.axis_index("col") * z.w - PAD + lane
+    across = ((x >= 0) & (x < z.width)).astype(f32)
+    first = lax.axis_index("row") * z.h - PAD
+    for t in range(0, z.T, 2):
+        recon = recon_of(t)
+        for n in range(2):
+            line = first + S * ((t + n) % z.YB)
+            inside = jnp.where((line >= 0) & (line < z.height), across, 0.0)
+            resid_ref[t + n] = ((recon[n] - window_ref[t + n].astype(f32)) * inside).astype(bf16)
+
+
+def fill_factor(z, q, resid_ref, pooled_ref, hidden_ref, first_ref, wide_ref, factor_ref):
+    B, F = z.B, z.F
+    factor_ref[...] = jnp.zeros_like(factor_ref)
+    for p in range(z.rd):
+        weight = first_ref.at[p] if p < HELD else wide_ref.at[p - HELD]
+        back = dot(field(z, p, resid_ref), weight[:, q * F : (q + 1) * F])
+        group, at = p // z.per, p % z.per * B
+        columns = slice(p % z.per * F, (p % z.per + 1) * F)
+        factor_ref[group, at : at + B, columns] = (pooled_ref[p, q] + back).astype(bf16)
+        factor_ref[group, 128 + at : 128 + at + B, columns] = hidden_ref[p, q]
 
 
 def vmem_call(kernel, shapes, scratch, *args):
@@ -349,18 +377,31 @@
                 ref[z.T // 2 + 2 * i + k] = tall_ref[i, first + k].astype(bf16)
 
 
-def merge_kernel(z, sum_ref, near_ref, far_ref, late_ref, out_ref):
+def merge_kernel(
+    z, sum_ref, near_ref, far_ref, late_ref, window_ref, hidden_ref, pooled_ref, first_ref, wide_ref,
+    out_ref, patch_ref, factor_ref, resid_ref, flat_ref, dense_ref,
+):
     even = is_even()
     col = lax.axis_index("col")
     exists = jnp.where(even, col > 0, col < z.C - 1)
     late_exists = jnp.where(even, col > 1, col < z.C - 2)
     slots = z.stride // z.late
-    for t in range(0, z.T, 2):
+
+    def recon_of(t):
         near = unpack_side(z, jnp.logical_not(even), near_ref[t // 2].astype(f32))
         came = unpack_side(z, even, jnp.where(exists, far_ref[t // 2].astype(f32), 0.0))
         late = jnp.where(late_exists, late_ref[t // slots].astype(f32), 0.0)
+        recon = []
         for k in range(2):
-            out_ref[t + k] = sum_ref[t + k] + near[k] + came[k] + unpack_late(z, even, late, t % slots + k)
+            recon.append(sum_ref[t + k] + near[k] + came[k] + unpack_late(z, even, late, t % slots + k))
+            out_ref[t + k] = recon[k]
+        return recon
+
+    store_residual(z, recon_of, window_ref, resid_ref)
+    turn_fields(z, lambda t: resid_ref[t], flat_ref)
+    fill_factor(z, z.early, resid_ref, pooled_ref, hidden_ref, first_ref, wide_ref, factor_ref)
+    for c in range(CH):
+        place_fields(z, z.early, c, flat_ref, dense_ref, patch_ref)
 
 
 def unpack_last(z, packed):
@@ -407,44 +448,39 @@
 
 def grad_kernel(
     z, sum_ref, last_ref, window_ref, patch_ref, hidden_ref, pooled_ref, first_ref, wide_ref,
+    early_patch_ref, early_factor_ref,
     out_hbm, resid_ref, flat_ref, dense_ref, resid_patch_ref, factor_ref, out_ref, sems,
 ):
     B, F = z.B, z.F
-    lane = lax.broadcasted_iota(jnp.int32, (1, z.lanes), 1) % z.stride
-    x = lax.axis_index("col") * z.w - PAD + lane
-    across = ((x >= 0) & (x < z.width)).astype(f32)
-    first = lax.axis_index("row") * z.h - PAD
-    for t in range(0, z.T, 2):
+    copies = []
+
+    def write(q, k, resid_patch, factor):
+        rows = slice(k * FIELD * FIELD, (k + 1) * FIELD * FIELD)
+        for group in range(z.groups):
+            both = jnp.concatenate([patch_ref[q, group, rows, :], resid_patch[group, rows, :]], axis=1)
+            value = dot(both, factor[group]) * (1.0 / B)
+            for inner in range(z.per):
+                out_ref[group * z.per + inner, q, rows, :] = value[:, inner * F : (inner + 1) * F]
+        copy = pltpu.make_async_copy(out_ref.at[:, q, rows, :], out_hbm.at[:, q, rows, :], sems.at[q, k])
+        copy.start()
+        copies.append(copy)
+
+    for k in range(CH):
+        write(z.early, k, early_patch_ref, early_factor_ref)
+
+    def recon_of(t):
         came = unpack_last(z, last_ref[t // 2].astype(f32))
-        for n in range(2):
-            line = first + S * ((t + n) % z.YB)
-            inside = jnp.where((line >= 0) & (line < z.height), across, 0.0)
-            recon = sum_ref[t + n] + came[n]
-            resid_ref[t + n] = ((recon - window_ref[t + n].astype(f32)) * inside).astype(bf16)
-
+        return [sum_ref[t + k] + came[k] for k in range(2)]
+
+    store_residual(z, recon_of, window_ref, resid_ref)
     turn_fields(z, lambda t: resid_ref[t], flat_ref)
-    factor_ref[...] = jnp.zeros_like(factor_ref)
-    copies = []
     for q in range(z.cd):
-        for p in range(z.rd):
-            weight = first_ref.at[p] if p < HELD else wide_ref.at[p - HELD]
-            back = dot(field(z, p, resid_ref), weight[:, q * F : (q + 1) * F])
-            group, inner = p // z.per, p % z.per
-            columns = slice(inner * F, (inner + 1) * F)
-            at = inner * B
-            factor_ref[q, group, at : at + B, columns] = (pooled_ref[p, q] + back).astype(bf16)
-            factor_ref[q, group, 128 + at : 128 + at + B, columns] = hidden_ref[p, q]
+        if q == z.early:
+            continue
+        fill_factor(z, q, resid_ref, pooled_ref, hidden_ref, first_ref, wide_ref, factor_ref.at[q])
         for k in range(CH):
-            place_fields(z, q, k, flat_ref, dense_ref, resid_patch_ref)
-            rows = slice(k * FIELD * FIELD, (k + 1) * FIELD * FIELD)
-            for group in range(z.groups):
-                both = jnp.concatenate([patch_ref[q, group, rows, :], resid_patch_ref[q, group, rows, :]], axis=1)
-                value = dot(both, factor_ref[q, group]) * (1.0 / B)
-                for inner in range(z.per):
-                    out_ref[group * z.per + inner, q, rows, :] = value[:, inner * F : (inner + 1) * F]
-            copy = pltpu.make_async_copy(out_ref.at[:, q, rows, :], out_hbm.at[:, q, rows, :], sems.at[q, k])
-            copy.start()
-            copies.append(copy)
+            place_fields(z, q, k, flat_ref, dense_ref, resid_patch_ref.at[q])
+            write(q, k, resid_patch_ref.at[q], factor_ref.at[q])
     for copy in copies:
         copy.wait()
 
@@ -531,14 +567,22 @@
     )
     far, near, late, patch = lax.optimization_barrier((far, near, late, patch))
     last = exchange(z, far, swap_col)
-    (total,) = vmem_call(functools.partial(merge_kernel, z), [tiles], [], total, near, far, late)
     (pooled,) = vmem_call(
         functools.partial(pool_kernel, z),
         [((z.rd, z.cd, B, z.F), f32)],
         [((z.cd + 4, B, z.F), f32), ((z.rd + 2, z.cd + 2, B, z.F), f32)],
         hidden, tall, near, far,
     )
-    return jnp.swapaxes(gradient(z, total, last, window, patch, hidden, pooled, wide_first, wide), 2, 3)
+    total, early_patch, early_factor = vmem_call(
+        functools.partial(merge_kernel, z),
+        [tiles, ((z.groups, K, 128), bf16), ((z.groups, 256, z.per * z.F), bf16)],
+        [((z.T, B, L), bf16), ((z.groups, z.KW, 128), f32), ((K, 128), f32)],
+        total, near, far, late, window, hidden, pooled, wide_first, wide,
+    )
+    out = gradient(
+        z, total, last, window, patch, hidden, pooled, wide_first, wide, early_patch, early_factor
+    )
+    return jnp.swapaxes(out, 2, 3)
 
 
 def solution(mesh):

time: 40.6 us -> 40 us (0.985)
    pallas_call x1, Pallas kernels: 4.04 us -> 3.45 us  [gradient(): pl.pallas_call(functools.partial(grad_kernel, z), out_shape=pltpu.HBM((z....]
  transfers between devices with their start and end apart: 7 -> 7, of which waited for: 4 -> 4; matrix products, arithmetic and copies ran while one was open for 0% -> 0% of each run, Pallas kernels for 9% -> 10%
where the time goes in v6:
time: 40 us; the launch traced here: 39.7 us
  waiting for transfers between devices  14.1 us (35%)
  Pallas kernels  13.1 us (33%)
  starting transfers between devices  10.5 us (26%)
  local copies, waits for them, and re-layouts  2.04 us (5%)
    all_to_all x1, starting transfers between devices, body(): lax.all_to_all(blocks.reshape(z.R * z.C, z.bd * z.T, L), ('row', 'col'),...  7.3 us
    ppermute x5, waiting for transfers between devices, exchange(): return lax.ppermute(value, ('row', 'col'), pairs)  5.54 us
    ppermute x1, waiting for transfers between devices, shift(): return lax.ppermute(value, ('row', 'col'), pairs)  4.32 us
    all_to_all x1, waiting for transfers between devices, body(): lax.all_to_all(blocks.reshape(z.R * z.C, z.bd * z.T, L), ('row', 'col'),...  4.25 us
    pallas_call x1, Pallas kernels, gradient(): pl.pallas_call(functools.partial(grad_kernel, z), out_shape=pltpu.HBM((z....  3.45 us
    pallas_call x1, Pallas kernels, encode(): pl.pallas_call(functools.partial(encode_kernel, z), out_shape=[pltpu.VMEM...  3.3 us
    ppermute x5, starting transfers between devices, exchange(): return lax.ppermute(value, ('row', 'col'), pairs)  3.16 us
    pallas_call x2, Pallas kernels, spread_weights(): pl.pallas_call(functools.partial(spread_kernel, z), grid=(count,), out_sh...  2.58 us
  transfers between devices with their start and end apart: 7, of which 4 were waited for; matrix products, arithmetic and copies ran while one was open for 0% of the time, Pallas kernels for 10%

profile of v6, /device:TPU:0, one launch (start us, length us, event | category | flops | bytes accessed | tf_op | source)
XLA Modules:
  0.0 39.7 jit_solution(852150755296849185)
XLA Ops:
  0.0 1.9 %shard_map.28 = bf16[4,192,128]{2,1,0:T(8,128)(2,1)} custom-call(bf16[1,3,64,96]{3,2,1,0:T(8,128)(2,1)} %images_hbm.1), custom_call_target="tpu_custom_call" | custom-call | tf_op jit(solution)/shard_map/pallas_call | solution.py:117
  1.9 7.3 %all-to-all-start = ((bf16[32,24,128]{2,1,0:T(8,128)(2,1)}), bf16[32,24,128]{2,1,0:T(8,128)(2,1)S(1)}, u32[]{:S(2)}, u32[]{:S(2)}) async-start(bf16[32,24,128]{2,1,0:T(8,128)(2,1)} %bitcast.5), calls=%async_computation | async-start | bytes 393216 | tf_op jit(solution)/shard_map/all_to_all | solution.py:544
  9.3 0.0 copy-start
  9.3 2.0 %copy-done = bf16[4,3,128,1200]{2,3,1,0:T(8,128)(2,1)S(1)} copy-done((bf16[4,3,128,1200]{2,3,1,0:T(8,128)(2,1)S(1)}, bf16[4,3,128,1200]{2,3,1,0:T(8,128)(2,1)}, u32[]{:S(2)}) %copy-start) | copy-done | bytes 3686424
  11.3 0.6 %shard_map.29.first_ref = bf16[2,1920,384]{2,1,0:T(8,128)(2,1)S(1)} custom-call(bf16[4,3,1200,128]{3,2,1,0:T(8,128)(2,1)S(1)} %bitcast.3), custom_call_target="tpu_custom_call" | custom-call | tf_op jit(solution)/shard_map/pallas_call | solution.py:147
  12.0 1.9 %shard_map.30.wide_hbm = bf16[2,1920,384]{2,1,0:T(8,128)(2,1)} custom-call(bf16[4,3,1200,128]{3,2,1,0:T(8,128)(2,1)S(1)} %bitcast.4), custom_call_target="tpu_custom_call" | custom-call | tf_op jit(solution)/shard_map/pallas_call | solution.py:147
  13.9 4.2 %all-to-all-done.moved_ref = bf16[32,24,128]{2,1,0:T(8,128)(2,1)S(1)} async-done(((bf16[32,24,128]{2,1,0:T(8,128)(2,1)}), bf16[32,24,128]{2,1,0:T(8,128)(2,1)S(1)}, u32[]{:S(2)}, u32[]{:S(2)}) %all-to-all-start) | async-done | bytes 196640 | tf_op jit(solution)/shard_map/all_to_all | solution.py:544
  18.1 3.3 %shard_map.31 = (bf16[24,32,128]{2,1,0:T(8,128)(2,1)S(1)}, bf16[4,3,32,128]{3,2,1,0:T(8,128)(2,1)S(1)}, f32[24,32,128]{2,1,0:T(8,128)S(1)}, bf16[18,32,128]{2,1,...) custom-call(bf16[32,24,128]{2,1,0:T(8,128)(2,1)S(1)} %all-to-all-done.moved_ref, ...), custom_call_target="tpu_custom_call" | custom-call | tf_op jit(solution)/shard_map/pallas_call | solution.py:217
  21.4 1.1 %collective-permute-start = (bf16[18,32,128]{2,1,0:T(8,128)(2,1)S(1)}, bf16[18,32,128]{2,1,0:T(8,128)(2,1)S(1)}, u32[]{:S(2)}, u32[]{:S(2)}) collective-permute-start(bf16[18,32,128]{2,1,0:T(8,128)(2,1)S(1)} %get-tuple-element.25), channel_id=1, source_target_pairs={{0,8},{1,9},{2,10},{3,11},{4,12},{5,13},{6,14},{7,15},{8,0},{9,1},... | collective-permute-start | bytes 442376 | tf_op jit(solution)/shard_map/ppermute | solution.py:514
  22.5 0.0 collective-permute-start.1
  22.5 5.3 %collective-permute-done.swap_ref = bf16[18,32,128]{2,1,0:T(8,128)(2,1)S(1)} collective-permute-done((bf16[18,32,128]{2,1,0:T(8,128)(2,1)S(1)}, bf16[18,32,128]{2,1,0:T(8,128)(2,1)S(1)}, u32[]{:S(2)}, u32[]{:S(2)}) %collective-permute-start) | collective-permute-done | bytes 147488 | tf_op jit(solution)/shard_map/ppermute | solution.py:514
  27.9 0.0 collective-permute-done.1.cross_ref
  27.9 0.4 %shard_map.32 = (f32[24,32,128]{2,1,0:T(8,128)S(1)}, f32[6,3,32,128]{3,2,1,0:T(8,128)S(1)}, bf16[24,32,128]{2,1,0:T(8,128)(2,1)S(1)}, bf16[24,32,128]{2,1,0:T(8,128)(2,1)S(1)}, bf16[3,32,128]{2,1,0:T(8,128)(2,1)S(1)}) custom-call(f32[24,32,128]{2,1,0:T(8,128)S(1)} %get-tuple-element.23.contrib_ref, bf16[4,3,32,128]{3,2,1,0:T(8,128)(2,1)S(1)} %get-tuple-element.24.hidden_ref, ...), custom_call_target="tpu_custom_call" | custom-call | tf_op jit(solution)/shard_map/pallas_call | solution.py:283
  28.3 1.8 %collective-permute-start.2 = (bf16[24,32,128]{2,1,0:T(8,128)(2,1)S(1)}, bf16[24,32,128]{2,1,0:T(8,128)(2,1)S(1)}, u32[]{:S(2)}, u32[]{:S(2)}) collective-permute-start(bf16[24,32,128]{2,1,0:T(8,128)(2,1)S(1)} %get-tuple-element.28), channel_id=1, source_target_pairs={{0,8},{1,2},{2,1},{3,4},{4,3},{5,6},{6,5},{7,15},{8,0},{9,10},{10,... | collective-permute-start | bytes 589832 | tf_op jit(solution)/shard_map/ppermute | solution.py:514
  30.1 0.0 collective-permute-start.3
  30.1 0.0 collective-permute-start.4
  30.1 0.4 %shard_map.33.patch_ref = bf16[3,1,1200,128]{3,2,1,0:T(8,128)(2,1)S(1)} custom-call(bf16[24,32,128]{2,1,0:T(8,128)(2,1)S(1)} %get-tuple-element.31.window_ref), custom_call_target="tpu_custom_call" | custom-call | tf_op jit(solution)/shard_map/pallas_call | solution.py:283
  30.5 4.3 %collective-permute-done.4.late_ref = bf16[3,32,128]{2,1,0:T(8,128)(2,1)S(1)} collective-permute-done((bf16[3,32,128]{2,1,0:T(8,128)(2,1)S(1)}, bf16[3,32,128]{2,1,0:T(8,128)(2,1)S(1)}, u32[]{:S(2)}, u32[]{:S(2)}) %collective-permute-start.4) | collective-permute-done | bytes 24608 | tf_op jit(solution)/shard_map/ppermute | solution.py:523
  34.8 0.0 collective-permute-done.2.far_ref
  34.8 0.0 collective-permute-done.3.near_ref
  34.8 0.3 collective-permute-start.5
  35.1 0.4 shard_map.34.pooled_ref
  35.5 0.6 %shard_map.35 = (f32[24,32,128]{2,1,0:T(8,128)S(1)}, bf16[1,1200,128]{2,1,0:T(8,128)(2,1)S(1)}, bf16[1,256,512]{2,1,0:T(8,128)(2,1)S(1)}) custom-call(f32[24,32,128]{2,1,0:T(8,128)S(1)} %get-tuple-element.27.sum_ref, bf16[24,32,128]{2,1,0:T(8,128)(2,1)S(1)} %collective-permute-done.3.near_ref, bf16[24,32,128]{2,1,0:T(8,128)(2,1)S(1)} %collective-permute-done.2.far_ref, ...), custom_call_target="tpu_custom_call" | custom-call | tf_op jit(solution)/shard_map/pallas_call | solution.py:283
  36.1 0.2 collective-permute-done.5.last_ref
  36.3 3.5 %shard_map.36 = f32[4,3,1200,128]{3,2,1,0:T(8,128)} custom-call(f32[24,32,128]{2,1,0:T(8,128)S(1)} %get-tuple-element.37.sum_ref, bf16[24,32,128]{2,1,0:T(8,128)(2,1)S(1)} %collective-permute-done.5.last_ref, bf16[24,32,128]{2,1,0:T(8,128)(2,1)S(1)} %get-tuple-element.31.window_ref, bf16[3,1,1200,128]{3,2,1,0:T(8,128)(2,1)S(1)} %shard_map.33.patch_ref, ...), custom_call_target="tpu_custom_call" | custom-call | tf_op jit(solution)/shard_map/pallas_call | solution.py:490
Async XLA Ops:
  1.9 16.2 %all-to-all-start = ((bf16[32,24,128]{2,1,0:T(8,128)(2,1)}), bf16[32,24,128]{2,1,0:T(8,128)(2,1)S(1)}, u32[]{:S(2)}, u32[]{:S(2)}) async-start(bf16[32,24,128]{2,1,0:T(8,128)(2,1)} %bitcast.5), calls=%async_computation | async-start | bytes 393216 | tf_op jit(solution)/shard_map/all_to_all | solution.py:544
  9.3 2.0 %copy-start = (bf16[4,3,128,1200]{2,3,1,0:T(8,128)(2,1)S(1)}, bf16[4,3,128,1200]{2,3,1,0:T(8,128)(2,1)}, u32[]{:S(2)}) copy-start(bf16[4,3,128,1200]{2,3,1,0:T(8,128)(2,1)} %param.3) | copy-start | bytes 11059204
  21.4 6.4 %collective-permute-start = (bf16[18,32,128]{2,1,0:T(8,128)(2,1)S(1)}, bf16[18,32,128]{2,1,0:T(8,128)(2,1)S(1)}, u32[]{:S(2)}, u32[]{:S(2)}) collective-permute-start(bf16[18,32,128]{2,1,0:T(8,128)(2,1)S(1)} %get-tuple-element.25), channel_id=1, source_target_pairs={{0,8},{1,9},{2,10},{3,11},{4,12},{5,13},{6,14},{7,15},{8,0},{9,1},... | collective-permute-start | bytes 442376 | tf_op jit(solution)/shard_map/ppermute | solution.py:514
  22.5 5.3 %collective-permute-start.1 = (bf16[18,32,128]{2,1,0:T(8,128)(2,1)S(1)}, bf16[18,32,128]{2,1,0:T(8,128)(2,1)S(1)}, u32[]{:S(2)}, u32[]{:S(2)}) collective-permute-start(bf16[18,32,128]{2,1,0:T(8,128)(2,1)S(1)} %get-tuple-element.26), channel_id=1, source_target_pairs={{0,1},{1,0},{2,3},{3,2},{4,5},{5,4},{6,7},{7,6},{8,16},{9,17},{10,... | collective-permute-start | bytes 442376 | tf_op jit(solution)/shard_map/ppermute | solution.py:514
  28.3 6.5 %collective-permute-start.2 = (bf16[24,32,128]{2,1,0:T(8,128)(2,1)S(1)}, bf16[24,32,128]{2,1,0:T(8,128)(2,1)S(1)}, u32[]{:S(2)}, u32[]{:S(2)}) collective-permute-start(bf16[24,32,128]{2,1,0:T(8,128)(2,1)S(1)} %get-tuple-element.28), channel_id=1, source_target_pairs={{0,8},{1,2},{2,1},{3,4},{4,3},{5,6},{6,5},{7,15},{8,0},{9,10},{10,... | collective-permute-start | bytes 589832 | tf_op jit(solution)/shard_map/ppermute | solution.py:514
  30.1 4.7 %collective-permute-start.3 = (bf16[24,32,128]{2,1,0:T(8,128)(2,1)S(1)}, bf16[24,32,128]{2,1,0:T(8,128)(2,1)S(1)}, u32[]{:S(2)}, u32[]{:S(2)}) collective-permute-start(bf16[24,32,128]{2,1,0:T(8,128)(2,1)S(1)} %get-tuple-element.29), channel_id=1, source_target_pairs={{0,1},{1,0},{2,3},{3,2},{4,5},{5,4},{6,7},{7,6},{8,9},{9,8},{10,11... | collective-permute-start | bytes 589832 | tf_op jit(solution)/shard_map/ppermute | solution.py:514
  30.1 4.7 %collective-permute-start.4 = (bf16[3,32,128]{2,1,0:T(8,128)(2,1)S(1)}, bf16[3,32,128]{2,1,0:T(8,128)(2,1)S(1)}, u32[]{:S(2)}, u32[]{:S(2)}) collective-permute-start(bf16[3,32,128]{2,1,0:T(8,128)(2,1)S(1)} %get-tuple-element.30), channel_id=1, source_target_pairs={{0,2},{1,7},{2,4},{3,1},{4,6},{5,3},{6,0},{7,5},{8,10},{9,15},{10,... | collective-permute-start | bytes 73736 | tf_op jit(solution)/shard_map/ppermute | solution.py:523
  34.8 1.4 %collective-permute-start.5 = (bf16[24,32,128]{2,1,0:T(8,128)(2,1)S(1)}, bf16[24,32,128]{2,1,0:T(8,128)(2,1)S(1)}, u32[]{:S(2)}, u32[]{:S(2)}) collective-permute-start(bf16[24,32,128]{2,1,0:T(8,128)(2,1)S(1)} %collective-permute-done.2.far_ref), channel_id=1, source_target_pairs={{0,1},{1,0},{2,3},{3,2},{4,5},{5,4},{6,7},{7,6},{8,9},{9,8},{10,11... | collective-permute-start | bytes 589832 | tf_op jit(solution)/shard_map/ppermute | solution.py:514

commit v7 on v6

--- a/solution.py
+++ b/solution.py
@@ -566,7 +566,7 @@
         window,
     )
     far, near, late, patch = lax.optimization_barrier((far, near, late, patch))
-    last = exchange(z, far, swap_col)
+    last = exchange(z, far[: z.T // 2], swap_col)
     (pooled,) = vmem_call(
         functools.partial(pool_kernel, z),
         [((z.rd, z.cd, B, z.F), f32)],

time: 40 us -> 40 us (level)
  no operation moved by 1% of the time
where the time goes in v7:
time: 40 us; the launch traced here: 39.7 us
  waiting for transfers between devices  14 us (35%)
  Pallas kernels  13 us (32%)
  starting transfers between devices  10.5 us (26%)
  local copies, waits for them, and re-layouts  2.05 us (5%)
    all_to_all x1, starting transfers between devices, body(): lax.all_to_all(blocks.reshape(z.R * z.C, z.bd * z.T, L), ('row', 'col'),...  7.3 us
    ppermute x5, waiting for transfers between devices, exchange(): return lax.ppermute(value, ('row', 'col'), pairs)  5.39 us
    ppermute x1, waiting for transfers between devices, shift(): return lax.ppermute(value, ('row', 'col'), pairs)  4.32 us
    all_to_all x1, waiting for transfers between devices, body(): lax.all_to_all(blocks.reshape(z.R * z.C, z.bd * z.T, L), ('row', 'col'),...  4.25 us
    pallas_call x1, Pallas kernels, gradient(): pl.pallas_call(functools.partial(grad_kernel, z), out_shape=pltpu.HBM((z....  3.45 us
    pallas_call x1, Pallas kernels, encode(): pl.pallas_call(functools.partial(encode_kernel, z), out_shape=[pltpu.VMEM...  3.3 us
    ppermute x5, starting transfers between devices, exchange(): return lax.ppermute(value, ('row', 'col'), pairs)  3.22 us
    pallas_call x2, Pallas kernels, spread_weights(): pl.pallas_call(functools.partial(spread_kernel, z), grid=(count,), out_sh...  2.58 us
  transfers between devices with their start and end apart: 7, of which 4 were waited for; matrix products, arithmetic and copies ran while one was open for 0% of the time, Pallas kernels for 10%

profile of v7, /device:TPU:0, one launch (start us, length us, event | category | flops | bytes accessed | tf_op | source)
XLA Modules:
  0.0 39.7 jit_solution(16565962930243662742)
XLA Ops:
  0.0 1.9 %shard_map.28 = bf16[4,192,128]{2,1,0:T(8,128)(2,1)} custom-call(bf16[1,3,64,96]{3,2,1,0:T(8,128)(2,1)} %images_hbm.1), custom_call_target="tpu_custom_call" | custom-call | tf_op jit(solution)/shard_map/pallas_call | solution.py:117
  1.9 7.3 %all-to-all-start = ((bf16[32,24,128]{2,1,0:T(8,128)(2,1)}), bf16[32,24,128]{2,1,0:T(8,128)(2,1)S(1)}, u32[]{:S(2)}, u32[]{:S(2)}) async-start(bf16[32,24,128]{2,1,0:T(8,128)(2,1)} %bitcast.5), calls=%async_computation | async-start | bytes 393216 | tf_op jit(solution)/shard_map/all_to_all | solution.py:544
  9.3 0.0 copy-start
  9.3 2.0 %copy-done = bf16[4,3,128,1200]{2,3,1,0:T(8,128)(2,1)S(1)} copy-done((bf16[4,3,128,1200]{2,3,1,0:T(8,128)(2,1)S(1)}, bf16[4,3,128,1200]{2,3,1,0:T(8,128)(2,1)}, u32[]{:S(2)}) %copy-start) | copy-done | bytes 3686424
  11.3 0.6 %shard_map.29.first_ref = bf16[2,1920,384]{2,1,0:T(8,128)(2,1)S(1)} custom-call(bf16[4,3,1200,128]{3,2,1,0:T(8,128)(2,1)S(1)} %bitcast.3), custom_call_target="tpu_custom_call" | custom-call | tf_op jit(solution)/shard_map/pallas_call | solution.py:147
  12.0 1.9 %shard_map.30.wide_hbm = bf16[2,1920,384]{2,1,0:T(8,128)(2,1)} custom-call(bf16[4,3,1200,128]{3,2,1,0:T(8,128)(2,1)S(1)} %bitcast.4), custom_call_target="tpu_custom_call" | custom-call | tf_op jit(solution)/shard_map/pallas_call | solution.py:147
  13.9 4.2 %all-to-all-done.moved_ref = bf16[32,24,128]{2,1,0:T(8,128)(2,1)S(1)} async-done(((bf16[32,24,128]{2,1,0:T(8,128)(2,1)}), bf16[32,24,128]{2,1,0:T(8,128)(2,1)S(1)}, u32[]{:S(2)}, u32[]{:S(2)}) %all-to-all-start) | async-done | bytes 196640 | tf_op jit(solution)/shard_map/all_to_all | solution.py:544
  18.1 3.3 %shard_map.31 = (bf16[24,32,128]{2,1,0:T(8,128)(2,1)S(1)}, bf16[4,3,32,128]{3,2,1,0:T(8,128)(2,1)S(1)}, f32[24,32,128]{2,1,0:T(8,128)S(1)}, bf16[18,32,128]{2,1,...) custom-call(bf16[32,24,128]{2,1,0:T(8,128)(2,1)S(1)} %all-to-all-done.moved_ref, ...), custom_call_target="tpu_custom_call" | custom-call | tf_op jit(solution)/shard_map/pallas_call | solution.py:217
  21.4 1.1 %collective-permute-start = (bf16[18,32,128]{2,1,0:T(8,128)(2,1)S(1)}, bf16[18,32,128]{2,1,0:T(8,128)(2,1)S(1)}, u32[]{:S(2)}, u32[]{:S(2)}) collective-permute-start(bf16[18,32,128]{2,1,0:T(8,128)(2,1)S(1)} %get-tuple-element.25), channel_id=1, source_target_pairs={{0,8},{1,9},{2,10},{3,11},{4,12},{5,13},{6,14},{7,15},{8,0},{9,1},... | collective-permute-start | bytes 442376 | tf_op jit(solution)/shard_map/ppermute | solution.py:514
  22.5 0.0 collective-permute-start.1
  22.5 5.3 %collective-permute-done.swap_ref = bf16[18,32,128]{2,1,0:T(8,128)(2,1)S(1)} collective-permute-done((bf16[18,32,128]{2,1,0:T(8,128)(2,1)S(1)}, bf16[18,32,128]{2,1,0:T(8,128)(2,1)S(1)}, u32[]{:S(2)}, u32[]{:S(2)}) %collective-permute-start) | collective-permute-done | bytes 147488 | tf_op jit(solution)/shard_map/ppermute | solution.py:514
  27.9 0.0 collective-permute-done.1.cross_ref
  27.9 0.4 %shard_map.32 = (f32[24,32,128]{2,1,0:T(8,128)S(1)}, f32[6,3,32,128]{3,2,1,0:T(8,128)S(1)}, bf16[24,32,128]{2,1,0:T(8,128)(2,1)S(1)}, bf16[24,32,128]{2,1,0:T(8,128)(2,1)S(1)}, bf16[3,32,128]{2,1,0:T(8,128)(2,1)S(1)}) custom-call(f32[24,32,128]{2,1,0:T(8,128)S(1)} %get-tuple-element.23.contrib_ref, bf16[4,3,32,128]{3,2,1,0:T(8,128)(2,1)S(1)} %get-tuple-element.24.hidden_ref, ...), custom_call_target="tpu_custom_call" | custom-call | tf_op jit(solution)/shard_map/pallas_call | solution.py:283
  28.3 1.8 %collective-permute-start.2 = (bf16[24,32,128]{2,1,0:T(8,128)(2,1)S(1)}, bf16[24,32,128]{2,1,0:T(8,128)(2,1)S(1)}, u32[]{:S(2)}, u32[]{:S(2)}) collective-permute-start(bf16[24,32,128]{2,1,0:T(8,128)(2,1)S(1)} %get-tuple-element.28), channel_id=1, source_target_pairs={{0,8},{1,2},{2,1},{3,4},{4,3},{5,6},{6,5},{7,15},{8,0},{9,10},{10,... | collective-permute-start | bytes 589832 | tf_op jit(solution)/shard_map/ppermute | solution.py:514
  30.1 0.0 collective-permute-start.3
  30.1 0.0 collective-permute-start.4
  30.1 0.4 %shard_map.33.patch_ref = bf16[3,1,1200,128]{3,2,1,0:T(8,128)(2,1)S(1)} custom-call(bf16[24,32,128]{2,1,0:T(8,128)(2,1)S(1)} %get-tuple-element.31.window_ref), custom_call_target="tpu_custom_call" | custom-call | tf_op jit(solution)/shard_map/pallas_call | solution.py:283
  30.5 4.3 %collective-permute-done.4.late_ref = bf16[3,32,128]{2,1,0:T(8,128)(2,1)S(1)} collective-permute-done((bf16[3,32,128]{2,1,0:T(8,128)(2,1)S(1)}, bf16[3,32,128]{2,1,0:T(8,128)(2,1)S(1)}, u32[]{:S(2)}, u32[]{:S(2)}) %collective-permute-start.4) | collective-permute-done | bytes 24608 | tf_op jit(solution)/shard_map/ppermute | solution.py:523
  34.8 0.0 collective-permute-done.2.far_ref
  34.8 0.0 collective-permute-done.3.near_ref
  34.8 0.3 collective-permute-start.5
  35.2 0.4 shard_map.34.pooled_ref
  35.5 0.6 %shard_map.35 = (f32[24,32,128]{2,1,0:T(8,128)S(1)}, bf16[1,1200,128]{2,1,0:T(8,128)(2,1)S(1)}, bf16[1,256,512]{2,1,0:T(8,128)(2,1)S(1)}) custom-call(f32[24,32,128]{2,1,0:T(8,128)S(1)} %get-tuple-element.27.sum_ref, bf16[24,32,128]{2,1,0:T(8,128)(2,1)S(1)} %collective-permute-done.3.near_ref, bf16[24,32,128]{2,1,0:T(8,128)(2,1)S(1)} %collective-permute-done.2.far_ref, ...), custom_call_target="tpu_custom_call" | custom-call | tf_op jit(solution)/shard_map/pallas_call | solution.py:283
  36.1 0.1 collective-permute-done.5.last_ref
  36.2 3.5 %shard_map.36 = f32[4,3,1200,128]{3,2,1,0:T(8,128)} custom-call(f32[24,32,128]{2,1,0:T(8,128)S(1)} %get-tuple-element.37.sum_ref, bf16[12,32,128]{2,1,0:T(8,128)(2,1)S(1)} %collective-permute-done.5.last_ref, bf16[24,32,128]{2,1,0:T(8,128)(2,1)S(1)} %get-tuple-element.31.window_ref, bf16[3,1,1200,128]{3,2,1,0:T(8,128)(2,1)S(1)} %shard_map.33.patch_ref, ...), custom_call_target="tpu_custom_call" | custom-call | tf_op jit(solution)/shard_map/pallas_call | solution.py:490
  (1 shorter events, 0.0 us)
Async XLA Ops:
  1.9 16.2 %all-to-all-start = ((bf16[32,24,128]{2,1,0:T(8,128)(2,1)}), bf16[32,24,128]{2,1,0:T(8,128)(2,1)S(1)}, u32[]{:S(2)}, u32[]{:S(2)}) async-start(bf16[32,24,128]{2,1,0:T(8,128)(2,1)} %bitcast.5), calls=%async_computation | async-start | bytes 393216 | tf_op jit(solution)/shard_map/all_to_all | solution.py:544
  9.3 2.0 %copy-start = (bf16[4,3,128,1200]{2,3,1,0:T(8,128)(2,1)S(1)}, bf16[4,3,128,1200]{2,3,1,0:T(8,128)(2,1)}, u32[]{:S(2)}) copy-start(bf16[4,3,128,1200]{2,3,1,0:T(8,128)(2,1)} %param.3) | copy-start | bytes 11059204
  21.4 6.4 %collective-permute-start = (bf16[18,32,128]{2,1,0:T(8,128)(2,1)S(1)}, bf16[18,32,128]{2,1,0:T(8,128)(2,1)S(1)}, u32[]{:S(2)}, u32[]{:S(2)}) collective-permute-start(bf16[18,32,128]{2,1,0:T(8,128)(2,1)S(1)} %get-tuple-element.25), channel_id=1, source_target_pairs={{0,8},{1,9},{2,10},{3,11},{4,12},{5,13},{6,14},{7,15},{8,0},{9,1},... | collective-permute-start | bytes 442376 | tf_op jit(solution)/shard_map/ppermute | solution.py:514
  22.5 5.3 %collective-permute-start.1 = (bf16[18,32,128]{2,1,0:T(8,128)(2,1)S(1)}, bf16[18,32,128]{2,1,0:T(8,128)(2,1)S(1)}, u32[]{:S(2)}, u32[]{:S(2)}) collective-permute-start(bf16[18,32,128]{2,1,0:T(8,128)(2,1)S(1)} %get-tuple-element.26), channel_id=1, source_target_pairs={{0,1},{1,0},{2,3},{3,2},{4,5},{5,4},{6,7},{7,6},{8,16},{9,17},{10,... | collective-permute-start | bytes 442376 | tf_op jit(solution)/shard_map/ppermute | solution.py:514
  28.3 6.5 %collective-permute-start.2 = (bf16[24,32,128]{2,1,0:T(8,128)(2,1)S(1)}, bf16[24,32,128]{2,1,0:T(8,128)(2,1)S(1)}, u32[]{:S(2)}, u32[]{:S(2)}) collective-permute-start(bf16[24,32,128]{2,1,0:T(8,128)(2,1)S(1)} %get-tuple-element.28), channel_id=1, source_target_pairs={{0,8},{1,2},{2,1},{3,4},{4,3},{5,6},{6,5},{7,15},{8,0},{9,10},{10,... | collective-permute-start | bytes 589832 | tf_op jit(solution)/shard_map/ppermute | solution.py:514
  30.1 4.7 %collective-permute-start.3 = (bf16[24,32,128]{2,1,0:T(8,128)(2,1)S(1)}, bf16[24,32,128]{2,1,0:T(8,128)(2,1)S(1)}, u32[]{:S(2)}, u32[]{:S(2)}) collective-permute-start(bf16[24,32,128]{2,1,0:T(8,128)(2,1)S(1)} %get-tuple-element.29), channel_id=1, source_target_pairs={{0,1},{1,0},{2,3},{3,2},{4,5},{5,4},{6,7},{7,6},{8,9},{9,8},{10,11... | collective-permute-start | bytes 589832 | tf_op jit(solution)/shard_map/ppermute | solution.py:514
  30.1 4.7 %collective-permute-start.4 = (bf16[3,32,128]{2,1,0:T(8,128)(2,1)S(1)}, bf16[3,32,128]{2,1,0:T(8,128)(2,1)S(1)}, u32[]{:S(2)}, u32[]{:S(2)}) collective-permute-start(bf16[3,32,128]{2,1,0:T(8,128)(2,1)S(1)} %get-tuple-element.30), channel_id=1, source_target_pairs={{0,2},{1,7},{2,4},{3,1},{4,6},{5,3},{6,0},{7,5},{8,10},{9,15},{10,... | collective-permute-start | bytes 73736 | tf_op jit(solution)/shard_map/ppermute | solution.py:523
  34.8 1.4 %collective-permute-start.5 = (bf16[12,32,128]{2,1,0:T(8,128)(2,1)S(1)}, bf16[12,32,128]{2,1,0:T(8,128)(2,1)S(1)}, u32[]{:S(2)}, u32[]{:S(2)}) collective-permute-start(bf16[12,32,128]{2,1,0:T(8,128)(2,1)S(1)} %slice.3), channel_id=1, source_target_pairs={{0,1},{1,0},{2,3},{3,2},{4,5},{5,4},{6,7},{7,6},{8,9},{9,8},{10,11... | collective-permute-start | bytes 294920 | tf_op jit(solution)/shard_map/ppermute | solution.py:514

commit v8 on v7

--- a/solution.py
+++ b/solution.py
@@ -51,7 +51,7 @@
         self.groups = self.rd // self.per
         assert self.late > 0 and self.stride % self.late == 0 and self.T % (self.stride // self.late) == 0
         assert self.B * self.per == 128 and self.groups * self.per == self.rd and self.F == 128
-        assert self.C % 2 == 0 and self.R % 2 == 0 and self.rd >= 4 and self.cd >= 2 and self.lanes == 128
+        assert self.C % 2 == 0 and self.R % 2 == 0 and self.YB % 2 == 0 and self.rd >= 4 and self.cd >= 2 and self.lanes == 128
         assert self.height == self.R * self.h and self.width == self.C * self.w
 
 
@@ -338,7 +338,6 @@
     z, contrib_ref, hidden_ref, swap_ref, cross_ref, sum_ref, tall_ref, near_ref, far_ref, late_ref
 ):
     half = z.YB // 2
-    sum_ref[...] = contrib_ref[...]
     row = lax.axis_index("row")
     even_row = row_is_even()
     above_exists, below_exists = row > 0, row < z.R - 1
@@ -347,7 +346,8 @@
         first = jnp.where(below, z.YB - half, 0)
         for c in range(CH):
             for y in range(half):
-                sum_ref[c * z.YB + first + y] += jnp.where(exists, ref[c * half + y].astype(f32), 0.0)
+                t = c * z.YB + first + y
+                sum_ref[t] = contrib_ref[t] + jnp.where(exists, ref[c * half + y].astype(f32), 0.0)
     even = is_even()
     odd = jnp.logical_not(even)
     for t in range(0, z.T, 2):

time: 40 us -> 39.9 us (level)
  no operation moved by 1% of the time
where the time goes in v8:
time: 39.9 us; the launch traced here: 39.6 us
  waiting for transfers between devices  14 us (35%)
  Pallas kernels  13 us (33%)
  starting transfers between devices  10.5 us (26%)
  local copies, waits for them, and re-layouts  2.05 us (5%)
    all_to_all x1, starting transfers between devices, body(): lax.all_to_all(blocks.reshape(z.R * z.C, z.bd * z.T, L), ('row', 'col'),...  7.3 us
    ppermute x5, waiting for transfers between devices, exchange(): return lax.ppermute(value, ('row', 'col'), pairs)  5.39 us
    ppermute x1, waiting for transfers between devices, shift(): return lax.ppermute(value, ('row', 'col'), pairs)  4.32 us
    all_to_all x1, waiting for transfers between devices, body(): lax.all_to_all(blocks.reshape(z.R * z.C, z.bd * z.T, L), ('row', 'col'),...  4.25 us
    pallas_call x1, Pallas kernels, gradient(): pl.pallas_call(functools.partial(grad_kernel, z), out_shape=pltpu.HBM((z....  3.45 us
    pallas_call x1, Pallas kernels, encode(): pl.pallas_call(functools.partial(encode_kernel, z), out_shape=[pltpu.VMEM...  3.3 us
    ppermute x5, starting transfers between devices, exchange(): return lax.ppermute(value, ('row', 'col'), pairs)  3.22 us
    pallas_call x2, Pallas kernels, spread_weights(): pl.pallas_call(functools.partial(spread_kernel, z), grid=(count,), out_sh...  2.58 us
  transfers between devices with their start and end apart: 7, of which 4 were waited for; matrix products, arithmetic and copies ran while one was open for 0% of the time, Pallas kernels for 10%

profile of v8, /device:TPU:0, one launch (start us, length us, event | category | flops | bytes accessed | tf_op | source)
XLA Modules:
  0.0 39.6 jit_solution(2404796604064841754)
XLA Ops:
  0.0 1.9 %shard_map.28 = bf16[4,192,128]{2,1,0:T(8,128)(2,1)} custom-call(bf16[1,3,64,96]{3,2,1,0:T(8,128)(2,1)} %images_hbm.1), custom_call_target="tpu_custom_call" | custom-call | tf_op jit(solution)/shard_map/pallas_call | solution.py:117
  1.9 7.3 %all-to-all-start = ((bf16[32,24,128]{2,1,0:T(8,128)(2,1)}), bf16[32,24,128]{2,1,0:T(8,128)(2,1)S(1)}, u32[]{:S(2)}, u32[]{:S(2)}) async-start(bf16[32,24,128]{2,1,0:T(8,128)(2,1)} %bitcast.5), calls=%async_computation | async-start | bytes 393216 | tf_op jit(solution)/shard_map/all_to_all | solution.py:544
  9.3 0.0 copy-start
  9.3 2.0 %copy-done = bf16[4,3,128,1200]{2,3,1,0:T(8,128)(2,1)S(1)} copy-done((bf16[4,3,128,1200]{2,3,1,0:T(8,128)(2,1)S(1)}, bf16[4,3,128,1200]{2,3,1,0:T(8,128)(2,1)}, u32[]{:S(2)}) %copy-start) | copy-done | bytes 3686424
  11.3 0.6 %shard_map.29.first_ref = bf16[2,1920,384]{2,1,0:T(8,128)(2,1)S(1)} custom-call(bf16[4,3,1200,128]{3,2,1,0:T(8,128)(2,1)S(1)} %bitcast.3), custom_call_target="tpu_custom_call" | custom-call | tf_op jit(solution)/shard_map/pallas_call | solution.py:147
  12.0 1.9 %shard_map.30.wide_hbm = bf16[2,1920,384]{2,1,0:T(8,128)(2,1)} custom-call(bf16[4,3,1200,128]{3,2,1,0:T(8,128)(2,1)S(1)} %bitcast.4), custom_call_target="tpu_custom_call" | custom-call | tf_op jit(solution)/shard_map/pallas_call | solution.py:147
  13.9 4.2 %all-to-all-done.moved_ref = bf16[32,24,128]{2,1,0:T(8,128)(2,1)S(1)} async-done(((bf16[32,24,128]{2,1,0:T(8,128)(2,1)}), bf16[32,24,128]{2,1,0:T(8,128)(2,1)S(1)}, u32[]{:S(2)}, u32[]{:S(2)}) %all-to-all-start) | async-done | bytes 196640 | tf_op jit(solution)/shard_map/all_to_all | solution.py:544
  18.1 3.3 %shard_map.31 = (bf16[24,32,128]{2,1,0:T(8,128)(2,1)S(1)}, bf16[4,3,32,128]{3,2,1,0:T(8,128)(2,1)S(1)}, f32[24,32,128]{2,1,0:T(8,128)S(1)}, bf16[18,32,128]{2,1,...) custom-call(bf16[32,24,128]{2,1,0:T(8,128)(2,1)S(1)} %all-to-all-done.moved_ref, ...), custom_call_target="tpu_custom_call" | custom-call | tf_op jit(solution)/shard_map/pallas_call | solution.py:217
  21.4 1.1 %collective-permute-start = (bf16[18,32,128]{2,1,0:T(8,128)(2,1)S(1)}, bf16[18,32,128]{2,1,0:T(8,128)(2,1)S(1)}, u32[]{:S(2)}, u32[]{:S(2)}) collective-permute-start(bf16[18,32,128]{2,1,0:T(8,128)(2,1)S(1)} %get-tuple-element.25), channel_id=1, source_target_pairs={{0,8},{1,9},{2,10},{3,11},{4,12},{5,13},{6,14},{7,15},{8,0},{9,1},... | collective-permute-start | bytes 442376 | tf_op jit(solution)/shard_map/ppermute | solution.py:514
  22.5 0.0 collective-permute-start.1
  22.5 5.3 %collective-permute-done.swap_ref = bf16[18,32,128]{2,1,0:T(8,128)(2,1)S(1)} collective-permute-done((bf16[18,32,128]{2,1,0:T(8,128)(2,1)S(1)}, bf16[18,32,128]{2,1,0:T(8,128)(2,1)S(1)}, u32[]{:S(2)}, u32[]{:S(2)}) %collective-permute-start) | collective-permute-done | bytes 147488 | tf_op jit(solution)/shard_map/ppermute | solution.py:514
  27.9 0.0 collective-permute-done.1.cross_ref
  27.9 0.4 shard_map.32
  28.2 1.8 %collective-permute-start.2 = (bf16[24,32,128]{2,1,0:T(8,128)(2,1)S(1)}, bf16[24,32,128]{2,1,0:T(8,128)(2,1)S(1)}, u32[]{:S(2)}, u32[]{:S(2)}) collective-permute-start(bf16[24,32,128]{2,1,0:T(8,128)(2,1)S(1)} %get-tuple-element.28), channel_id=1, source_target_pairs={{0,8},{1,2},{2,1},{3,4},{4,3},{5,6},{6,5},{7,15},{8,0},{9,10},{10,... | collective-permute-start | bytes 589832 | tf_op jit(solution)/shard_map/ppermute | solution.py:514
  30.0 0.0 collective-permute-start.3
  30.0 0.0 collective-permute-start.4
  30.1 0.4 %shard_map.33.patch_ref = bf16[3,1,1200,128]{3,2,1,0:T(8,128)(2,1)S(1)} custom-call(bf16[24,32,128]{2,1,0:T(8,128)(2,1)S(1)} %get-tuple-element.31.window_ref), custom_call_target="tpu_custom_call" | custom-call | tf_op jit(solution)/shard_map/pallas_call | solution.py:283
  30.5 4.3 %collective-permute-done.4.late_ref = bf16[3,32,128]{2,1,0:T(8,128)(2,1)S(1)} collective-permute-done((bf16[3,32,128]{2,1,0:T(8,128)(2,1)S(1)}, bf16[3,32,128]{2,1,0:T(8,128)(2,1)S(1)}, u32[]{:S(2)}, u32[]{:S(2)}) %collective-permute-start.4) | collective-permute-done | bytes 24608 | tf_op jit(solution)/shard_map/ppermute | solution.py:523
  34.8 0.0 collective-permute-done.2.far_ref
  34.8 0.0 collective-permute-done.3.near_ref
  34.8 0.3 collective-permute-start.5
  35.1 0.4 shard_map.34.pooled_ref
  35.5 0.6 %shard_map.35 = (f32[24,32,128]{2,1,0:T(8,128)S(1)}, bf16[1,1200,128]{2,1,0:T(8,128)(2,1)S(1)}, bf16[1,256,512]{2,1,0:T(8,128)(2,1)S(1)}) custom-call(f32[24,32,128]{2,1,0:T(8,128)S(1)} %get-tuple-element.27.sum_ref, bf16[24,32,128]{2,1,0:T(8,128)(2,1)S(1)} %collective-permute-done.3.near_ref, bf16[24,32,128]{2,1,0:T(8,128)(2,1)S(1)} %collective-permute-done.2.far_ref, ...), custom_call_target="tpu_custom_call" | custom-call | tf_op jit(solution)/shard_map/pallas_call | solution.py:283
  36.1 0.1 collective-permute-done.5.last_ref
  36.2 3.5 %shard_map.36 = f32[4,3,1200,128]{3,2,1,0:T(8,128)} custom-call(f32[24,32,128]{2,1,0:T(8,128)S(1)} %get-tuple-element.37.sum_ref, bf16[12,32,128]{2,1,0:T(8,128)(2,1)S(1)} %collective-permute-done.5.last_ref, bf16[24,32,128]{2,1,0:T(8,128)(2,1)S(1)} %get-tuple-element.31.window_ref, bf16[3,1,1200,128]{3,2,1,0:T(8,128)(2,1)S(1)} %shard_map.33.patch_ref, ...), custom_call_target="tpu_custom_call" | custom-call | tf_op jit(solution)/shard_map/pallas_call | solution.py:490
  (1 shorter events, 0.0 us)
Async XLA Ops:
  1.9 16.2 %all-to-all-start = ((bf16[32,24,128]{2,1,0:T(8,128)(2,1)}), bf16[32,24,128]{2,1,0:T(8,128)(2,1)S(1)}, u32[]{:S(2)}, u32[]{:S(2)}) async-start(bf16[32,24,128]{2,1,0:T(8,128)(2,1)} %bitcast.5), calls=%async_computation | async-start | bytes 393216 | tf_op jit(solution)/shard_map/all_to_all | solution.py:544
  9.3 2.0 %copy-start = (bf16[4,3,128,1200]{2,3,1,0:T(8,128)(2,1)S(1)}, bf16[4,3,128,1200]{2,3,1,0:T(8,128)(2,1)}, u32[]{:S(2)}) copy-start(bf16[4,3,128,1200]{2,3,1,0:T(8,128)(2,1)} %param.3) | copy-start | bytes 11059204
  21.4 6.4 %collective-permute-start = (bf16[18,32,128]{2,1,0:T(8,128)(2,1)S(1)}, bf16[18,32,128]{2,1,0:T(8,128)(2,1)S(1)}, u32[]{:S(2)}, u32[]{:S(2)}) collective-permute-start(bf16[18,32,128]{2,1,0:T(8,128)(2,1)S(1)} %get-tuple-element.25), channel_id=1, source_target_pairs={{0,8},{1,9},{2,10},{3,11},{4,12},{5,13},{6,14},{7,15},{8,0},{9,1},... | collective-permute-start | bytes 442376 | tf_op jit(solution)/shard_map/ppermute | solution.py:514
  22.5 5.3 %collective-permute-start.1 = (bf16[18,32,128]{2,1,0:T(8,128)(2,1)S(1)}, bf16[18,32,128]{2,1,0:T(8,128)(2,1)S(1)}, u32[]{:S(2)}, u32[]{:S(2)}) collective-permute-start(bf16[18,32,128]{2,1,0:T(8,128)(2,1)S(1)} %get-tuple-element.26), channel_id=1, source_target_pairs={{0,1},{1,0},{2,3},{3,2},{4,5},{5,4},{6,7},{7,6},{8,16},{9,17},{10,... | collective-permute-start | bytes 442376 | tf_op jit(solution)/shard_map/ppermute | solution.py:514
  28.2 6.5 %collective-permute-start.2 = (bf16[24,32,128]{2,1,0:T(8,128)(2,1)S(1)}, bf16[24,32,128]{2,1,0:T(8,128)(2,1)S(1)}, u32[]{:S(2)}, u32[]{:S(2)}) collective-permute-start(bf16[24,32,128]{2,1,0:T(8,128)(2,1)S(1)} %get-tuple-element.28), channel_id=1, source_target_pairs={{0,8},{1,2},{2,1},{3,4},{4,3},{5,6},{6,5},{7,15},{8,0},{9,10},{10,... | collective-permute-start | bytes 589832 | tf_op jit(solution)/shard_map/ppermute | solution.py:514
  30.0 4.7 %collective-permute-start.3 = (bf16[24,32,128]{2,1,0:T(8,128)(2,1)S(1)}, bf16[24,32,128]{2,1,0:T(8,128)(2,1)S(1)}, u32[]{:S(2)}, u32[]{:S(2)}) collective-permute-start(bf16[24,32,128]{2,1,0:T(8,128)(2,1)S(1)} %get-tuple-element.29), channel_id=1, source_target_pairs={{0,1},{1,0},{2,3},{3,2},{4,5},{5,4},{6,7},{7,6},{8,9},{9,8},{10,11... | collective-permute-start | bytes 589832 | tf_op jit(solution)/shard_map/ppermute | solution.py:514
  30.0 4.7 %collective-permute-start.4 = (bf16[3,32,128]{2,1,0:T(8,128)(2,1)S(1)}, bf16[3,32,128]{2,1,0:T(8,128)(2,1)S(1)}, u32[]{:S(2)}, u32[]{:S(2)}) collective-permute-start(bf16[3,32,128]{2,1,0:T(8,128)(2,1)S(1)} %get-tuple-element.30), channel_id=1, source_target_pairs={{0,2},{1,7},{2,4},{3,1},{4,6},{5,3},{6,0},{7,5},{8,10},{9,15},{10,... | collective-permute-start | bytes 73736 | tf_op jit(solution)/shard_map/ppermute | solution.py:523
  34.8 1.4 %collective-permute-start.5 = (bf16[12,32,128]{2,1,0:T(8,128)(2,1)S(1)}, bf16[12,32,128]{2,1,0:T(8,128)(2,1)S(1)}, u32[]{:S(2)}, u32[]{:S(2)}) collective-permute-start(bf16[12,32,128]{2,1,0:T(8,128)(2,1)S(1)} %slice.3), channel_id=1, source_target_pairs={{0,1},{1,0},{2,3},{3,2},{4,5},{5,4},{6,7},{7,6},{8,9},{9,8},{10,11... | collective-permute-start | bytes 294920 | tf_op jit(solution)/shard_map/ppermute | solution.py:514

commit v9 on v8

--- a/solution.py
+++ b/solution.py
@@ -378,8 +378,8 @@
 
 
 def merge_kernel(
-    z, sum_ref, near_ref, far_ref, late_ref, window_ref, hidden_ref, pooled_ref, first_ref, wide_ref,
-    out_ref, patch_ref, factor_ref, resid_ref, flat_ref, dense_ref,
+    z, sum_ref, near_ref, far_ref, late_ref, window_ref, hidden_ref, tall_ref, first_ref, wide_ref,
+    out_ref, patch_ref, factor_ref, pooled_ref, resid_ref, flat_ref, dense_ref, wide_edge_ref, inverse_ref,
 ):
     even = is_even()
     col = lax.axis_index("col")
@@ -397,6 +397,7 @@
             out_ref[t + k] = recon[k]
         return recon
 
+    pool_kernel(z, hidden_ref, tall_ref, near_ref, far_ref, pooled_ref, wide_edge_ref, inverse_ref)
     store_residual(z, recon_of, window_ref, resid_ref)
     turn_fields(z, lambda t: resid_ref[t], flat_ref)
     fill_factor(z, z.early, resid_ref, pooled_ref, hidden_ref, first_ref, wide_ref, factor_ref)
@@ -567,17 +568,22 @@
     )
     far, near, late, patch = lax.optimization_barrier((far, near, late, patch))
     last = exchange(z, far[: z.T // 2], swap_col)
-    (pooled,) = vmem_call(
-        functools.partial(pool_kernel, z),
-        [((z.rd, z.cd, B, z.F), f32)],
-        [((z.cd + 4, B, z.F), f32), ((z.rd + 2, z.cd + 2, B, z.F), f32)],
-        hidden, tall, near, far,
-    )
-    total, early_patch, early_factor = vmem_call(
+    total, early_patch, early_factor, pooled = vmem_call(
         functools.partial(merge_kernel, z),
-        [tiles, ((z.groups, K, 128), bf16), ((z.groups, 256, z.per * z.F), bf16)],
-        [((z.T, B, L), bf16), ((z.groups, z.KW, 128), f32), ((K, 128), f32)],
-        total, near, far, late, window, hidden, pooled, wide_first, wide,
+        [
+            tiles,
+            ((z.groups, K, 128), bf16),
+            ((z.groups, 256, z.per * z.F), bf16),
+            ((z.rd, z.cd, B, z.F), f32),
+        ],
+        [
+            ((z.T, B, L), bf16),
+            ((z.groups, z.KW, 128), f32),
+            ((K, 128), f32),
+            ((z.cd + 4, B, z.F), f32),
+            ((z.rd + 2, z.cd + 2, B, z.F), f32),
+        ],
+        total, near, far, late, window, hidden, tall, wide_first, wide,
     )
     out = gradient(
         z, total, last, window, patch, hidden, pooled, wide_first, wide, early_patch, early_factor

time: 39.9 us -> 39.9 us (level)
    pallas_call x4 -> x3, Pallas kernels: 1.73 us -> 1.68 us  [vmem_call(): pl.pallas_call(kernel, out_shape=[pltpu.VMEM(*s) for s in shapes], in_spe...]
where the time goes in v9:
time: 39.9 us; the launch traced here: 39.6 us
  waiting for transfers between devices  14 us (35%)
  Pallas kernels  13 us (33%)
  starting transfers between devices  10.5 us (26%)
  local copies, waits for them, and re-layouts  2.05 us (5%)
    all_to_all x1, starting transfers between devices, body(): lax.all_to_all(blocks.reshape(z.R * z.C, z.bd * z.T, L), ('row', 'col'),...  7.3 us
    ppermute x5, waiting for transfers between devices, exchange(): return lax.ppermute(value, ('row', 'col'), pairs)  5.46 us
    ppermute x1, waiting for transfers between devices, shift(): return lax.ppermute(value, ('row', 'col'), pairs)  4.31 us
    all_to_all x1, waiting for transfers between devices, body(): lax.all_to_all(blocks.reshape(z.R * z.C, z.bd * z.T, L), ('row', 'col'),...  4.25 us
    pallas_call x1, Pallas kernels, gradient(): pl.pallas_call(functools.partial(grad_kernel, z), out_shape=pltpu.HBM((z....  3.46 us
    pallas_call x1, Pallas kernels, encode(): pl.pallas_call(functools.partial(encode_kernel, z), out_shape=[pltpu.VMEM...  3.31 us
    ppermute x5, starting transfers between devices, exchange(): return lax.ppermute(value, ('row', 'col'), pairs)  3.22 us
    pallas_call x2, Pallas kernels, spread_weights(): pl.pallas_call(functools.partial(spread_kernel, z), grid=(count,), out_sh...  2.58 us
  transfers between devices with their start and end apart: 7, of which 4 were waited for; matrix products, arithmetic and copies ran while one was open for 0% of the time, Pallas kernels for 10%

profile of v9, /device:TPU:0, one launch (start us, length us, event | category | flops | bytes accessed | tf_op | source)
XLA Modules:
  0.0 39.6 jit_solution(17116102088011215564)
XLA Ops:
  0.0 1.9 %shard_map.28 = bf16[4,192,128]{2,1,0:T(8,128)(2,1)} custom-call(bf16[1,3,64,96]{3,2,1,0:T(8,128)(2,1)} %images_hbm.1), custom_call_target="tpu_custom_call" | custom-call | tf_op jit(solution)/shard_map/pallas_call | solution.py:117
  1.9 7.3 %all-to-all-start = ((bf16[32,24,128]{2,1,0:T(8,128)(2,1)}), bf16[32,24,128]{2,1,0:T(8,128)(2,1)S(1)}, u32[]{:S(2)}, u32[]{:S(2)}) async-start(bf16[32,24,128]{2,1,0:T(8,128)(2,1)} %bitcast.5), calls=%async_computation | async-start | bytes 393216 | tf_op jit(solution)/shard_map/all_to_all | solution.py:545
  9.3 0.0 copy-start
  9.3 2.0 %copy-done = bf16[4,3,128,1200]{2,3,1,0:T(8,128)(2,1)S(1)} copy-done((bf16[4,3,128,1200]{2,3,1,0:T(8,128)(2,1)S(1)}, bf16[4,3,128,1200]{2,3,1,0:T(8,128)(2,1)}, u32[]{:S(2)}) %copy-start) | copy-done | bytes 3686424
  11.3 0.6 %shard_map.29.first_ref = bf16[2,1920,384]{2,1,0:T(8,128)(2,1)S(1)} custom-call(bf16[4,3,1200,128]{3,2,1,0:T(8,128)(2,1)S(1)} %bitcast.3), custom_call_target="tpu_custom_call" | custom-call | tf_op jit(solution)/shard_map/pallas_call | solution.py:147
  12.0 1.9 %shard_map.30.wide_hbm = bf16[2,1920,384]{2,1,0:T(8,128)(2,1)} custom-call(bf16[4,3,1200,128]{3,2,1,0:T(8,128)(2,1)S(1)} %bitcast.4), custom_call_target="tpu_custom_call" | custom-call | tf_op jit(solution)/shard_map/pallas_call | solution.py:147
  13.9 4.2 %all-to-all-done.moved_ref = bf16[32,24,128]{2,1,0:T(8,128)(2,1)S(1)} async-done(((bf16[32,24,128]{2,1,0:T(8,128)(2,1)}), bf16[32,24,128]{2,1,0:T(8,128)(2,1)S(1)}, u32[]{:S(2)}, u32[]{:S(2)}) %all-to-all-start) | async-done | bytes 196640 | tf_op jit(solution)/shard_map/all_to_all | solution.py:545
  18.1 3.3 %shard_map.31 = (bf16[24,32,128]{2,1,0:T(8,128)(2,1)S(1)}, bf16[4,3,32,128]{3,2,1,0:T(8,128)(2,1)S(1)}, f32[24,32,128]{2,1,0:T(8,128)S(1)}, bf16[18,32,128]{2,1,...) custom-call(bf16[32,24,128]{2,1,0:T(8,128)(2,1)S(1)} %all-to-all-done.moved_ref, ...), custom_call_target="tpu_custom_call" | custom-call | tf_op jit(solution)/shard_map/pallas_call | solution.py:217
  21.5 1.1 %collective-permute-start = (bf16[18,32,128]{2,1,0:T(8,128)(2,1)S(1)}, bf16[18,32,128]{2,1,0:T(8,128)(2,1)S(1)}, u32[]{:S(2)}, u32[]{:S(2)}) collective-permute-start(bf16[18,32,128]{2,1,0:T(8,128)(2,1)S(1)} %get-tuple-element.26), channel_id=1, source_target_pairs={{0,8},{1,9},{2,10},{3,11},{4,12},{5,13},{6,14},{7,15},{8,0},{9,1},... | collective-permute-start | bytes 442376 | tf_op jit(solution)/shard_map/ppermute | solution.py:515
  22.5 0.0 collective-permute-start.1
  22.6 5.3 %collective-permute-done.swap_ref = bf16[18,32,128]{2,1,0:T(8,128)(2,1)S(1)} collective-permute-done((bf16[18,32,128]{2,1,0:T(8,128)(2,1)S(1)}, bf16[18,32,128]{2,1,0:T(8,128)(2,1)S(1)}, u32[]{:S(2)}, u32[]{:S(2)}) %collective-permute-start) | collective-permute-done | bytes 147488 | tf_op jit(solution)/shard_map/ppermute | solution.py:515
  27.9 0.0 collective-permute-done.1.cross_ref
  27.9 0.4 shard_map.32
  28.3 1.8 %collective-permute-start.2 = (bf16[24,32,128]{2,1,0:T(8,128)(2,1)S(1)}, bf16[24,32,128]{2,1,0:T(8,128)(2,1)S(1)}, u32[]{:S(2)}, u32[]{:S(2)}) collective-permute-start(bf16[24,32,128]{2,1,0:T(8,128)(2,1)S(1)} %get-tuple-element.29), channel_id=1, source_target_pairs={{0,8},{1,2},{2,1},{3,4},{4,3},{5,6},{6,5},{7,15},{8,0},{9,10},{10,... | collective-permute-start | bytes 589832 | tf_op jit(solution)/shard_map/ppermute | solution.py:515
  30.1 0.0 collective-permute-start.3
  30.1 0.0 collective-permute-start.4
  30.1 0.4 %shard_map.33.patch_ref = bf16[3,1,1200,128]{3,2,1,0:T(8,128)(2,1)S(1)} custom-call(bf16[24,32,128]{2,1,0:T(8,128)(2,1)S(1)} %get-tuple-element.32.window_ref), custom_call_target="tpu_custom_call" | custom-call | tf_op jit(solution)/shard_map/pallas_call | solution.py:283
  30.5 4.3 %collective-permute-done.4.late_ref = bf16[3,32,128]{2,1,0:T(8,128)(2,1)S(1)} collective-permute-done((bf16[3,32,128]{2,1,0:T(8,128)(2,1)S(1)}, bf16[3,32,128]{2,1,0:T(8,128)(2,1)S(1)}, u32[]{:S(2)}, u32[]{:S(2)}) %collective-permute-start.4) | collective-permute-done | bytes 24608 | tf_op jit(solution)/shard_map/ppermute | solution.py:524
  34.8 0.0 collective-permute-done.2.far_ref
  34.8 0.0 collective-permute-done.3.near_ref
  34.8 0.3 collective-permute-start.5
  35.1 0.9 %shard_map.34 = (f32[24,32,128]{2,1,0:T(8,128)S(1)}, bf16[1,1200,128]{2,1,0:T(8,128)(2,1)S(1)}, bf16[1,256,512]{2,1,0:T(8,128)(2,1)S(1)}, f32[4,3,32,128]{3,2,1,0:T(8,128)S(1)}) custom-call(f32[24,32,128]{2,1,0:T(8,128)S(1)} %get-tuple-element.28.sum_ref, bf16[24,32,128]{2,1,0:T(8,128)(2,1)S(1)} %collective-permute-done.3.near_ref, ...), custom_call_target="tpu_custom_call" | custom-call | tf_op jit(solution)/shard_map/pallas_call | solution.py:283
  36.0 0.1 collective-permute-done.5.last_ref
  36.2 3.5 %shard_map.35 = f32[4,3,1200,128]{3,2,1,0:T(8,128)} custom-call(f32[24,32,128]{2,1,0:T(8,128)S(1)} %get-tuple-element.38.sum_ref, bf16[12,32,128]{2,1,0:T(8,128)(2,1)S(1)} %collective-permute-done.5.last_ref, bf16[24,32,128]{2,1,0:T(8,128)(2,1)S(1)} %get-tuple-element.32.window_ref, bf16[3,1,1200,128]{3,2,1,0:T(8,128)(2,1)S(1)} %shard_map.33.patch_ref, ...), custom_call_target="tpu_custom_call" | custom-call | tf_op jit(solution)/shard_map/pallas_call | solution.py:491
  (1 shorter events, 0.0 us)
Async XLA Ops:
  1.9 16.2 %all-to-all-start = ((bf16[32,24,128]{2,1,0:T(8,128)(2,1)}), bf16[32,24,128]{2,1,0:T(8,128)(2,1)S(1)}, u32[]{:S(2)}, u32[]{:S(2)}) async-start(bf16[32,24,128]{2,1,0:T(8,128)(2,1)} %bitcast.5), calls=%async_computation | async-start | bytes 393216 | tf_op jit(solution)/shard_map/all_to_all | solution.py:545
  9.3 2.0 %copy-start = (bf16[4,3,128,1200]{2,3,1,0:T(8,128)(2,1)S(1)}, bf16[4,3,128,1200]{2,3,1,0:T(8,128)(2,1)}, u32[]{:S(2)}) copy-start(bf16[4,3,128,1200]{2,3,1,0:T(8,128)(2,1)} %param.3) | copy-start | bytes 11059204
  21.5 6.4 %collective-permute-start = (bf16[18,32,128]{2,1,0:T(8,128)(2,1)S(1)}, bf16[18,32,128]{2,1,0:T(8,128)(2,1)S(1)}, u32[]{:S(2)}, u32[]{:S(2)}) collective-permute-start(bf16[18,32,128]{2,1,0:T(8,128)(2,1)S(1)} %get-tuple-element.26), channel_id=1, source_target_pairs={{0,8},{1,9},{2,10},{3,11},{4,12},{5,13},{6,14},{7,15},{8,0},{9,1},... | collective-permute-start | bytes 442376 | tf_op jit(solution)/shard_map/ppermute | solution.py:515
  22.5 5.3 %collective-permute-start.1 = (bf16[18,32,128]{2,1,0:T(8,128)(2,1)S(1)}, bf16[18,32,128]{2,1,0:T(8,128)(2,1)S(1)}, u32[]{:S(2)}, u32[]{:S(2)}) collective-permute-start(bf16[18,32,128]{2,1,0:T(8,128)(2,1)S(1)} %get-tuple-element.27), channel_id=1, source_target_pairs={{0,1},{1,0},{2,3},{3,2},{4,5},{5,4},{6,7},{7,6},{8,16},{9,17},{10,... | collective-permute-start | bytes 442376 | tf_op jit(solution)/shard_map/ppermute | solution.py:515
  28.3 6.5 %collective-permute-start.2 = (bf16[24,32,128]{2,1,0:T(8,128)(2,1)S(1)}, bf16[24,32,128]{2,1,0:T(8,128)(2,1)S(1)}, u32[]{:S(2)}, u32[]{:S(2)}) collective-permute-start(bf16[24,32,128]{2,1,0:T(8,128)(2,1)S(1)} %get-tuple-element.29), channel_id=1, source_target_pairs={{0,8},{1,2},{2,1},{3,4},{4,3},{5,6},{6,5},{7,15},{8,0},{9,10},{10,... | collective-permute-start | bytes 589832 | tf_op jit(solution)/shard_map/ppermute | solution.py:515
  30.1 4.7 %collective-permute-start.3 = (bf16[24,32,128]{2,1,0:T(8,128)(2,1)S(1)}, bf16[24,32,128]{2,1,0:T(8,128)(2,1)S(1)}, u32[]{:S(2)}, u32[]{:S(2)}) collective-permute-start(bf16[24,32,128]{2,1,0:T(8,128)(2,1)S(1)} %get-tuple-element.30), channel_id=1, source_target_pairs={{0,1},{1,0},{2,3},{3,2},{4,5},{5,4},{6,7},{7,6},{8,9},{9,8},{10,11... | collective-permute-start | bytes 589832 | tf_op jit(solution)/shard_map/ppermute | solution.py:515
  30.1 4.7 %collective-permute-start.4 = (bf16[3,32,128]{2,1,0:T(8,128)(2,1)S(1)}, bf16[3,32,128]{2,1,0:T(8,128)(2,1)S(1)}, u32[]{:S(2)}, u32[]{:S(2)}) collective-permute-start(bf16[3,32,128]{2,1,0:T(8,128)(2,1)S(1)} %get-tuple-element.31), channel_id=1, source_target_pairs={{0,2},{1,7},{2,4},{3,1},{4,6},{5,3},{6,0},{7,5},{8,10},{9,15},{10,... | collective-permute-start | bytes 73736 | tf_op jit(solution)/shard_map/ppermute | solution.py:524
  34.8 1.4 %collective-permute-start.5 = (bf16[12,32,128]{2,1,0:T(8,128)(2,1)S(1)}, bf16[12,32,128]{2,1,0:T(8,128)(2,1)S(1)}, u32[]{:S(2)}, u32[]{:S(2)}) collective-permute-start(bf16[12,32,128]{2,1,0:T(8,128)(2,1)S(1)} %slice.3), channel_id=1, source_target_pairs={{0,1},{1,0},{2,3},{3,2},{4,5},{5,4},{6,7},{7,6},{8,9},{9,8},{10,11... | collective-permute-start | bytes 294920 | tf_op jit(solution)/shard_map/ppermute | solution.py:515
